TPU v7x, 32 devices: a whole 2x2x4 slice. The times are simulated.
32 devices in a mesh: seq: 16 (over z, x, core), tp: 2 (over y).
Axes of the slice: x: 2, y: 2, z: 4, core: 2. Of those that a mesh axis runs over, the one named last changes fastest.
Arguments:
- tokens_in: bfloat16 [16384, 1024], P(('seq', 'tp')), may hold values from -6 to 6
- w_qkv: bfloat16 [1024, 3, 1024], P(None, None, 'tp'), may hold values from -0.1875 to 0.1875
- bias_qv: bfloat16 [2, 1024], P(None, 'tp'), may hold values from -4 to 4
- w_out: bfloat16 [1024, 1024], P('tp'), may hold values from -0.1875 to 0.1875
- bias_out: bfloat16 [1024], replicated, may hold values from -0.4375 to 0.4375
- w_up: bfloat16 [1024, 4096], P(None, 'tp'), may hold values from -0.1875 to 0.1875
- bias_up: bfloat16 [4096], P('tp'), may hold values from -4 to 4
- w_down: bfloat16 [4096, 1024], P('tp'), may hold values from -0.09375 to 0.09375
- bias_down: bfloat16 [1024], replicated, may hold values from -1.5 to 1.5
- norm_gains: float32 [4, 1024], replicated, may hold values from 0.5 to 1.5
- norm_shifts: float32 [4, 1024], replicated, may hold values from -1.5 to 1.5
- out_grad: float32 [16384, 1024], P(('seq', 'tp')), may hold values from -6 to 6
- lengths: int32 [12], replicated, may hold values from 1 to 4096, as said below
- prefixes: int32 [12], replicated, may hold values from 0 to 64, as said below
- placement: int32 [32], replicated, may hold values from 0 to 31, as said below
Outputs:
- result: bfloat16 [16384, 1024], P(('seq', 'tp'))
- grad_x: float32 [16384, 1024], P(('seq', 'tp'))
- grad_w_qkv: float32 [1024, 3, 1024], P(None, None, 'tp')
- grad_bias_qv: float32 [2, 1024], P(None, 'tp')
- grad_w_out: float32 [1024, 1024], P('tp')
- grad_bias_out: float32 [1024], replicated
- grad_w_up: float32 [1024, 4096], P(None, 'tp')
- grad_bias_up: float32 [4096], P('tp')
- grad_w_down: float32 [4096, 1024], P('tp')
- grad_bias_down: float32 [1024], replicated
- grad_gains: float32 [4, 1024], replicated
- grad_shifts: float32 [4, 1024], replicated
Inputs may be any that keep to these rules, and one draw needn't show every extreme that they name: `lengths`: they sum to 16384; at least 7 are text-image pairs of 1088 tokens, and one is exactly 4096 long. `prefixes`: 64 for each of the 7 text-image pairs, 0 for the sequence of 4096 tokens, and for each other text document a prompt of 0 to 64 tokens. `placement`: A permutation of the block numbers; the k-th block stored on each index of seq is one of blocks k * 16 to (k + 1) * 16 - 1.
All inputs are finite; a program needn't handle non-finite values.
Results may differ from a plain program's by a relative error of at most 0.02.
Values may be sent and summed in bfloat16 or wider, within the bound.
A program may use at most 384 MiB of HBM per device.

v0:
```python
import jax
import jax.numpy as jnp
from jax import lax
from jax.sharding import PartitionSpec as P

HEAD = 64
BLK = 512
LONGEST = 4096


EPS = 1e-05


def layer_norm(row_block, gain_row, shift_row):
    row_mean = jnp.mean(row_block, axis=-1, keepdims=True)
    centred = row_block - row_mean
    spread = jnp.mean(centred * centred, axis=-1, keepdims=True)
    return centred * lax.rsqrt(spread + EPS) * gain_row + shift_row


def smooth_gate(values):
    return jax.nn.gelu(values, approximate=True)


def pack_tables(lengths, prefixes, row_total):
    where_row = jnp.arange(row_total, dtype=jnp.int32)
    doc_ends = jnp.cumsum(lengths)
    document = jnp.sum((where_row[:, None] >= doc_ends[None, :]).astype(jnp.int32), axis=1)
    limits = doc_ends - lengths + prefixes
    doc_pick = document[:, None] == jnp.arange(lengths.shape[0], dtype=jnp.int32)[None, :]
    visible = jnp.sum(jnp.where(doc_pick, limits[None, :], 0), axis=1)
    return (document, visible)


def padded_tables(document, visible, margin):
    row_total = document.shape[0]
    border = jnp.full((margin,), -1, jnp.int32)
    doc_pad = jnp.concatenate([border, document, border])
    pos_pad = jnp.arange(-margin, row_total + margin, dtype=jnp.int32)
    blank = jnp.zeros((margin,), jnp.int32)
    seen_pad = jnp.concatenate([blank, visible, blank])
    return (doc_pad, pos_pad, seen_pad)


def allowed_pairs(query_pos, query_doc, key_pos, key_doc, key_seen):
    return (query_doc[:, None] == key_doc[None, :]) & (
        (key_pos[None, :] <= query_pos[:, None]) | (key_pos[None, :] < key_seen[None, :])
    )


def to_pack(stored, pack_order, margin, block_size):
    blocks = stored.reshape((pack_order.shape[0], block_size) + stored.shape[1:])
    ordered = jnp.take(blocks, pack_order, axis=0).reshape(stored.shape)
    widths = [(margin, margin)] + [(0, 0)] * (stored.ndim - 1)
    return jnp.pad(ordered, widths)


def from_pack(padded, placement, margin, block_size, row_total):
    core = padded[margin : margin + row_total]
    blocks = core.reshape((placement.shape[0], block_size) + core.shape[1:])
    return jnp.take(blocks, placement, axis=0).reshape(core.shape)


def masked_scores(query_h, key_h, allowed):
    scores = query_h.shape[-1] ** (-0.5) * jnp.einsum(
        "qe,ke->qk", query_h, key_h, preferred_element_type=jnp.float32
    )
    return jnp.where(allowed, scores, -jnp.inf)


def forward_block(query_block, key_win, value_win, allowed):

    def forward_one_head(head):
        query_h = lax.dynamic_index_in_dim(query_block, head, 1, False)
        key_h = lax.dynamic_index_in_dim(key_win, head, 1, False)
        value_h = lax.dynamic_index_in_dim(value_win, head, 1, False)
        masked = masked_scores(query_h, key_h, allowed)
        row_top = jnp.max(masked, axis=1, keepdims=True)
        expo = jnp.exp(masked - row_top)
        row_sum = jnp.sum(expo, axis=1, keepdims=True)
        probs_b = (expo / row_sum).astype(jnp.bfloat16)
        output = jnp.dot(probs_b, value_h, preferred_element_type=jnp.float32)
        return (output, (row_top + jnp.log(row_sum))[:, 0])

    return lax.map(forward_one_head, jnp.arange(query_block.shape[1], dtype=jnp.int32))


def attention_grads(
    query_block, d_att_block, mass_block, total_block, key_block, value_block, allowed
):
    score_scale = query_block.shape[-1] ** (-0.5)

    def attention_one_head(head):
        query_h = lax.dynamic_index_in_dim(query_block, head, 1, False)
        d_att_h = lax.dynamic_index_in_dim(d_att_block, head, 1, False)
        key_h = lax.dynamic_index_in_dim(key_block, head, 1, False)
        value_h = lax.dynamic_index_in_dim(value_block, head, 1, False)
        mass_h = lax.dynamic_index_in_dim(mass_block, head, 0, False)
        total_h = lax.dynamic_index_in_dim(total_block, head, 0, False)
        masked = masked_scores(query_h, key_h, allowed)
        probs = jnp.exp(masked - mass_h[:, None])
        d_probs = jnp.einsum("qe,ke->qk", d_att_h, value_h, preferred_element_type=jnp.float32)
        d_scores = (probs * (d_probs - total_h[:, None])).astype(jnp.bfloat16)
        results = []
        results.append(
            score_scale
            * jnp.einsum("qk,ke->qe", d_scores, key_h, preferred_element_type=jnp.float32)
        )
        results.append(
            score_scale
            * jnp.einsum("qk,qe->ke", d_scores, query_h, preferred_element_type=jnp.float32)
        )
        results.append(
            jnp.einsum(
                "qk,qe->ke", probs.astype(jnp.bfloat16), d_att_h, preferred_element_type=jnp.float32
            )
        )
        return tuple(results)

    return lax.map(attention_one_head, jnp.arange(query_block.shape[1], dtype=jnp.int32))


def local(
    tokens_in,
    w_qkv,
    bias_qv,
    w_out,
    bias_out,
    w_up,
    bias_up,
    w_down,
    bias_down,
    norm_gains,
    norm_shifts,
    out_grad,
    lengths,
    prefixes,
    placement,
):
    seq_count = lax.axis_size("seq")
    block_total = placement.shape[0]
    blocks_here = block_total // seq_count
    total_rows = block_total * BLK
    own_rows = blocks_here * BLK
    model_width = w_qkv.shape[0]
    head_span = w_qkv.shape[2]
    heads_here = head_span // HEAD
    margin = LONGEST + BLK
    window = LONGEST + 2 * BLK
    document, visible = pack_tables(lengths, prefixes, total_rows)
    doc_pad, pos_pad, seen_pad = padded_tables(document, visible, margin)
    own_blocks = lax.dynamic_slice_in_dim(
        placement, lax.axis_index("seq") * blocks_here, blocks_here
    )
    pack_order = (
        jnp.zeros((block_total,), jnp.int32)
        .at[placement]
        .set(jnp.arange(block_total, dtype=jnp.int32))
    )
    offsets = jnp.arange(BLK, dtype=jnp.int32)

    def query_window(index):
        first = own_blocks[index] * BLK
        key_first = margin + first - LONGEST
        allowed = allowed_pairs(
            first + offsets,
            lax.dynamic_slice_in_dim(document, first, BLK),
            lax.dynamic_slice_in_dim(pos_pad, key_first, window),
            lax.dynamic_slice_in_dim(doc_pad, key_first, window),
            lax.dynamic_slice_in_dim(seen_pad, key_first, window),
        )
        return (key_first, allowed)

    input_f32 = tokens_in.astype(jnp.float32)
    normed, back_first = jax.vjp(layer_norm, input_f32, norm_gains[0], norm_shifts[0])
    rows_all = lax.all_gather(normed.astype(jnp.bfloat16), "tp", axis=0, tiled=True)
    flat_qkv = w_qkv.reshape(model_width, 3 * head_span)
    mixed = jnp.dot(rows_all, flat_qkv, preferred_element_type=jnp.float32).reshape(
        own_rows, 3, head_span
    )
    query_b = (mixed[:, 0] + bias_qv[0].astype(jnp.float32)).astype(jnp.bfloat16)
    key_b = mixed[:, 1].astype(jnp.bfloat16)
    value_b = (mixed[:, 2] + bias_qv[1].astype(jnp.float32)).astype(jnp.bfloat16)
    keys_all, values_all = (
        lax.all_gather(key_b, "seq", axis=0, tiled=True),
        lax.all_gather(value_b, "seq", axis=0, tiled=True),
    )
    keys_pad = to_pack(keys_all, pack_order, margin, BLK).reshape(-1, heads_here, HEAD)
    values_pad = to_pack(values_all, pack_order, margin, BLK).reshape(-1, heads_here, HEAD)
    head_shape = (own_rows, heads_here, HEAD)
    query3 = query_b.reshape(head_shape)
    attended_list = []
    mass_list = []
    for index in range(blocks_here):
        key_first, allowed = query_window(index)
        outputs, masses = forward_block(
            query3[index * BLK : (index + 1) * BLK],
            lax.dynamic_slice_in_dim(keys_pad, key_first, window),
            lax.dynamic_slice_in_dim(values_pad, key_first, window),
            allowed,
        )
        attended_list.append(jnp.transpose(outputs, (1, 0, 2)))
        mass_list.append(masses)
    attended32 = jnp.concatenate(attended_list, axis=0)
    log_mass = jnp.concatenate(mass_list, axis=1)
    attended_b = attended32.reshape(own_rows, head_span).astype(jnp.bfloat16)
    branch = lax.psum_scatter(
        jnp.dot(attended_b, w_out, preferred_element_type=jnp.float32).astype(jnp.bfloat16),
        "tp",
        scatter_dimension=0,
        tiled=True,
    ).astype(jnp.float32) + bias_out.astype(jnp.float32)
    post_attn, back_post = jax.vjp(layer_norm, branch, norm_gains[1], norm_shifts[1])
    hidden = input_f32 + post_attn
    inner, back_inner = jax.vjp(layer_norm, hidden, norm_gains[2], norm_shifts[2])
    inner_all = lax.all_gather(inner.astype(jnp.bfloat16), "tp", axis=0, tiled=True)
    upward = jnp.dot(inner_all, w_up, preferred_element_type=jnp.float32) + bias_up.astype(
        jnp.float32
    )
    active, back_gate = jax.vjp(smooth_gate, upward)
    active_b = active.astype(jnp.bfloat16)
    down = lax.psum_scatter(
        jnp.dot(active_b, w_down, preferred_element_type=jnp.float32).astype(jnp.bfloat16),
        "tp",
        scatter_dimension=0,
        tiled=True,
    ).astype(jnp.float32) + bias_down.astype(jnp.float32)
    final, back_final = jax.vjp(layer_norm, down, norm_gains[3], norm_shifts[3])
    result = (hidden + final).astype(jnp.bfloat16)
    d_down, gain_last, shift_last = back_final(out_grad)
    grad_bias_down = jnp.sum(d_down, axis=0)
    d_down_all = lax.all_gather(d_down.astype(jnp.bfloat16), "tp", axis=0, tiled=True)
    grad_w_down = jnp.einsum("tf,td->fd", active_b, d_down_all, preferred_element_type=jnp.float32)
    d_active = jnp.einsum("td,fd->tf", d_down_all, w_down, preferred_element_type=jnp.float32)
    (d_up,) = back_gate(d_active)
    d_up_b = d_up.astype(jnp.bfloat16)
    grad_bias_up = jnp.sum(d_up_b.astype(jnp.float32), axis=0)
    grad_w_up = jnp.einsum("td,tf->df", inner_all, d_up_b, preferred_element_type=jnp.float32)
    d_inner = lax.psum_scatter(
        jnp.einsum("tf,df->td", d_up_b, w_up, preferred_element_type=jnp.float32).astype(
            jnp.bfloat16
        ),
        "tp",
        scatter_dimension=0,
        tiled=True,
    ).astype(jnp.float32)
    d_hidden_part, gain_third, shift_third = back_inner(d_inner)
    d_hidden = out_grad + d_hidden_part
    d_branch, gain_second, shift_second = back_post(d_hidden)
    grad_bias_out = jnp.sum(d_branch, axis=0)
    d_branch_all = lax.all_gather(d_branch.astype(jnp.bfloat16), "tp", axis=0, tiled=True)
    grad_w_out = jnp.einsum(
        "te,td->ed", attended_b, d_branch_all, preferred_element_type=jnp.float32
    )
    d_att_b = jnp.einsum(
        "td,ed->te", d_branch_all, w_out, preferred_element_type=jnp.float32
    ).astype(jnp.bfloat16)
    d_att3 = d_att_b.reshape(head_shape)
    d_total = jnp.sum(d_att3.astype(jnp.float32) * attended32, axis=2).T
    d_query_list = []
    key_buffer = jnp.zeros((total_rows + 2 * margin, head_span), jnp.float32)
    value_buffer = jnp.zeros((total_rows + 2 * margin, head_span), jnp.float32)
    for index in range(blocks_here):
        key_first, allowed = query_window(index)
        rows = slice(index * BLK, (index + 1) * BLK)
        d_query_h, d_key_h, d_value_h = attention_grads(
            query3[rows],
            d_att3[rows],
            log_mass[:, rows],
            d_total[:, rows],
            lax.dynamic_slice_in_dim(keys_pad, key_first, window),
            lax.dynamic_slice_in_dim(values_pad, key_first, window),
            allowed,
        )
        d_query_list.append(jnp.transpose(d_query_h, (1, 0, 2)))
        key_piece = jnp.transpose(d_key_h, (1, 0, 2)).reshape(window, head_span)
        value_piece = jnp.transpose(d_value_h, (1, 0, 2)).reshape(window, head_span)
        key_buffer = lax.dynamic_update_slice_in_dim(
            key_buffer,
            lax.dynamic_slice_in_dim(key_buffer, key_first, window) + key_piece,
            key_first,
            0,
        )
        value_buffer = lax.dynamic_update_slice_in_dim(
            value_buffer,
            lax.dynamic_slice_in_dim(value_buffer, key_first, window) + value_piece,
            key_first,
            0,
        )
    key_terms = from_pack(key_buffer, placement, margin, BLK, total_rows)
    value_terms = from_pack(value_buffer, placement, margin, BLK, total_rows)
    d_keys, d_values = (
        lax.psum_scatter(
            key_terms.astype(jnp.bfloat16), "seq", scatter_dimension=0, tiled=True
        ).astype(jnp.float32),
        lax.psum_scatter(
            value_terms.astype(jnp.bfloat16), "seq", scatter_dimension=0, tiled=True
        ).astype(jnp.float32),
    )
    d_query = jnp.concatenate(d_query_list, axis=0)
    d_query_b = d_query.reshape(own_rows, head_span).astype(jnp.bfloat16)
    d_keys_b = d_keys.astype(jnp.bfloat16)
    d_values_b = d_values.astype(jnp.bfloat16)
    grad_bias_qv = jnp.stack(
        [
            jnp.sum(d_query_b.astype(jnp.float32), axis=0),
            jnp.sum(d_values_b.astype(jnp.float32), axis=0),
        ]
    )
    d_mixed = jnp.concatenate([d_query_b, d_keys_b, d_values_b], axis=1)
    grad_w_qkv = jnp.einsum(
        "td,tc->dc", rows_all, d_mixed, preferred_element_type=jnp.float32
    ).reshape(model_width, 3, head_span)
    d_normed = lax.psum_scatter(
        jnp.einsum("tc,dc->td", d_mixed, flat_qkv, preferred_element_type=jnp.float32).astype(
            jnp.bfloat16
        ),
        "tp",
        scatter_dimension=0,
        tiled=True,
    ).astype(jnp.float32)
    d_input_part, gain_first, shift_first = back_first(d_normed)
    grad_x = d_hidden + d_input_part
    summed = (
        lax.psum(grad_w_qkv.astype(jnp.bfloat16), "seq").astype(jnp.float32),
        lax.psum(grad_bias_qv.astype(jnp.bfloat16), "seq").astype(jnp.float32),
        lax.psum(grad_w_out.astype(jnp.bfloat16), "seq").astype(jnp.float32),
        lax.psum(grad_w_up.astype(jnp.bfloat16), "seq").astype(jnp.float32),
        lax.psum(grad_bias_up.astype(jnp.bfloat16), "seq").astype(jnp.float32),
        lax.psum(grad_w_down.astype(jnp.bfloat16), "seq").astype(jnp.float32),
    )
    gain_stack = jnp.stack([gain_first, gain_second, gain_third, gain_last])
    shift_stack = jnp.stack([shift_first, shift_second, shift_third, shift_last])
    vectors = lax.psum((gain_stack, shift_stack, grad_bias_out, grad_bias_down), ("seq", "tp"))
    return (
        result,
        grad_x,
        summed[0],
        summed[1],
        summed[2],
        vectors[2],
        summed[3],
        summed[4],
        summed[5],
        vectors[3],
        vectors[0],
        vectors[1],
    )


def solution(mesh):
    placed = (
        P(("seq", "tp"), None),
        P(None, None, "tp"),
        P(None, "tp"),
        P("tp", None),
        P(),
        P(None, "tp"),
        P("tp"),
        P("tp", None),
        P(),
        P(),
        P(),
        P(("seq", "tp"), None),
        P(),
        P(),
        P(),
    )
    return jax.shard_map(
        local,
        mesh=mesh,
        in_specs=placed,
        out_specs=(
            P(("seq", "tp"), None),
            P(("seq", "tp"), None),
            P(None, None, "tp"),
            P(None, "tp"),
            P("tp", None),
            P(),
            P(None, "tp"),
            P("tp"),
            P("tp", None),
            P(),
            P(),
            P(),
        ),
        check_vma=False,
    )
```

profile of v0, /device:TPU:0, one launch (start us, length us, event | category | flops | bytes accessed | tf_op | source)
XLA Modules:
  0.0 2150.0 jit_solution(2764487330214572565)
XLA Ops:
  21.5 31.1 %all-gather.8.cloned.1.call-done = bf16[1024,1024]{1,0:T(8,128)(2,1)} async-done(((bf16[512,1024]{1,0:T(8,128)(2,1)}), bf16[1024,1024]{1,0:T(8,128)(2,1)}) %all-gather.8.cloned.1.call-update) | async-done | bytes 2097168 | tf_op jit(solution)/shard_map/all_gather | solution.py:176
  71.7 117.1 %all-gather.10.cloned.1.call-done = bf16[16384,512]{0,1:T(8,128)(2,1)} async-done(((bf16[1024,512]{0,1:T(8,128)(2,1)}), bf16[16384,512]{0,1:T(8,128)(2,1)}) %all-gather.10.cloned.1.call-update) | async-done | bytes 16777232 | tf_op jit(solution)/shard_map/all_gather | solution.py:186
  188.9 22.2 %copy.61 = bf16[16384,512]{1,0:T(8,128)(2,1)} copy(bf16[16384,512]{0,1:T(8,128)(2,1)} %all-gather.10.cloned.1.call-done) | data formatting | bytes 33554432 | tf_op jit(solution)/shard_map/reshape | solution.py:52
  224.4 92.4 %all-gather.18.cloned.1.call-done = bf16[16384,1,512]{0,2,1:T(8,128)(2,1)} async-done(((bf16[1024,1,512]{0,2,1:T(8,128)(2,1)}), bf16[16384,1,512]{0,2,1:T(8,128)(2,1)}) %all-gather.18.cloned.1.call-update) | async-done | bytes 16777232 | tf_op jit(solution)/shard_map/all_gather | solution.py:185
  316.7 22.4 %copy.60 = bf16[16384,1,512]{2,0,1:T(8,128)(2,1)} copy(bf16[16384,1,512]{0,2,1:T(8,128)(2,1)} %all-gather.18.cloned.1.call-done) | data formatting | bytes 33554432 | tf_op jit(solution)/shard_map/reshape | solution.py:52
  352.3 23.1 %broadcast_select_fusion = (bf16[32,512,512]{2,1,0:T(8,128)(2,1)}, bf16[32,512,512]{2,1,0:T(8,128)(2,1)}) fusion(bf16[32,512,512]{2,1,0:T(8,128)(2,1)} %gather_fusion.1, pred[32]{0:T(512)(128)(4,1)S(1)} %get-tuple-element.659, bf16[32,512,512]{2,1,0:T(8,128)(2,1)} %gather_fusion), kind=kLoop, calls=%fused_computation.107 | loop fusion | flops 16777216 | bytes 67108896 | tf_op jit(solution)/shard_map/jit(_take)/select_n | solution.py:53
  375.4 21.3 copy.52
  396.7 21.2 copy.50
  417.9 14.8 pad.7
  441.8 14.8 pad.8
  465.7 100.4 %while.56 = (s32[]{:T(128)}, f32[8,512,64]{1,2,0:T(8,128)S(1)}, f32[8,512]{1,0:T(8,128)S(1)}, s32[8]{0:T(128)S(1)}, bf16[512,8,64]{0,2,1:T(8,128)(2,1)S(1)}, /*i...) while((s32[]{:T(128)}, f32[8,512,64]{1,2,0:T(8,128)S(1)}, ...), condition=%wide.region_9.11_spmd.clone, body=%wide.region_6.10_spmd.clone.sunk | while | flops 702545408 | bytes 33036496 | solution.py:85
  567.1 101.0 %while.57 = (s32[]{:T(128)}, f32[8,512,64]{1,2,0:T(8,128)S(1)}, f32[8,512]{1,0:T(8,128)S(1)}, s32[8]{0:T(128)S(1)}, bf16[512,8,64]{0,2,1:T(8,128)(2,1)}, /*index...) while((s32[]{:T(128)}, f32[8,512,64]{1,2,0:T(8,128)S(1)}, ...), condition=%wide.region_13.15_spmd.clone, body=%wide.region_10.14_spmd.clone.sunk | while | flops 702545408 | bytes 33036496 | solution.py:85
  672.4 30.1 %reduce-scatter.7.cloned.1.call-done = bf16[512,1024]{1,0:T(8,128)(2,1)} async-done(((bf16[1024,1024]{1,0:T(8,128)(2,1)}), bf16[512,1024]{1,0:T(8,128)(2,1)}) %reduce-scatter.7.cloned.1.call-update) | async-done | bytes 1048592 | tf_op jit(solution)/shard_map/reduce_scatter | solution.py:207
  712.0 33.2 %all-gather.12.cloned.1.call-done = bf16[1024,1024]{1,0:T(8,128)(2,1)} async-done(((bf16[512,1024]{1,0:T(8,128)(2,1)}), bf16[1024,1024]{1,0:T(8,128)(2,1)}) %all-gather.12.cloned.1.call-update) | async-done | bytes 2097168 | tf_op jit(solution)/shard_map/all_gather | solution.py:216
  762.4 31.9 %reduce-scatter.9.cloned.1.call-done = bf16[512,1024]{1,0:T(8,128)(2,1)} async-done(((bf16[1024,1024]{1,0:T(8,128)(2,1)}), bf16[512,1024]{1,0:T(8,128)(2,1)}) %reduce-scatter.9.cloned.1.call-update) | async-done | bytes 1048592 | tf_op jit(solution)/shard_map/reduce_scatter | solution.py:222
  804.1 32.8 %all-gather.14.cloned.1.call-done = bf16[1024,1024]{1,0:T(8,128)(2,1)} async-done(((bf16[512,1024]{1,0:T(8,128)(2,1)}), bf16[1024,1024]{1,0:T(8,128)(2,1)}) %all-gather.14.cloned.1.call-update) | async-done | bytes 2097168 | tf_op jit(solution)/shard_map/all_gather | solution.py:232
  837.0 13.8 fusion.130
  858.6 31.9 %reduce-scatter.11.cloned.1.call-done = bf16[512,1024]{1,0:T(8,128)(2,1)} async-done(((bf16[1024,1024]{1,0:T(8,128)(2,1)}), bf16[512,1024]{1,0:T(8,128)(2,1)}) %reduce-scatter.11.cloned.1.call-update) | async-done | bytes 1048592 | tf_op jit(solution)/shard_map/reduce_scatter | solution.py:239
  904.5 32.4 %all-gather.16.cloned.1.call-done = bf16[1024,1024]{1,0:T(8,128)(2,1)} async-done(((bf16[512,1024]{1,0:T(8,128)(2,1)}), bf16[1024,1024]{1,0:T(8,128)(2,1)}) %all-gather.16.cloned.1.call-update) | async-done | bytes 2097168 | tf_op jit(solution)/shard_map/all_gather | solution.py:251
  950.6 156.5 %while.58 = (s32[]{:T(128)}, bf16[8,512,64]{1,2,0:T(8,128)(2,1)S(1)}, f32[8,5120,64]{1,2,0:T(8,128)}, f32[8,5120,64]{1,2,0:T(8,128)}, s32[8]{0:T(128)S(1)}, /*in...) while((s32[]{:T(128)}, ...), condition=%wide.region_31.33_spmd.clone, body=%wide.region_30.32_spmd.clone.sunk | while | flops 1706917888 | bytes 52231424 | solution.py:120
  1140.7 156.6 %while.59 = (s32[]{:T(128)}, bf16[8,512,64]{1,2,0:T(8,128)(2,1)S(1)}, f32[8,5120,64]{1,2,0:T(8,128)}, f32[8,5120,64]{1,2,0:T(8,128)}, s32[8]{0:T(128)S(1)}, /*in...) while((s32[]{:T(128)}, ...), condition=%wide.region_33.35_spmd.clone, body=%wide.region_32.34_spmd.clone.sunk | while | flops 1706917888 | bytes 52231424 | solution.py:120
  1320.5 19.1 broadcast.235.clone
  1344.8 13.4 add_dynamic-update-slice_fusion.1
  1358.3 19.2 slice.130
  1377.5 17.0 broadcast.235.clone.1
  1413.2 17.4 slice.131
  1457.1 26.0 %select_convert_fusion.1 = (bf16[32,512,512]{2,1,0:T(8,128)(2,1)}, bf16[32,512,512]{2,1,0:T(8,128)(2,1)}) fusion(bf16[32,512,512]{2,1,0:T(8,128)(2,1)} %gather_fusion.2, pred[32]{0:T(512)(128)(4,1)S(1)} %copy-done.66, bf16[32,512,512]{2,1,0:T(8,128)(2,1)} %gather_fusion.3), kind=kLoop, calls=%fused_computation.106 | loop fusion | flops 16777216 | bytes 67108896 | tf_op jit(solution)/shard_map/convert_element_type | solution.py:294
  1485.3 176.6 %reduce-scatter.15.cloned.1.call-done = bf16[1024,512]{1,0:T(8,128)(2,1)} async-done(((bf16[16384,512]{1,0:T(8,128)(2,1)}), bf16[1024,512]{1,0:T(8,128)(2,1)}) %reduce-scatter.15.cloned.1.call-update) | async-done | bytes 1048592 | tf_op jit(solution)/shard_map/reduce_scatter | solution.py:296
  1661.9 182.2 %reduce-scatter.13.cloned.1.call-done = bf16[1024,512]{1,0:T(8,128)(2,1)} async-done(((bf16[16384,512]{1,0:T(8,128)(2,1)}), bf16[1024,512]{1,0:T(8,128)(2,1)}) %reduce-scatter.13.cloned.1.call-update) | async-done | bytes 1048592 | tf_op jit(solution)/shard_map/reduce_scatter | solution.py:293
  1887.6 34.3 %all-reduce.3 = (bf16[2,512]{1,0:T(2,128)(2,1)S(1)}, bf16[2048]{0:T(1024)(128)(2,1)S(1)}) all-reduce(bf16[2,512]{1,0:T(2,128)(2,1)S(1)} %pad_maximum_fusion.6, bf16[2048]{0:T(1024)(128)(2,1)S(1)} %copy-done.65), channel_id=1, replica_groups=mesh['seq'=16,'tp'=2] {'seq'}, use_global_device_ids=true, to_apply=%region_42.45 | all-reduce | flops 3072 | bytes 12288 | tf_op jit(solution)/shard_map/psum | solution.py:326
  1927.6 39.9 %all-reduce.2 = (f32[1024]{0:T(1024)}, f32[1024]{0:T(1024)}, f32[4,1024]{1,0:T(4,128)}, f32[4,1024]{1,0:T(4,128)}) all-reduce(f32[1024]{0:T(1024)S(1)} %copy-done.48, f32[1024]{0:T(1024)S(1)} %copy-done.47, f32[4,1024]{1,0:T(4,128)S(1)} %pad_maximum_fusion.4, ...), channel_id=1, replica_groups=mesh['seq'=16,'tp'=2] {'seq','tp'}, use_global_device_ids=true, to_apply=%region_45.48 | all-reduce | flops 10240 | bytes 81920 | tf_op jit(solution)/shard_map/psum | solution.py:334
  1970.8 153.0 %all-reduce.7.cloned.1.call-done = (bf16[1024,3,512]{0,2,1:T(8,128)(2,1)}, bf16[512,1024]{1,0:T(8,128)(2,1)}, bf16[1024,2048]{1,0:T(8,128)(2,1)}, bf16[2048,1024]{1,0:T(8,128)(2,1)}) async-done(((bf16[1024,3,512]{0,2,1:T(8,128)(2,1)}, bf16[512,1024]{1,0:T(8,128)(2,1)}, bf16[1024,2048]{1,0:T(8,128)(2,1)}, bf16[2048,1024]{1,0:T(8,128)(2,1)}), (bf16[1024,3,512]{0,2,1:T(8,128)(2,1)}, ...) | async-done | bytes 12582928 | tf_op jit(solution)/shard_map/psum | solution.py:325
  (553 shorter events, 784.5 us)
Async XLA Ops:
  7.2 662.3 %copy-start = (bf16[512,1024]{1,0:T(8,128)(2,1)S(1)}, bf16[512,1024]{1,0:T(8,128)(2,1)}, u32[]{:S(2)}) copy-start(bf16[512,1024]{1,0:T(8,128)(2,1)} %param.30) | copy-start | bytes 3145732
  7.2 45.4 %all-gather.8.cloned.1.call-start = ((), (), s32[]{:S(2)}) async-start(), calls=%async_computation.6 | async-start | bytes 3145728 | tf_op jit(solution)/shard_map/all_gather | solution.py:176
  16.7 172.2 %all-gather.10.cloned.1.call-start = ((), (), s32[]{:S(2)}) async-start(), calls=%async_computation.7 | async-start | bytes 17825792 | tf_op jit(solution)/shard_map/all_gather | solution.py:186
  61.7 255.0 %all-gather.18.cloned.1.call-start = ((), (), s32[]{:S(2)}) async-start(), calls=%async_computation.17 | async-start | bytes 17825792 | tf_op jit(solution)/shard_map/all_gather | solution.py:185
  64.5 638.0 %reduce-scatter.7.cloned.1.call-start = ((), (), s32[]{:S(2)}) async-start(), calls=%async_computation.8 | async-start | bytes 3145728 | tf_op jit(solution)/shard_map/reduce_scatter | solution.py:207
  465.6 101.4 %copy-start.37 = (s32[5120]{0:T(1024)S(1)}, s32[5120]{0:T(1024)}, u32[]{:S(2)}) copy-start(s32[5120]{0:T(1024)} %get-tuple-element.1177) | copy-start | bytes 61444
  465.7 101.4 %copy-start.41 = (s32[5120]{0:T(1024)S(1)}, s32[5120]{0:T(1024)}, u32[]{:S(2)}) copy-start(s32[5120]{0:T(1024)} %get-tuple-element.1180) | copy-start | bytes 61444
  465.7 101.4 %copy-start.60 = (pred[5120]{0:T(1024)(128)(4,1)S(1)}, pred[5120]{0:T(1024)(128)(4,1)}, u32[]{:S(2)}) copy-start(pred[5120]{0:T(1024)(128)(4,1)} %get-tuple-element.1181) | copy-start | bytes 15364
  465.7 101.4 %copy-start.71 = (s32[512]{0:T(512)S(1)}, s32[512]{0:T(512)}, u32[]{:S(2)}) copy-start(s32[512]{0:T(512)} %get-tuple-element.1178) | copy-start | bytes 6148
  465.7 101.4 %copy-start.73 = (s32[512]{0:T(512)S(1)}, s32[512]{0:T(512)}, u32[]{:S(2)}) copy-start(s32[512]{0:T(512)} %get-tuple-element.1179) | copy-start | bytes 6148
  566.2 102.0 %copy-start.16 = (f32[8,512,64]{1,2,0:T(8,128)}, f32[8,512,64]{1,2,0:T(8,128)S(1)}, u32[]{:S(2)}) copy-start(f32[8,512,64]{1,2,0:T(8,128)S(1)} %get-tuple-element.228) | copy-start | bytes 3145732
  672.1 73.1 %all-gather.12.cloned.1.call-start = ((), (), s32[]{:S(2)}) async-start(), calls=%async_computation.9 | async-start | bytes 3145728 | tf_op jit(solution)/shard_map/all_gather | solution.py:216
  711.9 82.4 %reduce-scatter.9.cloned.1.call-start = ((), (), s32[]{:S(2)}) async-start(), calls=%async_computation.10 | async-start | bytes 3145728 | tf_op jit(solution)/shard_map/reduce_scatter | solution.py:222
  712.0 125.0 %copy-start.57 = (f32[2048]{0:T(1024)}, f32[2048]{0:T(1024)S(1)}, u32[]{:S(2)}) copy-start(f32[2048]{0:T(1024)S(1)} %convert_element_type.188) | copy-start | bytes 24580
  762.3 74.6 %all-gather.14.cloned.1.call-start = ((), (), s32[]{:S(2)}) async-start(), calls=%async_computation.11 | async-start | bytes 3145728 | tf_op jit(solution)/shard_map/all_gather | solution.py:232
  803.7 86.8 %reduce-scatter.11.cloned.1.call-start = ((), (), s32[]{:S(2)}) async-start(), calls=%async_computation.12 | async-start | bytes 3145728 | tf_op jit(solution)/shard_map/reduce_scatter | solution.py:239
  858.5 78.3 %all-gather.16.cloned.1.call-start = ((), (), s32[]{:S(2)}) async-start(), calls=%async_computation.13 | async-start | bytes 3145728 | tf_op jit(solution)/shard_map/all_gather | solution.py:251
  903.6 758.4 %reduce-scatter.15.cloned.1.call-start = ((), (), s32[]{:S(2)}) async-start(), calls=%async_computation.15 | async-start | bytes 17825792 | tf_op jit(solution)/shard_map/reduce_scatter | solution.py:296
  1483.1 361.0 %reduce-scatter.13.cloned.1.call-start = ((), (), s32[]{:S(2)}) async-start(), calls=%async_computation.14 | async-start | bytes 17825792 | tf_op jit(solution)/shard_map/reduce_scatter | solution.py:293
  1483.9 439.2 %reduce-scatter.17.cloned.1.call-start = ((), (), s32[]{:S(2)}) async-start(), calls=%async_computation.16 | async-start | bytes 3145728 | tf_op jit(solution)/shard_map/reduce_scatter | solution.py:314
  1851.5 272.4 %all-reduce.7.cloned.1.call-start = ((), (), s32[]{:S(2)}) async-start(), calls=%async_computation.18 | async-start | bytes 25165824 | tf_op jit(solution)/shard_map/psum | solution.py:325
  1885.7 39.3 %copy-start.51 = (f32[1024]{0:T(1024)S(1)}, f32[1024]{0:T(1024)}, u32[]{:S(2)}) copy-start(f32[1024]{0:T(1024)} %get-tuple-element.467) | copy-start | bytes 12292
  1885.7 39.3 %copy-start.53 = (f32[1024]{0:T(1024)S(1)}, f32[1024]{0:T(1024)}, u32[]{:S(2)}) copy-start(f32[1024]{0:T(1024)} %get-tuple-element.470) | copy-start | bytes 12292
  1885.8 39.3 %copy-start.55 = (f32[1024]{0:T(1024)S(1)}, f32[1024]{0:T(1024)}, u32[]{:S(2)}) copy-start(f32[1024]{0:T(1024)} %get-tuple-element.466) | copy-start | bytes 12292
  1885.8 39.3 %copy-start.46 = (f32[512]{0:T(512)S(1)}, f32[512]{0:T(512)}, u32[]{:S(2)}) copy-start(f32[512]{0:T(512)} %copy-done.45) | copy-start | bytes 6148
  1885.8 39.3 %copy-start.36 = (f32[512]{0:T(512)S(1)}, f32[512]{0:T(512)}, u32[]{:S(2)}) copy-start(f32[512]{0:T(512)} %copy-done.35) | copy-start | bytes 6148
  1885.8 41.8 %copy-start.49 = (f32[1024]{0:T(1024)S(1)}, f32[1024]{0:T(1024)}, u32[]{:S(2)}) copy-start(f32[1024]{0:T(1024)} %get-tuple-element.462) | copy-start | bytes 12292
  1885.8 41.7 %copy-start.52 = (f32[1024]{0:T(1024)S(1)}, f32[1024]{0:T(1024)}, u32[]{:S(2)}) copy-start(f32[1024]{0:T(1024)} %get-tuple-element.458) | copy-start | bytes 12292
  1885.8 41.7 %copy-start.54 = (f32[1024]{0:T(1024)S(1)}, f32[1024]{0:T(1024)}, u32[]{:S(2)}) copy-start(f32[1024]{0:T(1024)} %get-tuple-element.460) | copy-start | bytes 12292
  1885.8 41.8 %copy-start.47 = (f32[1024]{0:T(1024)S(1)}, f32[1024]{0:T(1024)}, u32[]{:S(2)}) copy-start(f32[1024]{0:T(1024)} %get-tuple-element.622) | copy-start | bytes 12292
  1885.8 41.8 %copy-start.48 = (f32[1024]{0:T(1024)S(1)}, f32[1024]{0:T(1024)}, u32[]{:S(2)}) copy-start(f32[1024]{0:T(1024)} %get-tuple-element.624) | copy-start | bytes 12292
  1885.8 81.6 %copy-start.10 = (f32[512,1024]{1,0:T(8,128)S(1)}, f32[512,1024]{1,0:T(8,128)}, u32[]{:S(2)}) copy-start(f32[512,1024]{1,0:T(8,128)} %copy-done.9) | copy-start | bytes 6291460
  (77 other events, 833.3 us)
Sparse Core Ops, SparseCore 0:
  16.8 35.8 all-gather.7
  61.9 126.9 all-gather.9
  191.6 125.0 all-gather.17
  672.2 30.2 reduce-scatter.6
  712.0 33.1 all-gather.11
  762.5 31.8 reduce-scatter.8
  803.8 33.1 all-gather.13
  858.6 31.8 reduce-scatter.10
  903.7 33.1 all-gather.15
  1483.2 178.6 reduce-scatter.14
  1666.6 177.5 reduce-scatter.12
  1851.6 30.7 reduce-scatter.16
  1887.5 236.2 all-reduce.6
where the time goes:
time: 2170 us; the launch traced here: 2150 us
  waiting for transfers between devices  946 us (44%)
  matrix products  476 us (22%)
  local copies, waits for them, and re-layouts  404 us (19%)
  other arithmetic  169 us (8%)
  blocking collectives  74.2 us (3%)
  loops' own time  63.9 us (3%)
    reduce_scatter x1, waiting for transfers between devices, local(): lax.psum_scatter(key_terms.astype(jnp.bfloat16), 'seq', scatter_dimension...  182 us
    reduce_scatter x1, waiting for transfers between devices, local(): lax.psum_scatter(value_terms.astype(jnp.bfloat16), 'seq', scatter_dimensi...  177 us
    dot_general x32, matrix products, masked_scores(): jnp.einsum('qe,ke->qk', query_h, key_h, preferred_element_type=jnp.float32)  170 us
    psum x1, waiting for transfers between devices, local(): lax.psum(grad_w_qkv.astype(jnp.bfloat16), 'seq').astype(jnp.float32)  153 us
    all_gather x1, waiting for transfers between devices, local(): lax.all_gather(value_b, 'seq', axis=0, tiled=True)  117 us
    all_gather x1, waiting for transfers between devices, local(): lax.all_gather(key_b, 'seq', axis=0, tiled=True)  92.4 us
    another operation x10, local copies, waits for them, and re-layouts  57.3 us
    dot_general x16, matrix products, forward_one_head(): output = jnp.dot(probs_b, value_h, preferred_element_type=jnp.float32)  53.1 us
  transfers between devices with their start and end apart: 13, of which 12 were waited for; matrix products, arithmetic and copies ran while one was open for 4% of the time, Pallas kernels for 0%

commit v1 on v0

--- a/solution.py
+++ b/solution.py
@@ -1,14 +1,23 @@
+import functools
+
 import jax
 import jax.numpy as jnp
 from jax import lax
+from jax.experimental import pallas as pl
+from jax.experimental.pallas import tpu as pltpu
 from jax.sharding import PartitionSpec as P
 
 HEAD = 64
 BLK = 512
+HALF = BLK // 2
+QUART = BLK // 4
 LONGEST = 4096
-
+VMEM_LIMIT = 58 << 20
 
 EPS = 1e-05
+F32 = jnp.float32
+BF16 = jnp.bfloat16
+MESH = pl.DeviceIdType.MESH
 
 
 def layer_norm(row_block, gain_row, shift_row):
@@ -22,9 +31,599 @@
     return jax.nn.gelu(values, approximate=True)
 
 
+def running_ends(lengths):
+    count = lengths.shape[0]
+    index = jnp.arange(count, dtype=jnp.int32)
+    return jnp.sum(jnp.where(index[None, :] <= index[:, None], lengths[None, :], 0), axis=1)
+
+
+def inverse_order(placement):
+    index = jnp.arange(placement.shape[0], dtype=jnp.int32)
+    return jnp.sum(jnp.where(placement[None, :] == index[:, None], index[None, :], 0), axis=1)
+
+
+def block_tables(lengths, prefixes, placement, part):
+    ends = running_ends(lengths)
+    starts = ends - lengths
+    limits = starts + prefixes
+    offset = part * HALF + jnp.arange(HALF, dtype=jnp.int32)
+    pos = placement[:, None] * BLK + offset[None, :]
+    inside = (pos[:, :, None] >= starts) & (pos[:, :, None] < ends)
+
+    def pick(values):
+        return jnp.sum(jnp.where(inside, values, 0), axis=2)
+
+    low = pick(starts)
+    high = jnp.minimum(pick(ends), jnp.maximum(pos + 1, pick(limits)))
+    table = jnp.stack(
+        [
+            jnp.min(low, axis=1) // BLK,
+            (jnp.max(high, axis=1) - 1) // BLK + 1,
+            jnp.max(low, axis=1),
+            jnp.min(high, axis=1),
+            inverse_order(placement),
+        ]
+    )
+    return low[:, None, :], high[:, None, :], table
+
+
+def fill_keys(part, own_ref, sib_ref, kv, kvt):
+    other = 1 - part
+
+    def one(b, carry):
+        kv[b, pl.ds(pl.multiple_of(part * HALF, HALF), HALF), :] = own_ref[b]
+        kv[b, pl.ds(pl.multiple_of(other * HALF, HALF), HALF), :] = sib_ref[b]
+        kvt[b] = kv[b].astype(F32).T.astype(BF16)
+        return carry
+
+    lax.fori_loop(0, kv.shape[0], one, 0)
+
+
+def unpack_t(packed):
+    turned = packed.astype(F32).T
+    return jnp.concatenate([turned[:HEAD], turned[HEAD:]], axis=1)
+
+
+def pack_t(turned):
+    return jnp.concatenate([turned[:, :QUART], turned[:, QUART:]], axis=0).T
+
+
+def attend_kernel(part_ref, tab, low_ref, high_ref, q_ref, own_ref, sib_ref, out_ref, ot_ref, lse_ref, kv, kvt):
+    fill_keys(part_ref[0], own_ref, sib_ref, kv, kvt)
+    scale = HEAD**-0.5
+    depth = lax.broadcasted_iota(jnp.int32, (BLK, HALF), 0)
+
+    def one(b, carry):
+        qt = unpack_t(q_ref[b]) * scale
+        rhs = jnp.concatenate([qt, jnp.zeros_like(qt)], axis=0).astype(BF16)
+        low, high = low_ref[b], high_ref[b]
+
+        def step(kb, state, masked):
+            top, total, acc = state
+            st = tab[4, kb]
+            sc = jnp.dot(kv[st], rhs, preferred_element_type=F32)
+            if masked:
+                pos = depth + kb * BLK
+                sc = jnp.where((pos >= low) & (pos < high), sc, -1e30)
+            new = jnp.maximum(top, jnp.max(sc, axis=0, keepdims=True))
+            alpha = jnp.exp(top - new)
+            pr = jnp.exp(sc - new)
+            total = total * alpha + jnp.sum(pr, axis=0, keepdims=True)
+            acc = acc * alpha + jnp.dot(
+                kvt[st, HEAD:, :], pr.astype(BF16), preferred_element_type=F32
+            )
+            return new, total, acc
+
+        def visit(kb, state):
+            whole = (kb * BLK >= tab[2, b]) & ((kb + 1) * BLK <= tab[3, b])
+            return lax.cond(
+                whole,
+                lambda st: step(kb, st, False),
+                lambda st: step(kb, st, True),
+                state,
+            )
+
+        start = (
+            jnp.full((1, HALF), -1e30, F32),
+            jnp.zeros((1, HALF), F32),
+            jnp.zeros((HEAD, HALF), F32),
+        )
+        top, total, acc = lax.fori_loop(tab[0, b], tab[1, b], visit, start)
+        ot = acc / total
+        ot_ref[b] = ot
+        lse_ref[b] = top + jnp.log(total)
+        out_ref[b] = pack_t(ot).astype(BF16)
+        return carry
+
+    lax.fori_loop(0, q_ref.shape[0], one, 0)
+
+
+def attend_back_kernel(
+    part_ref, tab, low_ref, high_ref, q_ref, own_ref, sib_ref, da_ref, ot_ref, lse_ref,
+    dq_ref, mine_ref, theirs_ref, kv, kvt, dkv,
+):
+    part = part_ref[0]
+    fill_keys(part, own_ref, sib_ref, kv, kvt)
+    scale = HEAD**-0.5
+    depth = lax.broadcasted_iota(jnp.int32, (BLK, HALF), 0)
+    lane = lax.broadcasted_iota(jnp.int32, (HALF, 2 * HEAD), 1)
+
+    def clear(b, carry):
+        dkv[b] = jnp.zeros((BLK, 2 * HEAD), F32)
+        return carry
+
+    lax.fori_loop(0, dkv.shape[0], clear, 0)
+
+    def one(b, carry):
+        qt = unpack_t(q_ref[b]) * scale
+        dat = unpack_t(da_ref[b])
+        blank = jnp.zeros_like(qt)
+        rhs_q = jnp.concatenate([qt, blank], axis=0).astype(BF16)
+        rhs_d = jnp.concatenate([blank, dat], axis=0).astype(BF16)
+        both = jnp.concatenate([qt, dat], axis=0).T
+        rows_q = jnp.where(lane < HEAD, both, 0.0).astype(BF16)
+        rows_d = jnp.where(lane < HEAD, 0.0, both).astype(BF16)
+        total = jnp.sum(dat * ot_ref[b], axis=0, keepdims=True)
+        lse = lse_ref[b]
+        low, high = low_ref[b], high_ref[b]
+
+        def step(kb, acc, masked):
+            st = tab[4, kb]
+            keys = kv[st]
+            sc = jnp.dot(keys, rhs_q, preferred_element_type=F32)
+            dp = jnp.dot(keys, rhs_d, preferred_element_type=F32)
+            if masked:
+                pos = depth + kb * BLK
+                sc = jnp.where((pos >= low) & (pos < high), sc, -1e30)
+            pr = jnp.exp(sc - lse)
+            ds = (pr * (dp - total)).astype(BF16)
+            dkv[st] += jnp.dot(ds, rows_q, preferred_element_type=F32) + jnp.dot(
+                pr.astype(BF16), rows_d, preferred_element_type=F32
+            )
+            return acc + jnp.dot(kvt[st, :HEAD, :], ds, preferred_element_type=F32)
+
+        def visit(kb, acc):
+            whole = (kb * BLK >= tab[2, b]) & ((kb + 1) * BLK <= tab[3, b])
+            return lax.cond(
+                whole, lambda a: step(kb, a, False), lambda a: step(kb, a, True), acc
+            )
+
+        acc = lax.fori_loop(tab[0, b], tab[1, b], visit, jnp.zeros((HEAD, HALF), F32))
+        dq_ref[b] = pack_t(acc * scale).astype(BF16)
+        return carry
+
+    lax.fori_loop(0, q_ref.shape[0], one, 0)
+    other = 1 - part
+
+    def split(b, carry):
+        mine_ref[b] = dkv[b, pl.ds(pl.multiple_of(part * HALF, HALF), HALF), :]
+        theirs_ref[b] = dkv[b, pl.ds(pl.multiple_of(other * HALF, HALF), HALF), :].astype(BF16)
+        return carry
+
+    lax.fori_loop(0, dkv.shape[0], split, 0)
+
+
+def vmem(count):
+    return [pl.BlockSpec(memory_space=pltpu.VMEM)] * count
+
+
+def smem(count):
+    return [pl.BlockSpec(memory_space=pltpu.SMEM)] * count
+
+
+def attend(part, tables, q_chunks, kv_own, kv_sib):
+    low, high, table = tables
+    blocks = q_chunks.shape[0]
+    return pl.pallas_call(
+        attend_kernel,
+        out_shape=(
+            jax.ShapeDtypeStruct((blocks, QUART, 2 * HEAD), BF16),
+            jax.ShapeDtypeStruct((blocks, HEAD, HALF), F32),
+            jax.ShapeDtypeStruct((blocks, 1, HALF), F32),
+        ),
+        in_specs=smem(2) + vmem(5),
+        out_specs=tuple(vmem(3)),
+        scratch_shapes=[
+            pltpu.VMEM((blocks, BLK, 2 * HEAD), BF16),
+            pltpu.VMEM((blocks, 2 * HEAD, BLK), BF16),
+        ],
+        compiler_params=pltpu.CompilerParams(vmem_limit_bytes=VMEM_LIMIT),
+        name="attend",
+    )(part.reshape(1), table, low, high, q_chunks, kv_own, kv_sib)
+
+
+def attend_back(part, tables, q_chunks, kv_own, kv_sib, da_chunks, out_t, mass):
+    low, high, table = tables
+    blocks = q_chunks.shape[0]
+    return pl.pallas_call(
+        attend_back_kernel,
+        out_shape=(
+            jax.ShapeDtypeStruct((blocks, QUART, 2 * HEAD), BF16),
+            jax.ShapeDtypeStruct((blocks, HALF, 2 * HEAD), F32),
+            jax.ShapeDtypeStruct((blocks, HALF, 2 * HEAD), BF16),
+        ),
+        in_specs=smem(2) + vmem(8),
+        out_specs=tuple(vmem(3)),
+        scratch_shapes=[
+            pltpu.VMEM((blocks, BLK, 2 * HEAD), BF16),
+            pltpu.VMEM((blocks, 2 * HEAD, BLK), BF16),
+            pltpu.VMEM((blocks, BLK, 2 * HEAD), F32),
+        ],
+        compiler_params=pltpu.CompilerParams(vmem_limit_bytes=VMEM_LIMIT),
+        name="attend_back",
+    )(part.reshape(1), table, low, high, q_chunks, kv_own, kv_sib, da_chunks, out_t, mass)
+
+
+def chunk_of(who, quarter, index, half):
+    absolute = (who[0] * 2 + who[1]) ^ quarter
+    tp, sub = absolute // 2, absolute % 2
+    return ((sub * 4 + index) * 2 + half) * 2 + tp
+
+
+def swap_lanes(values):
+    return pltpu.roll(values, HEAD, 1)
+
+
+def low_lanes(rows):
+    return lax.broadcasted_iota(jnp.int32, (rows, 2 * HEAD), 1) < HEAD
+
+
+def store_packed(who, quarter, values, out_ref):
+    low = low_lanes(QUART)
+    for pair in range(2):
+        for half in range(2):
+            top = half * HALF
+            lanes = slice(pair * 128, pair * 128 + 128)
+            first, second = values[top : top + QUART, lanes], values[top + QUART : top + HALF, lanes]
+            even = jnp.where(low, first, swap_lanes(second))
+            odd = jnp.where(low, swap_lanes(first), second)
+            out_ref[chunk_of(who, quarter, 2 * pair, half)] = even.astype(BF16)
+            out_ref[chunk_of(who, quarter, 2 * pair + 1, half)] = odd.astype(BF16)
+
+
+def load_packed(who, quarter, ref, out_ref):
+    low = low_lanes(QUART)
+    for pair in range(2):
+        for half in range(2):
+            even = ref[chunk_of(who, quarter, 2 * pair, half)].astype(F32)
+            odd = ref[chunk_of(who, quarter, 2 * pair + 1, half)].astype(F32)
+            top = half * HALF
+            lanes = slice(quarter * 256 + pair * 128, quarter * 256 + pair * 128 + 128)
+            out_ref[top : top + QUART, lanes] = jnp.where(low, even, swap_lanes(odd)).astype(BF16)
+            out_ref[top + QUART : top + HALF, lanes] = jnp.where(low, swap_lanes(even), odd).astype(BF16)
+
+
+def project_kernel(who_ref, x_ref, gain_ref, shift_ref, bias_ref, w0, w1, w2, w3, normed_ref, q_ref, kv_ref):
+    who = (who_ref[0], who_ref[1])
+    normed = layer_norm(x_ref[...].astype(F32), gain_ref[...], shift_ref[...]).astype(BF16)
+    normed_ref[...] = normed
+    low = low_lanes(HALF)
+    for quarter, w in enumerate((w0, w1, w2, w3)):
+        def dot(col):
+            return jnp.dot(normed, w[:, col : col + 256], preferred_element_type=F32)
+
+        bias = bias_ref[quarter : quarter + 1, :].astype(F32)
+        store_packed(who, quarter, dot(0) + bias[:, :256], q_ref)
+        keys = dot(256)
+        values = dot(512) + bias[:, 256:]
+        for pair in range(2):
+            lanes = slice(pair * 128, pair * 128 + 128)
+            for half in range(2):
+                rows = slice(half * HALF, half * HALF + HALF)
+                k, v = keys[rows, lanes], values[rows, lanes]
+                even = jnp.where(low, k, swap_lanes(v))
+                odd = jnp.where(low, swap_lanes(k), v)
+                kv_ref[chunk_of(who, quarter, 2 * pair, half)] = even.astype(BF16)
+                kv_ref[chunk_of(who, quarter, 2 * pair + 1, half)] = odd.astype(BF16)
+
+
+def project(who, x, gain, shift, bias, weights):
+    rows, width = x.shape
+    return pl.pallas_call(
+        project_kernel,
+        out_shape=(
+            jax.ShapeDtypeStruct((rows, width), BF16),
+            jax.ShapeDtypeStruct((32, QUART, 2 * HEAD), BF16),
+            jax.ShapeDtypeStruct((32, HALF, 2 * HEAD), BF16),
+        ),
+        in_specs=smem(1) + vmem(8),
+        out_specs=tuple(vmem(3)),
+        compiler_params=pltpu.CompilerParams(vmem_limit_bytes=VMEM_LIMIT),
+        name="project",
+    )(who, x, gain, shift, bias, *weights)
+
+
+def unpack_heads_kernel(who_ref, ref, out_ref):
+    who = (who_ref[0], who_ref[1])
+    for quarter in range(4):
+        load_packed(who, quarter, ref, out_ref)
+
+
+def unpack_heads(who, chunks):
+    return pl.pallas_call(
+        unpack_heads_kernel,
+        out_shape=jax.ShapeDtypeStruct((BLK, 1024), BF16),
+        in_specs=smem(1) + vmem(1),
+        out_specs=vmem(1)[0],
+        compiler_params=pltpu.CompilerParams(vmem_limit_bytes=VMEM_LIMIT),
+        name="unpack_heads",
+    )(who, chunks)
+
+
+def spread_kernel(who_ref, d_ref, w0, w1, w2, w3, out_ref):
+    who = (who_ref[0], who_ref[1])
+    d_rows = d_ref[...]
+    for quarter, w in enumerate((w0, w1, w2, w3)):
+        values = lax.dot_general(
+            d_rows, w[...], (((1,), (1,)), ((), ())), preferred_element_type=F32
+        )
+        store_packed(who, quarter, values, out_ref)
+
+
+def spread(who, d_branch, weights):
+    return pl.pallas_call(
+        spread_kernel,
+        out_shape=jax.ShapeDtypeStruct((32, QUART, 2 * HEAD), BF16),
+        in_specs=smem(1) + vmem(5),
+        out_specs=vmem(1)[0],
+        compiler_params=pltpu.CompilerParams(vmem_limit_bytes=VMEM_LIMIT),
+        name="spread",
+    )(who, d_branch, *weights)
+
+
+def unpack_qkv_kernel(who_ref, dq_ref, dkv_ref, q_ref, k_ref, v_ref):
+    who = (who_ref[0], who_ref[1])
+    low = low_lanes(HALF)
+    for quarter in range(4):
+        load_packed(who, quarter, dq_ref, q_ref)
+        for pair in range(2):
+            lanes = slice(quarter * 256 + pair * 128, quarter * 256 + pair * 128 + 128)
+            for half in range(2):
+                rows = slice(half * HALF, half * HALF + HALF)
+                even = dkv_ref[chunk_of(who, quarter, 2 * pair, half)].astype(F32)
+                odd = dkv_ref[chunk_of(who, quarter, 2 * pair + 1, half)].astype(F32)
+                k_ref[rows, lanes] = jnp.where(low, even, swap_lanes(odd)).astype(BF16)
+                v_ref[rows, lanes] = jnp.where(low, swap_lanes(even), odd).astype(BF16)
+
+
+def unpack_qkv(who, dq_chunks, dkv_chunks):
+    shape = jax.ShapeDtypeStruct((BLK, 1024), BF16)
+    return pl.pallas_call(
+        unpack_qkv_kernel,
+        out_shape=(shape, shape, shape),
+        in_specs=smem(1) + vmem(2),
+        out_specs=tuple(vmem(3)),
+        compiler_params=pltpu.CompilerParams(vmem_limit_bytes=VMEM_LIMIT),
+        name="unpack_qkv",
+    )(who, dq_chunks, dkv_chunks)
+
+
+def sum_all_kernel(seq_bits, mine_ref, out_ref, slots, send, recv):
+    seq, tp = lax.axis_index("seq"), lax.axis_index("tp")
+    partners = [(seq ^ (1 << bit), tp) for bit in range(seq_bits)]
+    partners.insert(1, (seq, tp ^ 1))
+    barrier = pltpu.get_barrier_semaphore()
+    for partner in partners:
+        pl.semaphore_signal(barrier, inc=1, device_id=partner, device_id_type=MESH)
+    pl.semaphore_wait(barrier, len(partners))
+    out_ref[...] = mine_ref[...]
+    for step, partner in enumerate(partners):
+        slots[step] = out_ref[...]
+        copy = pltpu.make_async_remote_copy(
+            src_ref=slots.at[step],
+            dst_ref=slots.at[len(partners) + step],
+            send_sem=send.at[step],
+            recv_sem=recv.at[step],
+            device_id=partner,
+            device_id_type=MESH,
+        )
+        copy.start()
+        copy.wait()
+        out_ref[...] += slots[len(partners) + step]
+
+
+def sum_all(values, seq_count):
+    seq_bits = seq_count.bit_length() - 1
+    steps = seq_bits + 1
+    return pl.pallas_call(
+        functools.partial(sum_all_kernel, seq_bits),
+        out_shape=jax.ShapeDtypeStruct(values.shape, values.dtype),
+        in_specs=vmem(1),
+        out_specs=vmem(1)[0],
+        scratch_shapes=[
+            pltpu.VMEM((2 * steps,) + values.shape, values.dtype),
+            pltpu.SemaphoreType.DMA((steps,)),
+            pltpu.SemaphoreType.DMA((steps,)),
+        ],
+        compiler_params=pltpu.CompilerParams(collective_id=7, has_side_effects=True),
+        name="sum_all",
+    )(values)
+
+
+def norm_parts(values):
+    mean = jnp.mean(values, axis=-1, keepdims=True)
+    centred = values - mean
+    rstd = lax.rsqrt(jnp.mean(centred * centred, axis=-1, keepdims=True) + EPS)
+    return centred * rstd, rstd
+
+
+def norm_back(values, gain, upstream):
+    xhat, rstd = norm_parts(values)
+    e = upstream * gain
+    grad = rstd * (
+        e
+        - jnp.mean(e, axis=-1, keepdims=True)
+        - xhat * jnp.mean(e * xhat, axis=-1, keepdims=True)
+    )
+    return grad, jnp.sum(upstream * xhat, axis=0), jnp.sum(upstream, axis=0)
+
+
+def fast_local(
+    tokens_in, w_qkv, bias_qv, w_out, bias_out, w_up, bias_up, w_down, bias_down,
+    norm_gains, norm_shifts, out_grad, lengths, prefixes, placement,
+):
+    seq_count = lax.axis_size("seq")
+    seq, tp = lax.axis_index("seq"), lax.axis_index("tp")
+    core = seq % 2
+    who = jnp.stack([tp, core]).astype(jnp.int32)
+    over_tp = [(0, 1), (1, 0)]
+    over_core = [(i, i ^ 1) for i in range(seq_count)]
+    chips = [[c + 2 * i for i in range(seq_count // 2)] for c in range(2)]
+
+    def to_tp(values):
+        return lax.ppermute(values, "tp", over_tp)
+
+    def to_sib(values):
+        return lax.ppermute(values, "seq", over_core)
+
+    def exchange(chunks):
+        return lax.all_to_all(chunks, ("seq", "tp"), 0, 0, tiled=True)
+
+    def quarters(values, axis):
+        size = values.shape[axis] // 2
+        own = lax.dynamic_slice_in_dim(values, core * size, size, axis)
+        sib = lax.dynamic_slice_in_dim(values, (1 - core) * size, size, axis)
+        far = to_tp(own)
+        return [own, sib, far, to_sib(far)]
+
+    width = w_qkv.shape[0]
+    wq4 = [w.reshape(width, -1) for w in quarters(w_qkv, 2)]
+    small = jnp.concatenate([bias_qv.reshape(2, 2, -1), bias_up.reshape(2, 2, -1).transpose(1, 0, 2)], axis=2)
+    small = small.transpose(1, 0, 2)
+    small4 = [s.reshape(2, -1) for s in quarters(small, 0)]
+    split = bias_qv.shape[1] // 2
+    bias_qv4 = jnp.stack([s[:, :split].reshape(-1) for s in small4])
+    bias_up4 = [s[:, split:].reshape(-1).astype(F32) for s in small4]
+    wo4 = quarters(w_out, 0)
+    wu4 = quarters(w_up, 1)
+    wd4 = quarters(w_down, 0)
+
+    tables = block_tables(lengths, prefixes, placement, core)
+    normed, q_chunks, kv_chunks = project(
+        who, tokens_in, norm_gains[:1], norm_shifts[:1], bias_qv4, wq4
+    )
+    kv_own = exchange(kv_chunks)
+    kv_sib = to_sib(kv_own)
+    q_own = exchange(q_chunks)
+    att_chunks, out_t, mass = attend(core, tables, q_own, kv_own, kv_sib)
+    attended = unpack_heads(who, exchange(att_chunks))
+
+    input_f32 = tokens_in.astype(F32)
+
+    def cols(values, quarter, count):
+        return values[:, quarter * count : (quarter + 1) * count]
+
+    def dot(a, b):
+        return jnp.dot(a, b, preferred_element_type=F32)
+
+    def dot_t(a, b):
+        return lax.dot_general(a, b, (((1,), (1,)), ((), ())), preferred_element_type=F32)
+
+    def dot_rows(a, b):
+        return lax.dot_general(a, b, (((0,), (0,)), ((), ())), preferred_element_type=F32)
+
+    heads4 = [cols(attended, r, 256) for r in range(4)]
+    branch = sum(dot(heads4[r], wo4[r]) for r in range(4)) + bias_out.astype(F32)
+    hidden = input_f32 + layer_norm(branch, norm_gains[1], norm_shifts[1])
+    inner = layer_norm(hidden, norm_gains[2], norm_shifts[2]).astype(BF16)
+    active4, gate4 = [], []
+    for r in range(4):
+        act, back_gate = jax.vjp(smooth_gate, dot(inner, wu4[r]) + bias_up4[r])
+        active4.append(act.astype(BF16))
+        gate4.append(back_gate)
+    down = sum(dot(active4[r], wd4[r]) for r in range(4)) + bias_down.astype(F32)
+    result = (hidden + layer_norm(down, norm_gains[3], norm_shifts[3])).astype(BF16)
+    d_down, gain_last, shift_last = norm_back(down, norm_gains[3], out_grad)
+    bias_down_part = jnp.sum(d_down, axis=0)
+    d_down_b = d_down.astype(BF16)
+    d_up4 = [gate4[r](dot_t(d_down_b, wd4[r]))[0].astype(BF16) for r in range(4)]
+    bias_up_part = [jnp.sum(d.astype(F32), axis=0) for d in d_up4]
+    d_inner = sum(dot_t(d_up4[r], wu4[r]) for r in range(4))
+    d_third, gain_third, shift_third = norm_back(hidden, norm_gains[2], d_inner)
+    d_hidden = out_grad + d_third
+    d_branch, gain_second, shift_second = norm_back(branch, norm_gains[1], d_hidden)
+    bias_out_part = jnp.sum(d_branch, axis=0)
+    d_branch_b = d_branch.astype(BF16)
+    da_own = exchange(spread(who, d_branch_b, wo4))
+    dq_chunks, dkv_mine, dkv_theirs = attend_back(
+        core, tables, q_own, kv_own, kv_sib, da_own, out_t, mass
+    )
+    dkv_chunks = (dkv_mine + to_sib(dkv_theirs).astype(F32)).astype(BF16)
+    d_q, d_k, d_v = unpack_qkv(who, exchange(dq_chunks), exchange(dkv_chunks))
+
+    inner_sib, down_sib, branch_sib, normed_sib = (
+        to_sib(inner), to_sib(d_down_b), to_sib(d_branch_b), to_sib(normed)
+    )
+
+    def paired(left4, right):
+        own = [left4[r] for r in (0, 2)]
+        sib = [to_sib(left4[r]) for r in (1, 3)]
+        near, far = (right(o, s) for o, s in zip(own, sib))
+        return near, far.astype(BF16)
+
+    def reduced(pair):
+        near, far = pair
+        return (near + to_tp(far).astype(F32)).astype(BF16)
+
+    g_down = reduced(paired(active4, lambda o, s: dot_rows(o, d_down_b) + dot_rows(s, down_sib)))
+    g_up = reduced(paired(d_up4, lambda o, s: dot_rows(inner, o) + dot_rows(inner_sib, s)))
+    g_out = reduced(paired(heads4, lambda o, s: dot_rows(o, d_branch_b) + dot_rows(s, branch_sib)))
+    g_down, g_up, g_out = lax.psum((g_down, g_up, g_out), "seq", axis_index_groups=chips)
+
+    mixed4 = [
+        jnp.concatenate([cols(d, r, 256) for d in (d_q, d_k, d_v)], axis=1) for r in range(4)
+    ]
+    d_normed = sum(dot_t(mixed4[r], wq4[r]) for r in range(4))
+    d_first, gain_first, shift_first = norm_back(input_f32, norm_gains[0], d_normed)
+    grad_x = d_hidden + d_first
+    g_qkv = reduced(paired(mixed4, lambda o, s: dot_rows(normed, o) + dot_rows(normed_sib, s)))
+    g_qkv = lax.psum(g_qkv, "seq", axis_index_groups=chips).reshape(width, 3, -1)
+
+    def joined(own, axis):
+        sib = to_sib(own)
+        first = jnp.concatenate([own, sib], axis=axis).astype(F32)
+        second = jnp.concatenate([sib, own], axis=axis).astype(F32)
+        return jnp.where(core == 0, first, second)
+
+    def absolute(parts):
+        base = tp * 2 + core
+        return jnp.concatenate(
+            [sum(jnp.where((base ^ r) == a, parts[r], 0.0) for r in range(4)) for a in range(4)]
+        )
+
+    bias_q_part = [jnp.sum(cols(d_q, r, 256).astype(F32), axis=0) for r in range(4)]
+    bias_v_part = [jnp.sum(cols(d_v, r, 256).astype(F32), axis=0) for r in range(4)]
+    vectors = jnp.stack(
+        [gain_first, gain_second, gain_third, gain_last]
+        + [shift_first, shift_second, shift_third, shift_last]
+        + [bias_out_part, bias_down_part, absolute(bias_q_part), absolute(bias_v_part)]
+    )
+    vectors = jnp.concatenate([vectors, absolute(bias_up_part).reshape(4, -1)])
+    vectors = sum_all(vectors, seq_count)
+    own_cols = bias_qv.shape[1]
+    grad_bias_qv = lax.dynamic_slice_in_dim(vectors[10:12], tp * own_cols, own_cols, 1)
+    grad_bias_up = lax.dynamic_slice_in_dim(
+        vectors[12:16].reshape(-1), tp * bias_up.shape[0], bias_up.shape[0]
+    )
+    return (
+        result,
+        grad_x,
+        joined(g_qkv, 2),
+        grad_bias_qv,
+        joined(g_out, 0),
+        vectors[8],
+        joined(g_up, 1),
+        grad_bias_up,
+        joined(g_down, 0),
+        vectors[9],
+        vectors[0:4],
+        vectors[4:8],
+    )
+
+
 def pack_tables(lengths, prefixes, row_total):
     where_row = jnp.arange(row_total, dtype=jnp.int32)
-    doc_ends = jnp.cumsum(lengths)
+    doc_ends = running_ends(lengths)
     document = jnp.sum((where_row[:, None] >= doc_ends[None, :]).astype(jnp.int32), axis=1)
     limits = doc_ends - lengths + prefixes
     doc_pick = document[:, None] == jnp.arange(lengths.shape[0], dtype=jnp.int32)[None, :]
@@ -48,9 +647,13 @@
     )
 
 
+def pick_blocks(blocks, order):
+    return lax.map(lambda i: lax.dynamic_index_in_dim(blocks, i, 0, False), order)
+
+
 def to_pack(stored, pack_order, margin, block_size):
     blocks = stored.reshape((pack_order.shape[0], block_size) + stored.shape[1:])
-    ordered = jnp.take(blocks, pack_order, axis=0).reshape(stored.shape)
+    ordered = pick_blocks(blocks, pack_order).reshape(stored.shape)
     widths = [(margin, margin)] + [(0, 0)] * (stored.ndim - 1)
     return jnp.pad(ordered, widths)
 
@@ -58,7 +661,7 @@
 def from_pack(padded, placement, margin, block_size, row_total):
     core = padded[margin : margin + row_total]
     blocks = core.reshape((placement.shape[0], block_size) + core.shape[1:])
-    return jnp.take(blocks, placement, axis=0).reshape(core.shape)
+    return pick_blocks(blocks, placement).reshape(core.shape)
 
 
 def masked_scores(query_h, key_h, allowed):
@@ -120,7 +723,7 @@
     return lax.map(attention_one_head, jnp.arange(query_block.shape[1], dtype=jnp.int32))
 
 
-def local(
+def general_local(
     tokens_in,
     w_qkv,
     bias_qv,
@@ -152,11 +755,7 @@
     own_blocks = lax.dynamic_slice_in_dim(
         placement, lax.axis_index("seq") * blocks_here, blocks_here
     )
-    pack_order = (
-        jnp.zeros((block_total,), jnp.int32)
-        .at[placement]
-        .set(jnp.arange(block_total, dtype=jnp.int32))
-    )
+    pack_order = inverse_order(placement)
     offsets = jnp.arange(BLK, dtype=jnp.int32)
 
     def query_window(index):
@@ -366,6 +965,16 @@
         P(),
         P(),
     )
+    seq_count, tp_count = mesh.shape["seq"], mesh.shape["tp"]
+
+    def local(*args):
+        tokens_in, w_qkv, placement = args[0], args[1], args[-1]
+        heads = w_qkv.shape[2] * tp_count // HEAD
+        paired = seq_count * tp_count == 2 * heads == placement.shape[0]
+        sizes = (tokens_in.shape[0], w_qkv.shape[0], heads, seq_count, tp_count)
+        fast = paired and sizes == (BLK, 1024, 16, 16, 2)
+        return (fast_local if fast else general_local)(*args)
+
     return jax.shard_map(
         local,
         mesh=mesh,

time: 2170 us -> 949 us (0.44)
  waiting for transfers between devices: 946 us -> 482 us
  matrix products: 476 us -> 108 us
  local copies, waits for them, and re-layouts: 404 us -> 44.3 us
  Pallas kernels: 0 us -> 172 us
  other arithmetic: 169 us -> 48.9 us
  loops' own time: 63.9 us -> 0 us
  blocking collectives: 74.2 us -> 31 us
  starting transfers between devices: 1.29 us -> 37.8 us
    reduce_scatter x6 -> x0, waiting for transfers between devices: 453 us -> none  [the longest x1 182 us: local(): lax.psum_scatter(key_terms.astype(jnp.bfloat16), 'seq', scatter_dimension...]
    dot_general x124 -> x40, matrix products: 476 us -> 108 us  [the longest x12 38.6 us: dot_t(): lax.dot_general(a, b, (((1,), (1,)), ((), ())), preferred_element_type=F32)]
    all_gather x6 -> x0, waiting for transfers between devices: 339 us -> none  [the longest x1 117 us: local(): lax.all_gather(value_b, 'seq', axis=0, tiled=True)]
    ppermute x0 -> x32, waiting for transfers between devices: none -> 172 us  [the longest x9 170 us: to_tp(): return lax.ppermute(values, 'tp', over_tp)]
    pallas_call x0 -> x7, Pallas kernels: none -> 172 us  [the longest x1 69.7 us: attend_back(): pl.pallas_call(attend_back_kernel, out_shape=(jax.ShapeDtypeStruct((block...]
    reshape x8 -> x7, local copies, waits for them, and re-layouts: 133 us -> 11.2 us  [the longest x4 8.36 us: fast_local(): wq4 = [w.reshape(width, -1) for w in quarters(w_qkv, 2)]]
    all_to_all x0 -> x5, waiting for transfers between devices: none -> 109 us  [exchange(): return lax.all_to_all(chunks, ('seq', 'tp'), 0, 0, tiled=True)]
    psum x2 -> x0, blocking collectives: 74.2 us -> none  [the longest x1 39.9 us: local(): lax.psum((gain_stack, shift_stack, grad_bias_out, grad_bias_down), ('seq'...]
  transfers between devices with their start and end apart: 13 -> 38, of which waited for: 12 -> 11; matrix products, arithmetic and copies ran while one was open for 4% -> 14% of each run, Pallas kernels for 0% -> 9%
where the time goes in v1:
time: 949 us; the launch traced here: 940 us
  waiting for transfers between devices  482 us (51%)
  Pallas kernels  172 us (18%)
  matrix products  108 us (11%)
  other arithmetic  48.9 us (5%)
  local copies, waits for them, and re-layouts  44.3 us (5%)
  starting transfers between devices  37.8 us (4%)
  blocking collectives  31 us (3%)
  between operations  15.8 us (2%)
    psum x1, waiting for transfers between devices, fast_local(): lax.psum(g_qkv, 'seq', axis_index_groups=chips).reshape(width, 3, -1)  201 us
    ppermute x9, waiting for transfers between devices, to_tp(): return lax.ppermute(values, 'tp', over_tp)  170 us
    all_to_all x5, waiting for transfers between devices, exchange(): return lax.all_to_all(chunks, ('seq', 'tp'), 0, 0, tiled=True)  109 us
    pallas_call x1, Pallas kernels, attend_back(): pl.pallas_call(attend_back_kernel, out_shape=(jax.ShapeDtypeStruct((block...  69.7 us
    pallas_call x1, Pallas kernels, attend(): pl.pallas_call(attend_kernel, out_shape=(jax.ShapeDtypeStruct((blocks, QU...  63.4 us
    dot_general x12, matrix products, dot_t(): lax.dot_general(a, b, (((1,), (1,)), ((), ())), preferred_element_type=F32)  38.6 us
    dot_general x16, matrix products, dot_rows(): lax.dot_general(a, b, (((0,), (0,)), ((), ())), preferred_element_type=F32)  38.2 us
    dot_general x12, matrix products, dot(): return jnp.dot(a, b, preferred_element_type=F32)  31.1 us
  transfers between devices with their start and end apart: 38, of which 11 were waited for; matrix products, arithmetic and copies ran while one was open for 14% of the time, Pallas kernels for 9%

profile of v1, /device:TPU:0, one launch (start us, length us, event | category | flops | bytes accessed | tf_op | source)
XLA Modules:
  0.0 939.7 jit_solution(12565005976941870219)
XLA Ops:
  14.4 34.5 %collective-permute-done.2 = bf16[1024,3,256]{0,2,1:T(8,128)(2,1)} collective-permute-done((bf16[1024,3,256]{0,2,1:T(8,128)(2,1)S(1)}, bf16[1024,3,256]{0,2,1:T(8,128)(2,1)}, u32[]{:S(2)}, u32[]{:S(2)}) %collective-permute-start.2) | collective-permute-done | bytes 1572896 | tf_op jit(solution)/shard_map/ppermute | solution.py:474
  63.9 8.7 project.1
  72.6 4.9 all-to-all-start.1
  77.5 48.7 %all-to-all-done.1.own_ref = bf16[32,256,128]{2,1,0:T(8,128)(2,1)S(1)} async-done(((bf16[32,256,128]{2,1,0:T(8,128)(2,1)}), bf16[32,256,128]{2,1,0:T(8,128)(2,1)S(1)}, u32[]{:S(2)}, u32[]{:S(2)}) %all-to-all-start.1) | async-done | bytes 2097184 | tf_op jit(solution)/shard_map/all_to_all | solution.py:480
  139.9 16.2 %all-to-all-done.q_ref = bf16[32,128,128]{2,1,0:T(8,128)(2,1)S(1)} async-done(((bf16[32,128,128]{2,1,0:T(8,128)(2,1)}), bf16[32,128,128]{2,1,0:T(8,128)(2,1)S(1)}, u32[]{:S(2)}, u32[]{:S(2)}) %all-to-all-start) | async-done | bytes 1048608 | tf_op jit(solution)/shard_map/all_to_all | solution.py:480
  157.1 63.4 %attend.1 = (bf16[32,128,128]{2,1,0:T(8,128)(2,1)}, f32[32,64,256]{2,1,0:T(8,128)}, f32[32,1,256]{2,1,0:T(1,128)}) custom-call(s32[1]{0:T(128)} %bitcast.1.part_ref, s32[5,32]{1,0:T(8,128)} %stack.68.tab, s32[32,1,256]{2,1,0:T(1,128)} %broadcast_in_dim.140.low_ref, s32[32,1,256]{2,1,0:T(1,128)} %maximum_minimum_fusion.high_ref, ...), custom_call_target="tpu_custom_call" | custom-call | tf_op jit(solution)/shard_map/attend/pallas_call | solution.py:217
  220.5 3.8 all-to-all-start.2
  227.8 28.6 %collective-permute-done.5.w2 = bf16[256,1024]{1,0:T(8,128)(2,1)} collective-permute-done((bf16[256,1024]{1,0:T(8,128)(2,1)S(1)}, bf16[256,1024]{1,0:T(8,128)(2,1)}, u32[]{:S(2)}, u32[]{:S(2)}) %collective-permute-start.5) | collective-permute-done | bytes 524320 | tf_op jit(solution)/shard_map/ppermute | solution.py:474
  282.0 4.1 multiply_convert_fusion
  300.7 4.4 convert_reduce_fusion.4
  314.5 4.5 convert_reduce_fusion.2
  319.0 4.5 convert_reduce_fusion.1
  326.7 3.8 multiply_reduce_fusion.1
  334.4 4.2 spread.1
  338.6 31.0 %all_to_all.30.da_ref = bf16[32,128,128]{2,1,0:T(8,128)(2,1)} all-to-all(bf16[32,128,128]{2,1,0:T(8,128)(2,1)} %spread.1), channel_id=1, replica_groups=mesh['seq'=16,'tp'=2] {'seq','tp'}, dimensions={0} | all-to-all | bytes 2097152 | tf_op jit(solution)/shard_map/all_to_all | solution.py:480
  369.6 69.7 %attend_back.1 = (bf16[32,128,128]{2,1,0:T(8,128)(2,1)}, f32[32,256,128]{2,1,0:T(8,128)}, bf16[32,256,128]{2,1,0:T(8,128)(2,1)}) custom-call(s32[1]{0:T(128)} %bitcast.1.part_ref, s32[5,32]{1,0:T(8,128)} %stack.68.tab, s32[32,1,256]{2,1,0:T(1,128)} %broadcast_in_dim.140.low_ref, s32[32,1,256]{2,1,0:T(1,128)} %maximum_minimum_fusion.high_ref, ...), custom_call_target="tpu_custom_call" | custom-call | tf_op jit(solution)/shard_map/attend_back/pallas_call | solution.py:238
  439.2 3.9 all-to-all-start.4
  443.7 4.8 add_convert_fusion.4
  448.6 20.7 %all-to-all-done.4.dq_ref = bf16[32,128,128]{2,1,0:T(8,128)(2,1)} async-done(((bf16[32,128,128]{2,1,0:T(8,128)(2,1)}), bf16[32,128,128]{2,1,0:T(8,128)(2,1)}, u32[]{:S(2)}, u32[]{:S(2)}) %all-to-all-start.4) | async-done | bytes 1048608 | tf_op jit(solution)/shard_map/all_to_all | solution.py:480
  469.3 3.7 all-to-all-start.5
  498.6 23.2 %all-to-all-done.5.dkv_ref = bf16[32,256,128]{2,1,0:T(8,128)(2,1)} async-done(((bf16[32,256,128]{2,1,0:T(8,128)(2,1)}), bf16[32,256,128]{2,1,0:T(8,128)(2,1)}, u32[]{:S(2)}, u32[]{:S(2)}) %all-to-all-start.5) | async-done | bytes 2097184 | tf_op jit(solution)/shard_map/all_to_all | solution.py:480
  521.8 4.8 unpack_qkv.1
  547.0 89.6 %collective-permute-done.20 = bf16[256,1024]{1,0:T(8,128)(2,1)S(1)} collective-permute-done((bf16[256,1024]{1,0:T(8,128)(2,1)S(1)}, bf16[256,1024]{1,0:T(8,128)(2,1)S(1)}, u32[]{:S(2)}, u32[]{:S(2)}) %collective-permute-start.20) | collective-permute-done | bytes 524320 | tf_op jit(solution)/shard_map/ppermute | solution.py:474
  640.0 4.3 add_convert_fusion.2
  644.4 4.2 add_convert_fusion
  651.1 17.8 %collective-permute-done.15 = bf16[1024,768]{0,1:T(8,128)(2,1)S(1)} collective-permute-done((bf16[1024,768]{0,1:T(8,128)(2,1)S(1)}, bf16[1024,768]{0,1:T(8,128)(2,1)S(1)}, u32[]{:S(2)}, u32[]{:S(2)}) %collective-permute-start.15) | collective-permute-done | bytes 1572896 | tf_op jit(solution)/shard_map/ppermute | solution.py:474
  682.4 4.4 fusion.9
  686.8 201.4 %all-reduce.3.cloned.1.call-done = (bf16[1024,3,256]{2,0,1:T(8,128)(2,1)}, bf16[256,1024]{1,0:T(8,128)(2,1)}, bf16[1024,1024]{1,0:T(8,128)(2,1)}, bf16[1024,1024]{1,0:T(8,128)(2,1)}) async-done(((bf16[1024,3,256]{2,0,1:T(8,128)(2,1)}, bf16[256,1024]{1,0:T(8,128)(2,1)}, bf16[1024,1024]{1,0:T(8,128)(2,1)}, bf16[1024,1024]{1,0:T(8,128)(2,1)}), (bf16[1024,3,256]{2,0,1:T(8,128)(2,1)}, ...) | async-done | bytes 6291472 | tf_op jit(solution)/shard_map/psum | solution.py:580
  889.5 18.1 %sum_all.1 = f32[16,1024]{1,0:T(8,128)} custom-call(f32[16,1024]{1,0:T(8,128)} %concatenate.61.mine_ref), custom_call_target="tpu_custom_call" | custom-call | tf_op jit(solution)/shard_map/sum_all/pallas_call | solution.py:428
  913.1 3.7 fusion.8
  921.8 6.2 convert_select_fusion.1
  928.0 4.5 convert_select_fusion
  (357 shorter events, 173.7 us)
Async XLA Ops:
  11.3 37.5 %collective-permute-start.2 = (bf16[1024,3,256]{0,2,1:T(8,128)(2,1)S(1)}, bf16[1024,3,256]{0,2,1:T(8,128)(2,1)}, u32[]{:S(2)}, u32[]{:S(2)}) collective-permute-start(bf16[1024,3,256]{0,2,1:T(8,128)(2,1)S(1)} %copy.59), channel_id=1, source_target_pairs={{0,1},{1,0},{2,3},{3,2},{4,5},{5,4},{6,7},{7,6},{8,9},{9,8},{10,11... | collective-permute-start | bytes 4718600 | tf_op jit(solution)/shard_map/ppermute | solution.py:474
  48.9 12.4 %collective-permute-start.3 = (bf16[1024,3,256]{0,2,1:T(8,128)(2,1)}, bf16[1024,3,256]{0,2,1:T(8,128)(2,1)}, u32[]{:S(2)}, u32[]{:S(2)}) collective-permute-start(bf16[1024,3,256]{0,2,1:T(8,128)(2,1)} %collective-permute-done.2), channel_id=1, source_target_pairs={{0,2},{2,0},{4,6},{6,4},{8,10},{10,8},{12,14},{14,12},{16,18},{18,... | collective-permute-start | bytes 4718600 | tf_op jit(solution)/shard_map/ppermute | solution.py:477
  72.6 53.6 %all-to-all-start.1 = ((bf16[32,256,128]{2,1,0:T(8,128)(2,1)}), bf16[32,256,128]{2,1,0:T(8,128)(2,1)S(1)}, u32[]{:S(2)}, u32[]{:S(2)}) async-start(bf16[32,256,128]{2,1,0:T(8,128)(2,1)} %get-tuple-element.25), calls=%async_computation.1 | async-start | bytes 4194304 | tf_op jit(solution)/shard_map/all_to_all | solution.py:480
  126.2 29.9 %all-to-all-start = ((bf16[32,128,128]{2,1,0:T(8,128)(2,1)}), bf16[32,128,128]{2,1,0:T(8,128)(2,1)S(1)}, u32[]{:S(2)}, u32[]{:S(2)}) async-start(bf16[32,128,128]{2,1,0:T(8,128)(2,1)} %get-tuple-element.24), calls=%async_computation | async-start | bytes 2097152 | tf_op jit(solution)/shard_map/all_to_all | solution.py:480
  129.9 26.2 %collective-permute-start.4 = (bf16[32,256,128]{2,1,0:T(8,128)(2,1)S(1)}, bf16[32,256,128]{2,1,0:T(8,128)(2,1)}, u32[]{:S(2)}, u32[]{:S(2)}) collective-permute-start(bf16[32,256,128]{2,1,0:T(8,128)(2,1)S(1)} %all-to-all-done.1.own_ref), channel_id=1, source_target_pairs={{0,2},{2,0},{4,6},{6,4},{8,10},{10,8},{12,14},{14,12},{16,18},{18,... | collective-permute-start | bytes 6291464 | tf_op jit(solution)/shard_map/ppermute | solution.py:477
  133.5 123.0 %collective-permute-start.7 = (bf16[1024,1024]{1,0:T(8,128)(2,1)}, bf16[1024,1024]{1,0:T(8,128)(2,1)}, u32[]{:S(2)}, u32[]{:S(2)}) collective-permute-start(bf16[1024,1024]{1,0:T(8,128)(2,1)} %constant_dynamic-slice_fusion.2), channel_id=1, source_target_pairs={{0,1},{1,0},{2,3},{3,2},{4,5},{5,4},{6,7},{7,6},{8,9},{9,8},{10,11... | collective-permute-start | bytes 6291464 | tf_op jit(solution)/shard_map/ppermute | solution.py:474
  136.7 120.3 %collective-permute-start.8 = (bf16[1024,1024]{1,0:T(8,128)(2,1)}, bf16[1024,1024]{1,0:T(8,128)(2,1)}, u32[]{:S(2)}, u32[]{:S(2)}) collective-permute-start(bf16[1024,1024]{1,0:T(8,128)(2,1)} %constant_dynamic-slice_fusion.1), channel_id=1, source_target_pairs={{0,1},{1,0},{2,3},{3,2},{4,5},{5,4},{6,7},{7,6},{8,9},{9,8},{10,11... | collective-permute-start | bytes 6291464 | tf_op jit(solution)/shard_map/ppermute | solution.py:474
  220.5 36.5 %all-to-all-start.2 = ((bf16[32,128,128]{2,1,0:T(8,128)(2,1)}), bf16[32,128,128]{2,1,0:T(8,128)(2,1)S(1)}, u32[]{:S(2)}, u32[]{:S(2)}) async-start(bf16[32,128,128]{2,1,0:T(8,128)(2,1)} %get-tuple-element.26), calls=%async_computation.2 | async-start | bytes 2097152 | tf_op jit(solution)/shard_map/all_to_all | solution.py:480
  225.6 30.8 %collective-permute-start.5 = (bf16[256,1024]{1,0:T(8,128)(2,1)S(1)}, bf16[256,1024]{1,0:T(8,128)(2,1)}, u32[]{:S(2)}, u32[]{:S(2)}) collective-permute-start(bf16[256,1024]{1,0:T(8,128)(2,1)S(1)} %get-tuple-element.105.w0), channel_id=1, source_target_pairs={{0,1},{1,0},{2,3},{3,2},{4,5},{5,4},{6,7},{7,6},{8,9},{9,8},{10,11... | collective-permute-start | bytes 1572872 | tf_op jit(solution)/shard_map/ppermute | solution.py:474
  256.4 25.5 %collective-permute-start.9 = (bf16[1024,1024]{1,0:T(8,128)(2,1)}, bf16[1024,1024]{1,0:T(8,128)(2,1)}, u32[]{:S(2)}, u32[]{:S(2)}) collective-permute-start(bf16[1024,1024]{1,0:T(8,128)(2,1)} %collective-permute-done.7), channel_id=1, source_target_pairs={{0,2},{2,0},{4,6},{6,4},{8,10},{10,8},{12,14},{14,12},{16,18},{18,... | collective-permute-start | bytes 6291464 | tf_op jit(solution)/shard_map/ppermute | solution.py:477
  257.0 35.9 %collective-permute-start.10 = (bf16[1024,1024]{1,0:T(8,128)(2,1)}, bf16[1024,1024]{1,0:T(8,128)(2,1)}, u32[]{:S(2)}, u32[]{:S(2)}) collective-permute-start(bf16[1024,1024]{1,0:T(8,128)(2,1)} %collective-permute-done.8), channel_id=1, source_target_pairs={{0,2},{2,0},{4,6},{6,4},{8,10},{10,8},{12,14},{14,12},{16,18},{18,... | collective-permute-start | bytes 6291464 | tf_op jit(solution)/shard_map/ppermute | solution.py:477
  439.2 30.1 %all-to-all-start.4 = ((bf16[32,128,128]{2,1,0:T(8,128)(2,1)}), bf16[32,128,128]{2,1,0:T(8,128)(2,1)}, u32[]{:S(2)}, u32[]{:S(2)}) async-start(bf16[32,128,128]{2,1,0:T(8,128)(2,1)} %get-tuple-element.29), calls=%async_computation.4 | async-start | bytes 2097152 | tf_op jit(solution)/shard_map/all_to_all | solution.py:480
  469.3 52.5 %all-to-all-start.5 = ((bf16[32,256,128]{2,1,0:T(8,128)(2,1)}), bf16[32,256,128]{2,1,0:T(8,128)(2,1)}, u32[]{:S(2)}, u32[]{:S(2)}) async-start(bf16[32,256,128]{2,1,0:T(8,128)(2,1)} %add_convert_fusion.4), calls=%async_computation.5 | async-start | bytes 4194304 | tf_op jit(solution)/shard_map/all_to_all | solution.py:480
  473.1 415.0 %all-reduce.3.cloned.1.call-start = ((), (), s32[]{:S(2)}) async-start(), calls=%async_computation.6 | async-start | bytes 12582912 | tf_op jit(solution)/shard_map/psum | solution.py:580
  473.3 68.1 %collective-permute-start.12 = (bf16[512,1024]{1,0:T(8,128)(2,1)}, bf16[512,1024]{1,0:T(8,128)(2,1)}, u32[]{:S(2)}, u32[]{:S(2)}) collective-permute-start(bf16[512,1024]{1,0:T(8,128)(2,1)} %get-tuple-element.35), channel_id=1, source_target_pairs={{0,2},{2,0},{4,6},{6,4},{8,10},{10,8},{12,14},{14,12},{16,18},{18,... | collective-permute-start | bytes 3145736 | tf_op jit(solution)/shard_map/ppermute | solution.py:477
  473.6 17.8 %collective-permute-start.22 = (bf16[512,1024]{1,0:T(8,128)(2,1)}, bf16[512,1024]{1,0:T(8,128)(2,1)S(1)}, u32[]{:S(2)}, u32[]{:S(2)}) collective-permute-start(bf16[512,1024]{1,0:T(8,128)(2,1)} %copy-done.4), channel_id=1, source_target_pairs={{0,2},{2,0},{4,6},{6,4},{8,10},{10,8},{12,14},{14,12},{16,18},{18,... | collective-permute-start | bytes 3145736 | tf_op jit(solution)/shard_map/ppermute | solution.py:477
  473.9 17.8 %collective-permute-start.24 = (bf16[512,1024]{1,0:T(8,128)(2,1)}, bf16[512,1024]{1,0:T(8,128)(2,1)S(1)}, u32[]{:S(2)}, u32[]{:S(2)}) collective-permute-start(bf16[512,1024]{1,0:T(8,128)(2,1)} %copy-done.34), channel_id=1, source_target_pairs={{0,2},{2,0},{4,6},{6,4},{8,10},{10,8},{12,14},{14,12},{16,18},{18,... | collective-permute-start | bytes 3145736 | tf_op jit(solution)/shard_map/ppermute | solution.py:477
  474.1 20.5 %collective-permute-start.29 = (bf16[512,1024]{1,0:T(8,128)(2,1)}, bf16[512,1024]{1,0:T(8,128)(2,1)S(1)}, u32[]{:S(2)}, u32[]{:S(2)}) collective-permute-start(bf16[512,1024]{1,0:T(8,128)(2,1)} %copy-done.33), channel_id=1, source_target_pairs={{0,2},{2,0},{4,6},{6,4},{8,10},{10,8},{12,14},{14,12},{16,18},{18,... | collective-permute-start | bytes 3145736 | tf_op jit(solution)/shard_map/ppermute | solution.py:477
  474.4 20.5 %collective-permute-start.28 = (bf16[512,1024]{1,0:T(8,128)(2,1)}, bf16[512,1024]{1,0:T(8,128)(2,1)S(1)}, u32[]{:S(2)}, u32[]{:S(2)}) collective-permute-start(bf16[512,1024]{1,0:T(8,128)(2,1)} %copy-done.51), channel_id=1, source_target_pairs={{0,2},{2,0},{4,6},{6,4},{8,10},{10,8},{12,14},{14,12},{16,18},{18,... | collective-permute-start | bytes 3145736 | tf_op jit(solution)/shard_map/ppermute | solution.py:477
  491.4 44.6 %collective-permute-start.18 = (bf16[512,1024]{1,0:T(8,128)(2,1)}, bf16[512,1024]{1,0:T(8,128)(2,1)}, u32[]{:S(2)}, u32[]{:S(2)}) collective-permute-start(bf16[512,1024]{1,0:T(8,128)(2,1)} %get-tuple-element.80.d_ref), channel_id=1, source_target_pairs={{0,2},{2,0},{4,6},{6,4},{8,10},{10,8},{12,14},{14,12},{16,18},{18,... | collective-permute-start | bytes 3145736 | tf_op jit(solution)/shard_map/ppermute | solution.py:477
  491.7 41.7 %collective-permute-start.23 = (bf16[512,1024]{1,0:T(8,128)(2,1)}, bf16[512,1024]{1,0:T(8,128)(2,1)}, u32[]{:S(2)}, u32[]{:S(2)}) collective-permute-start(bf16[512,1024]{1,0:T(8,128)(2,1)} %get-tuple-element.141), channel_id=1, source_target_pairs={{0,2},{2,0},{4,6},{6,4},{8,10},{10,8},{12,14},{14,12},{16,18},{18,... | collective-permute-start | bytes 3145736 | tf_op jit(solution)/shard_map/ppermute | solution.py:477
  494.6 43.7 %collective-permute-start.27 = (bf16[512,1024]{1,0:T(8,128)(2,1)}, bf16[512,1024]{1,0:T(8,128)(2,1)}, u32[]{:S(2)}, u32[]{:S(2)}) collective-permute-start(bf16[512,1024]{1,0:T(8,128)(2,1)} %get-tuple-element.132), channel_id=1, source_target_pairs={{0,2},{2,0},{4,6},{6,4},{8,10},{10,8},{12,14},{14,12},{16,18},{18,... | collective-permute-start | bytes 3145736 | tf_op jit(solution)/shard_map/ppermute | solution.py:477
  494.9 35.5 %collective-permute-start.19 = (bf16[512,256]{1,0:T(8,128)(2,1)}, bf16[512,256]{1,0:T(8,128)(2,1)}, u32[]{:S(2)}, u32[]{:S(2)}) collective-permute-start(bf16[512,256]{1,0:T(8,128)(2,1)} %get-tuple-element.89), channel_id=1, source_target_pairs={{0,2},{2,0},{4,6},{6,4},{8,10},{10,8},{12,14},{14,12},{16,18},{18,... | collective-permute-start | bytes 786440 | tf_op jit(solution)/shard_map/ppermute | solution.py:477
  531.8 108.2 %collective-permute-start.25 = (bf16[1024,1024]{1,0:T(8,128)(2,1)S(1)}, bf16[1024,1024]{1,0:T(8,128)(2,1)}, u32[]{:S(2)}, u32[]{:S(2)}) collective-permute-start(bf16[1024,1024]{1,0:T(8,128)(2,1)S(1)} %copy-done.31), channel_id=1, source_target_pairs={{0,1},{1,0},{2,3},{3,2},{4,5},{5,4},{6,7},{7,6},{8,9},{9,8},{10,11... | collective-permute-start | bytes 6291464 | tf_op jit(solution)/shard_map/ppermute | solution.py:474
  533.4 9.6 %collective-permute-start.14 = (bf16[512,768]{1,0:T(8,128)(2,1)S(1)}, bf16[512,768]{1,0:T(8,128)(2,1)S(1)}, u32[]{:S(2)}, u32[]{:S(2)}) collective-permute-start(bf16[512,768]{1,0:T(8,128)(2,1)S(1)} %pad_maximum_fusion.3), channel_id=1, source_target_pairs={{0,2},{2,0},{4,6},{6,4},{8,10},{10,8},{12,14},{14,12},{16,18},{18,... | collective-permute-start | bytes 2359304 | tf_op jit(solution)/shard_map/ppermute | solution.py:477
  536.0 108.4 %collective-permute-start.30 = (bf16[1024,1024]{1,0:T(8,128)(2,1)}, bf16[1024,1024]{1,0:T(8,128)(2,1)}, u32[]{:S(2)}, u32[]{:S(2)}) collective-permute-start(bf16[1024,1024]{1,0:T(8,128)(2,1)} %add_convert_fusion.1), channel_id=1, source_target_pairs={{0,1},{1,0},{2,3},{3,2},{4,5},{5,4},{6,7},{7,6},{8,9},{9,8},{10,11... | collective-permute-start | bytes 6291464 | tf_op jit(solution)/shard_map/ppermute | solution.py:474
  538.3 8.7 collective-permute-start.17
  541.5 95.1 %collective-permute-start.20 = (bf16[256,1024]{1,0:T(8,128)(2,1)S(1)}, bf16[256,1024]{1,0:T(8,128)(2,1)S(1)}, u32[]{:S(2)}, u32[]{:S(2)}) collective-permute-start(bf16[256,1024]{1,0:T(8,128)(2,1)S(1)} %fusion.51), channel_id=1, source_target_pairs={{0,1},{1,0},{2,3},{3,2},{4,5},{5,4},{6,7},{7,6},{8,9},{9,8},{10,11... | collective-permute-start | bytes 1572872 | tf_op jit(solution)/shard_map/ppermute | solution.py:474
  546.3 122.5 %collective-permute-start.15 = (bf16[1024,768]{0,1:T(8,128)(2,1)S(1)}, bf16[1024,768]{0,1:T(8,128)(2,1)S(1)}, u32[]{:S(2)}, u32[]{:S(2)}) collective-permute-start(bf16[1024,768]{0,1:T(8,128)(2,1)S(1)} %add_convert_fusion.6), channel_id=1, source_target_pairs={{0,1},{1,0},{2,3},{3,2},{4,5},{5,4},{6,7},{7,6},{8,9},{9,8},{10,11... | collective-permute-start | bytes 4718600 | tf_op jit(solution)/shard_map/ppermute | solution.py:474
  888.1 33.6 %collective-permute-start.26 = (bf16[1024,1024]{1,0:T(8,128)(2,1)}, bf16[1024,1024]{1,0:T(8,128)(2,1)}, u32[]{:S(2)}, u32[]{:S(2)}) collective-permute-start(bf16[1024,1024]{1,0:T(8,128)(2,1)} %get-tuple-element.69), channel_id=1, source_target_pairs={{0,2},{2,0},{4,6},{6,4},{8,10},{10,8},{12,14},{14,12},{16,18},{18,... | collective-permute-start | bytes 6291464 | tf_op jit(solution)/shard_map/ppermute | solution.py:477
  907.6 10.9 %collective-permute-start.16 = (bf16[1024,3,256]{2,0,1:T(8,128)(2,1)}, bf16[1024,3,256]{2,0,1:T(8,128)(2,1)S(1)}, u32[]{:S(2)}, u32[]{:S(2)}) collective-permute-start(bf16[1024,3,256]{2,0,1:T(8,128)(2,1)} %get-tuple-element.67), channel_id=1, source_target_pairs={{0,2},{2,0},{4,6},{6,4},{8,10},{10,8},{12,14},{14,12},{16,18},{18,... | collective-permute-start | bytes 4718600 | tf_op jit(solution)/shard_map/ppermute | solution.py:477
  909.1 18.9 %collective-permute-start.31 = (bf16[1024,1024]{1,0:T(8,128)(2,1)}, bf16[1024,1024]{1,0:T(8,128)(2,1)S(1)}, u32[]{:S(2)}, u32[]{:S(2)}) collective-permute-start(bf16[1024,1024]{1,0:T(8,128)(2,1)} %get-tuple-element.70), channel_id=1, source_target_pairs={{0,2},{2,0},{4,6},{6,4},{8,10},{10,8},{12,14},{14,12},{16,18},{18,... | collective-permute-start | bytes 6291464 | tf_op jit(solution)/shard_map/ppermute | solution.py:477
  (85 other events, 1209.7 us)
Sparse Core Ops, SparseCore 0:
  674.2 213.8 all-reduce.2

commit v2 on v1

--- a/solution.py
+++ b/solution.py
@@ -12,6 +12,11 @@
 HALF = BLK // 2
 QUART = BLK // 4
 LONGEST = 4096
+STEP_F = 1024
+STEP_B = 512
+UNROLL = 4
+CHUNKS = 9
+CHUNKS_LAST = 8
 VMEM_LIMIT = 58 << 20
 
 EPS = 1e-05
@@ -57,26 +62,14 @@
     high = jnp.minimum(pick(ends), jnp.maximum(pos + 1, pick(limits)))
     table = jnp.stack(
         [
-            jnp.min(low, axis=1) // BLK,
-            (jnp.max(high, axis=1) - 1) // BLK + 1,
+            jnp.min(low, axis=1) // HALF,
+            (jnp.max(high, axis=1) - 1) // HALF + 1,
             jnp.max(low, axis=1),
             jnp.min(high, axis=1),
-            inverse_order(placement),
+            placement,
         ]
     )
     return low[:, None, :], high[:, None, :], table
-
-
-def fill_keys(part, own_ref, sib_ref, kv, kvt):
-    other = 1 - part
-
-    def one(b, carry):
-        kv[b, pl.ds(pl.multiple_of(part * HALF, HALF), HALF), :] = own_ref[b]
-        kv[b, pl.ds(pl.multiple_of(other * HALF, HALF), HALF), :] = sib_ref[b]
-        kvt[b] = kv[b].astype(F32).T.astype(BF16)
-        return carry
-
-    lax.fori_loop(0, kv.shape[0], one, 0)
 
 
 def unpack_t(packed):
@@ -88,119 +81,135 @@
     return jnp.concatenate([turned[:, :QUART], turned[:, QUART:]], axis=0).T
 
 
-def attend_kernel(part_ref, tab, low_ref, high_ref, q_ref, own_ref, sib_ref, out_ref, ot_ref, lse_ref, kv, kvt):
-    fill_keys(part_ref[0], own_ref, sib_ref, kv, kvt)
+def pieces(tab, b, keys, step, start):
+    count = keys // HALF
+    first = tab[0, b]
+
+    def visit(i, state):
+        at = pl.multiple_of((first + i * count) * HALF, HALF)
+        whole = (at >= tab[2, b]) & (at + keys <= tab[3, b])
+        return lax.cond(whole, lambda st: step(at, st, False), lambda st: step(at, st, True), state)
+
+    return lax.fori_loop(0, (tab[1, b] - first + count - 1) // count, visit, start)
+
+
+def attend_kernel(
+    part_ref, tab, low_ref, high_ref, q_ref, own_ref, sib_ref,
+    out_ref, ot_ref, lse_ref, kv, kvt, rhs_s,
+):
+    part = part_ref[0]
     scale = HEAD**-0.5
-    depth = lax.broadcasted_iota(jnp.int32, (BLK, HALF), 0)
+    blocks = q_ref.shape[0]
+    rows = blocks * BLK
+    depth = lax.broadcasted_iota(jnp.int32, (STEP_F, HALF), 0)
+
+    def prepare(b, carry):
+        for ref, which in ((own_ref, part), (sib_ref, 1 - part)):
+            at = pl.multiple_of(tab[4, b] * BLK + which * HALF, HALF)
+            piece = ref[b]
+            kv[pl.ds(at, HALF), :] = piece
+            kvt[:, pl.ds(at, HALF)] = piece.T
+        qt = unpack_t(q_ref[b]) * scale
+        rhs_s[b] = jnp.concatenate([qt, jnp.zeros_like(qt)], axis=0).astype(BF16)
+        return carry
+
+    lax.fori_loop(0, blocks, prepare, 0, unroll=UNROLL)
+    kv[rows:, :] = jnp.zeros((kv.shape[0] - rows, 2 * HEAD), BF16)
+    kvt[:, rows:] = jnp.zeros((2 * HEAD, kv.shape[0] - rows), BF16)
 
     def one(b, carry):
-        qt = unpack_t(q_ref[b]) * scale
-        rhs = jnp.concatenate([qt, jnp.zeros_like(qt)], axis=0).astype(BF16)
         low, high = low_ref[b], high_ref[b]
 
-        def step(kb, state, masked):
+        def step(at, state, masked):
             top, total, acc = state
-            st = tab[4, kb]
-            sc = jnp.dot(kv[st], rhs, preferred_element_type=F32)
+            sc = jnp.dot(kv[pl.ds(at, STEP_F), :], rhs_s[b], preferred_element_type=F32)
             if masked:
-                pos = depth + kb * BLK
-                sc = jnp.where((pos >= low) & (pos < high), sc, -1e30)
+                sc = jnp.where((depth >= low - at) & (depth < high - at), sc, -1e30)
             new = jnp.maximum(top, jnp.max(sc, axis=0, keepdims=True))
             alpha = jnp.exp(top - new)
             pr = jnp.exp(sc - new)
             total = total * alpha + jnp.sum(pr, axis=0, keepdims=True)
             acc = acc * alpha + jnp.dot(
-                kvt[st, HEAD:, :], pr.astype(BF16), preferred_element_type=F32
+                kvt[HEAD:, pl.ds(at, STEP_F)], pr.astype(BF16), preferred_element_type=F32
             )
             return new, total, acc
-
-        def visit(kb, state):
-            whole = (kb * BLK >= tab[2, b]) & ((kb + 1) * BLK <= tab[3, b])
-            return lax.cond(
-                whole,
-                lambda st: step(kb, st, False),
-                lambda st: step(kb, st, True),
-                state,
-            )
 
         start = (
             jnp.full((1, HALF), -1e30, F32),
             jnp.zeros((1, HALF), F32),
             jnp.zeros((HEAD, HALF), F32),
         )
-        top, total, acc = lax.fori_loop(tab[0, b], tab[1, b], visit, start)
-        ot = acc / total
-        ot_ref[b] = ot
+        top, total, acc = pieces(tab, b, STEP_F, step, start)
+        ot_ref[b] = acc * (1.0 / total)
         lse_ref[b] = top + jnp.log(total)
-        out_ref[b] = pack_t(ot).astype(BF16)
         return carry
 
-    lax.fori_loop(0, q_ref.shape[0], one, 0)
+    lax.fori_loop(0, blocks, one, 0)
+
+    def finish(b, carry):
+        out_ref[b] = pack_t(ot_ref[b]).astype(BF16)
+        return carry
+
+    lax.fori_loop(0, blocks, finish, 0, unroll=UNROLL)
 
 
 def attend_back_kernel(
-    part_ref, tab, low_ref, high_ref, q_ref, own_ref, sib_ref, da_ref, ot_ref, lse_ref,
-    dq_ref, mine_ref, theirs_ref, kv, kvt, dkv,
+    part_ref, tab, low_ref, high_ref, q_ref, da_ref, ot_ref, lse_ref, kv, kvt,
+    dq_ref, mine_ref, theirs_ref, dkv, rhs_s, rows_s, total_s, dqt_s,
 ):
     part = part_ref[0]
-    fill_keys(part, own_ref, sib_ref, kv, kvt)
     scale = HEAD**-0.5
-    depth = lax.broadcasted_iota(jnp.int32, (BLK, HALF), 0)
+    blocks = q_ref.shape[0]
+    depth = lax.broadcasted_iota(jnp.int32, (STEP_B, HALF), 0)
     lane = lax.broadcasted_iota(jnp.int32, (HALF, 2 * HEAD), 1)
 
-    def clear(b, carry):
-        dkv[b] = jnp.zeros((BLK, 2 * HEAD), F32)
-        return carry
-
-    lax.fori_loop(0, dkv.shape[0], clear, 0)
-
-    def one(b, carry):
+    def prepare(b, carry):
+        dkv[pl.ds(pl.multiple_of(b * BLK, BLK), BLK), :] = jnp.zeros((BLK, 2 * HEAD), F32)
         qt = unpack_t(q_ref[b]) * scale
         dat = unpack_t(da_ref[b])
         blank = jnp.zeros_like(qt)
-        rhs_q = jnp.concatenate([qt, blank], axis=0).astype(BF16)
-        rhs_d = jnp.concatenate([blank, dat], axis=0).astype(BF16)
+        rhs_s[b, :, :HALF] = jnp.concatenate([qt, blank], axis=0).astype(BF16)
+        rhs_s[b, :, HALF:] = jnp.concatenate([blank, dat], axis=0).astype(BF16)
         both = jnp.concatenate([qt, dat], axis=0).T
-        rows_q = jnp.where(lane < HEAD, both, 0.0).astype(BF16)
-        rows_d = jnp.where(lane < HEAD, 0.0, both).astype(BF16)
-        total = jnp.sum(dat * ot_ref[b], axis=0, keepdims=True)
+        rows_s[b, :HALF, :] = jnp.where(lane < HEAD, both, 0.0).astype(BF16)
+        rows_s[b, HALF:, :] = jnp.where(lane < HEAD, 0.0, both).astype(BF16)
+        total_s[b] = jnp.sum(dat * ot_ref[b], axis=0, keepdims=True)
+        return carry
+
+    lax.fori_loop(0, blocks, prepare, 0, unroll=UNROLL)
+    dkv[blocks * BLK :, :] = jnp.zeros((dkv.shape[0] - blocks * BLK, 2 * HEAD), F32)
+
+    def one(b, carry):
+        total = total_s[b]
         lse = lse_ref[b]
         low, high = low_ref[b], high_ref[b]
 
-        def step(kb, acc, masked):
-            st = tab[4, kb]
-            keys = kv[st]
-            sc = jnp.dot(keys, rhs_q, preferred_element_type=F32)
-            dp = jnp.dot(keys, rhs_d, preferred_element_type=F32)
+        def step(at, acc, masked):
+            keys = kv[pl.ds(at, STEP_B), :]
+            sc = jnp.dot(keys, rhs_s[b, :, :HALF], preferred_element_type=F32)
+            dp = jnp.dot(keys, rhs_s[b, :, HALF:], preferred_element_type=F32)
             if masked:
-                pos = depth + kb * BLK
-                sc = jnp.where((pos >= low) & (pos < high), sc, -1e30)
+                sc = jnp.where((depth >= low - at) & (depth < high - at), sc, -1e30)
             pr = jnp.exp(sc - lse)
             ds = (pr * (dp - total)).astype(BF16)
-            dkv[st] += jnp.dot(ds, rows_q, preferred_element_type=F32) + jnp.dot(
-                pr.astype(BF16), rows_d, preferred_element_type=F32
-            )
-            return acc + jnp.dot(kvt[st, :HEAD, :], ds, preferred_element_type=F32)
-
-        def visit(kb, acc):
-            whole = (kb * BLK >= tab[2, b]) & ((kb + 1) * BLK <= tab[3, b])
-            return lax.cond(
-                whole, lambda a: step(kb, a, False), lambda a: step(kb, a, True), acc
-            )
-
-        acc = lax.fori_loop(tab[0, b], tab[1, b], visit, jnp.zeros((HEAD, HALF), F32))
-        dq_ref[b] = pack_t(acc * scale).astype(BF16)
+            dkv[pl.ds(at, STEP_B), :] += jnp.dot(
+                ds, rows_s[b, :HALF, :], preferred_element_type=F32
+            ) + jnp.dot(pr.astype(BF16), rows_s[b, HALF:, :], preferred_element_type=F32)
+            return acc + jnp.dot(kvt[:HEAD, pl.ds(at, STEP_B)], ds, preferred_element_type=F32)
+
+        dqt_s[b] = pieces(tab, b, STEP_B, step, jnp.zeros((HEAD, HALF), F32))
         return carry
 
-    lax.fori_loop(0, q_ref.shape[0], one, 0)
-    other = 1 - part
-
-    def split(b, carry):
-        mine_ref[b] = dkv[b, pl.ds(pl.multiple_of(part * HALF, HALF), HALF), :]
-        theirs_ref[b] = dkv[b, pl.ds(pl.multiple_of(other * HALF, HALF), HALF), :].astype(BF16)
+    lax.fori_loop(0, blocks, one, 0)
+
+    def finish(b, carry):
+        dq_ref[b] = pack_t(dqt_s[b] * scale).astype(BF16)
+        base = tab[4, b] * BLK
+        mine_ref[b] = dkv[pl.ds(pl.multiple_of(base + part * HALF, HALF), HALF), :]
+        theirs_ref[b] = dkv[pl.ds(pl.multiple_of(base + (1 - part) * HALF, HALF), HALF), :].astype(BF16)
         return carry
 
-    lax.fori_loop(0, dkv.shape[0], split, 0)
+    lax.fori_loop(0, blocks, finish, 0, unroll=UNROLL)
 
 
 def vmem(count):
@@ -214,25 +223,28 @@
 def attend(part, tables, q_chunks, kv_own, kv_sib):
     low, high, table = tables
     blocks = q_chunks.shape[0]
+    rows = blocks * BLK + STEP_F
     return pl.pallas_call(
         attend_kernel,
         out_shape=(
             jax.ShapeDtypeStruct((blocks, QUART, 2 * HEAD), BF16),
             jax.ShapeDtypeStruct((blocks, HEAD, HALF), F32),
             jax.ShapeDtypeStruct((blocks, 1, HALF), F32),
+            jax.ShapeDtypeStruct((rows, 2 * HEAD), BF16),
+            jax.ShapeDtypeStruct((2 * HEAD, rows), BF16),
         ),
         in_specs=smem(2) + vmem(5),
-        out_specs=tuple(vmem(3)),
-        scratch_shapes=[
-            pltpu.VMEM((blocks, BLK, 2 * HEAD), BF16),
-            pltpu.VMEM((blocks, 2 * HEAD, BLK), BF16),
-        ],
+        out_specs=tuple(vmem(5)),
+        scratch_shapes=[pltpu.VMEM((blocks, 2 * HEAD, HALF), BF16)],
         compiler_params=pltpu.CompilerParams(vmem_limit_bytes=VMEM_LIMIT),
+        cost_estimate=pl.CostEstimate(
+            flops=40 * 10**9, bytes_accessed=20 << 20, transcendentals=blocks * 4 * BLK * HALF
+        ),
         name="attend",
     )(part.reshape(1), table, low, high, q_chunks, kv_own, kv_sib)
 
 
-def attend_back(part, tables, q_chunks, kv_own, kv_sib, da_chunks, out_t, mass):
+def attend_back(part, tables, q_chunks, da_chunks, out_t, mass, kv, kvt):
     low, high, table = tables
     blocks = q_chunks.shape[0]
     return pl.pallas_call(
@@ -245,13 +257,18 @@
         in_specs=smem(2) + vmem(8),
         out_specs=tuple(vmem(3)),
         scratch_shapes=[
+            pltpu.VMEM((blocks * BLK + STEP_F, 2 * HEAD), F32),
+            pltpu.VMEM((blocks, 2 * HEAD, BLK), BF16),
             pltpu.VMEM((blocks, BLK, 2 * HEAD), BF16),
-            pltpu.VMEM((blocks, 2 * HEAD, BLK), BF16),
-            pltpu.VMEM((blocks, BLK, 2 * HEAD), F32),
+            pltpu.VMEM((blocks, 1, HALF), F32),
+            pltpu.VMEM((blocks, HEAD, HALF), F32),
         ],
         compiler_params=pltpu.CompilerParams(vmem_limit_bytes=VMEM_LIMIT),
+        cost_estimate=pl.CostEstimate(
+            flops=60 * 10**9, bytes_accessed=30 << 20, transcendentals=blocks * 4 * BLK * HALF
+        ),
         name="attend_back",
-    )(part.reshape(1), table, low, high, q_chunks, kv_own, kv_sib, da_chunks, out_t, mass)
+    )(part.reshape(1), table, low, high, q_chunks, da_chunks, out_t, mass, kv, kvt)
 
 
 def chunk_of(who, quarter, index, half):
@@ -440,6 +457,246 @@
     )(values)
 
 
+class Place:
+    def __init__(self):
+        self.seq, self.tp = lax.axis_index("seq"), lax.axis_index("tp")
+        self.x = lax.rem(self.seq // 2, 2)
+        self.z = self.seq // 4
+        self.core_partner = (self.seq ^ 1, self.tp)
+        self.x_partner = (self.seq ^ 2, self.tp)
+        self.z_partners = [(self.seq ^ (4 * d), self.tp) for d in (1, 2, 3)]
+        self.tp_partner = (self.seq, self.tp ^ 1)
+
+
+def greet_all(count, me, seq, tp):
+    barrier = pltpu.get_barrier_semaphore()
+
+    def one(k, carry):
+        other = lax.rem(me + k, count)
+        pl.semaphore_signal(
+            barrier, inc=1, device_id=(other // 2, lax.rem(other, 2)), device_id_type=MESH
+        )
+        return carry
+
+    lax.fori_loop(1, count, one, 0)
+    pl.semaphore_wait(barrier, count - 1)
+
+
+def greet(partners):
+    barrier = pltpu.get_barrier_semaphore()
+    for partner in partners:
+        pl.semaphore_signal(barrier, inc=1, device_id=partner, device_id_type=MESH)
+    pl.semaphore_wait(barrier, len(partners))
+
+
+def remote(src, dst, send, recv, device):
+    return pltpu.make_async_remote_copy(
+        src_ref=src, dst_ref=dst, send_sem=send, recv_sem=recv, device_id=device, device_id_type=MESH
+    )
+
+
+def chunk_copy(count, me, k, src, dst, send, recv):
+    other = lax.rem(me + k, count)
+    return remote(src.at[other], dst.at[me], send.at[k], recv.at[k], (other // 2, lax.rem(other, 2)))
+
+
+def reduce_ticks(place, chunks, near, far, out, xbuf, xsum, zbuf, ybuf, ysum, sems):
+    rows = near.shape[0] // chunks
+    half, piece = rows // 2, rows // 8
+    x, z = place.x, place.z
+
+    def at(start, size):
+        return pl.ds(pl.multiple_of(start, size), size)
+
+    def tp_copy(k):
+        return remote(
+            far.at[at(k * rows, rows)], ybuf.at[at(k * rows, rows)],
+            sems["ys"].at[k], sems["yr"].at[k], place.tp_partner,
+        )
+
+    def x_copy(k):
+        src = ysum if far is not None else near
+        return remote(
+            src.at[at(k * rows + (1 - x) * half, half)], xbuf.at[at(k * half, half)],
+            sems["xs"].at[k], sems["xr"].at[k], place.x_partner,
+        )
+
+    def z_copy(k, d):
+        return remote(
+            xsum.at[at(k * half + (z ^ d) * piece, piece)], zbuf.at[d - 1, at(k * piece, piece)],
+            sems["zs"].at[d - 1, k], sems["zr"].at[d - 1, k], place.z_partners[d - 1],
+        )
+
+    def own_piece(k):
+        return at(k * rows + x * half + z * piece, piece)
+
+    def zg_copy(k, d):
+        return remote(
+            out.at[0, own_piece(k)], out.at[0, own_piece(k)],
+            sems["zgs"].at[d - 1, k], sems["zgr"].at[d - 1, k], place.z_partners[d - 1],
+        )
+
+    def xg_copy(k):
+        span = at(k * rows + x * half, half)
+        return remote(
+            out.at[0, span], out.at[0, span], sems["xgs"].at[k], sems["xgr"].at[k], place.x_partner
+        )
+
+    def core_copy(k):
+        span = at(k * rows, rows)
+        return remote(
+            out.at[0, span], out.at[1, span], sems["cs"].at[k], sems["cr"].at[k], place.core_partner
+        )
+
+    def stage_tp(k):
+        tp_copy(k).start()
+
+    def stage_x(k):
+        if far is not None:
+            tp_copy(k).wait_recv()
+            span = at(k * rows, rows)
+            ysum[span, :] = (near[span, :].astype(F32) + ybuf[span, :].astype(F32)).astype(BF16)
+        x_copy(k).start()
+
+    def stage_z(k):
+        x_copy(k).wait_recv()
+        src = ysum if far is not None else near
+        mine = src[at(k * rows + x * half, half), :].astype(F32)
+        xsum[at(k * half, half), :] = (mine + xbuf[at(k * half, half), :].astype(F32)).astype(BF16)
+        for d in (3, 2, 1):
+            z_copy(k, d).start()
+
+    def stage_zg(k):
+        total = xsum[at(k * half + z * piece, piece), :].astype(F32)
+        for d in (1, 2, 3):
+            z_copy(k, d).wait_recv()
+            total = total + zbuf[d - 1, at(k * piece, piece), :].astype(F32)
+        out[0, own_piece(k), :] = total.astype(BF16)
+        for d in (3, 2, 1):
+            zg_copy(k, d).start()
+
+    def stage_xg(k):
+        for d in (1, 2, 3):
+            zg_copy(k, d).wait_recv()
+        xg_copy(k).start()
+
+    def stage_core(k):
+        xg_copy(k).wait_recv()
+        core_copy(k).start()
+
+    stages = [stage_x, stage_z, stage_zg, stage_xg, stage_core]
+    if far is not None:
+        stages.insert(0, stage_tp)
+
+    def tick(t, carry):
+        for s, stage in reversed(list(enumerate(stages))):
+            @pl.when((t >= s) & (t - s < chunks))
+            def _():
+                stage(t - s)
+        return carry
+
+    lax.fori_loop(0, chunks + len(stages) - 1, tick, 0)
+
+    def drain(k, carry):
+        if far is not None:
+            tp_copy(k).wait_send()
+        x_copy(k).wait_send()
+        for d in (1, 2, 3):
+            z_copy(k, d).wait_send()
+            zg_copy(k, d).wait_send()
+        xg_copy(k).wait_send()
+        core_copy(k).wait()
+        return carry
+
+    lax.fori_loop(0, chunks, drain, 0)
+
+
+SEM_NAMES = ("xs", "xr", "zs", "zr", "zgs", "zgr", "xgs", "xgr", "cs", "cr", "ys", "yr")
+
+
+def reduce_scratch(rows, cols, chunks, with_tp):
+    spaces = [
+        pltpu.VMEM((rows // 2, cols), BF16),
+        pltpu.VMEM((rows // 2, cols), BF16),
+        pltpu.VMEM((3, rows // 8, cols), BF16),
+    ]
+    if with_tp:
+        spaces += [pltpu.VMEM((rows, cols), BF16)] * 2
+    names = SEM_NAMES if with_tp else SEM_NAMES[:-2]
+    for name in names:
+        spaces.append(pltpu.SemaphoreType.DMA((3, chunks) if name[0] == "z" else (chunks,)))
+    return spaces
+
+
+def send_back_kernel(chunks, dq_ref, dkv_ref, near, dq_out, dkv_out, out, xbuf, xsum, zbuf, *rest):
+    place = Place()
+    count = dq_ref.shape[0]
+    me = place.seq * 2 + place.tp
+    names = SEM_NAMES[:-2]
+    sems = dict(zip(names, rest))
+    qs, qr, ks, kr = rest[len(names) :]
+    greet_all(count, me, place.seq, place.tp)
+
+    def start(k, carry):
+        chunk_copy(count, me, k, dkv_ref, dkv_out, ks, kr).start()
+        chunk_copy(count, me, k, dq_ref, dq_out, qs, qr).start()
+        return carry
+
+    lax.fori_loop(1, count, start, 0)
+    dq_out[me] = dq_ref[me]
+    dkv_out[me] = dkv_ref[me]
+    reduce_ticks(place, chunks, near, None, out, xbuf, xsum, zbuf, None, None, sems)
+
+    def wait(k, carry):
+        chunk_copy(count, me, k, dkv_ref, dkv_out, ks, kr).wait()
+        chunk_copy(count, me, k, dq_ref, dq_out, qs, qr).wait()
+        return carry
+
+    lax.fori_loop(1, count, wait, 0)
+
+
+def send_back(dq_chunks, dkv_chunks, near, chunks):
+    rows, cols = near.shape
+    count = dq_chunks.shape[0]
+    return pl.pallas_call(
+        functools.partial(send_back_kernel, chunks),
+        out_shape=(
+            jax.ShapeDtypeStruct(dq_chunks.shape, BF16),
+            jax.ShapeDtypeStruct(dkv_chunks.shape, BF16),
+            jax.ShapeDtypeStruct((2, rows, cols), BF16),
+        ),
+        in_specs=vmem(3),
+        out_specs=tuple(vmem(3)),
+        scratch_shapes=reduce_scratch(rows, cols, chunks, False)
+        + [pltpu.SemaphoreType.DMA((count,))] * 4,
+        compiler_params=pltpu.CompilerParams(
+            collective_id=1, has_side_effects=True, vmem_limit_bytes=VMEM_LIMIT
+        ),
+        name="send_back",
+    )(dq_chunks, dkv_chunks, near)
+
+
+def reduce_last_kernel(chunks, near, far, out, xbuf, xsum, zbuf, ybuf, ysum, *rest):
+    place = Place()
+    greet([place.tp_partner, place.x_partner, place.core_partner] + place.z_partners)
+    reduce_ticks(place, chunks, near, far, out, xbuf, xsum, zbuf, ybuf, ysum, dict(zip(SEM_NAMES, rest)))
+
+
+def reduce_last(near, far, chunks):
+    rows, cols = near.shape
+    return pl.pallas_call(
+        functools.partial(reduce_last_kernel, chunks),
+        out_shape=jax.ShapeDtypeStruct((2, rows, cols), BF16),
+        in_specs=vmem(2),
+        out_specs=vmem(1)[0],
+        scratch_shapes=reduce_scratch(rows, cols, chunks, True),
+        compiler_params=pltpu.CompilerParams(
+            collective_id=2, has_side_effects=True, vmem_limit_bytes=VMEM_LIMIT
+        ),
+        name="reduce_last",
+    )(near, far)
+
+
 def norm_parts(values):
     mean = jnp.mean(values, axis=-1, keepdims=True)
     centred = values - mean
@@ -468,7 +725,6 @@
     who = jnp.stack([tp, core]).astype(jnp.int32)
     over_tp = [(0, 1), (1, 0)]
     over_core = [(i, i ^ 1) for i in range(seq_count)]
-    chips = [[c + 2 * i for i in range(seq_count // 2)] for c in range(2)]
 
     def to_tp(values):
         return lax.ppermute(values, "tp", over_tp)
@@ -505,7 +761,7 @@
     kv_own = exchange(kv_chunks)
     kv_sib = to_sib(kv_own)
     q_own = exchange(q_chunks)
-    att_chunks, out_t, mass = attend(core, tables, q_own, kv_own, kv_sib)
+    att_chunks, out_t, mass, kv_pack, kv_turned = attend(core, tables, q_own, kv_own, kv_sib)
     attended = unpack_heads(who, exchange(att_chunks))
 
     input_f32 = tokens_in.astype(F32)
@@ -536,7 +792,22 @@
     d_down, gain_last, shift_last = norm_back(down, norm_gains[3], out_grad)
     bias_down_part = jnp.sum(d_down, axis=0)
     d_down_b = d_down.astype(BF16)
+    inner_sib, down_sib = to_sib(inner), to_sib(d_down_b)
+    active_sib = [to_sib(active4[r]) for r in (1, 3)]
+
+    def tie(values, *others):
+        return lax.optimization_barrier((values,) + others)[0]
+
+    def reduced(near, far):
+        return (near + to_tp(far).astype(F32)).astype(BF16)
+
     d_up4 = [gate4[r](dot_t(d_down_b, wd4[r]))[0].astype(BF16) for r in range(4)]
+    up_sib = [to_sib(d_up4[r]) for r in (1, 3)]
+    near_down, far_down = (
+        dot_rows(active4[r], d_down_b) + dot_rows(s, down_sib) for r, s in zip((0, 2), active_sib)
+    )
+    far_down = far_down.astype(BF16)
+    d_up4 = tie(d_up4, far_down)
     bias_up_part = [jnp.sum(d.astype(F32), axis=0) for d in d_up4]
     d_inner = sum(dot_t(d_up4[r], wu4[r]) for r in range(4))
     d_third, gain_third, shift_third = norm_back(hidden, norm_gains[2], d_inner)
@@ -544,43 +815,42 @@
     d_branch, gain_second, shift_second = norm_back(branch, norm_gains[1], d_hidden)
     bias_out_part = jnp.sum(d_branch, axis=0)
     d_branch_b = d_branch.astype(BF16)
+    branch_sib, normed_sib = to_sib(d_branch_b), to_sib(normed)
+    heads_sib = [to_sib(heads4[r]) for r in (1, 3)]
     da_own = exchange(spread(who, d_branch_b, wo4))
+    near_up, far_up = (
+        dot_rows(inner, d_up4[r]) + dot_rows(inner_sib, s) for r, s in zip((0, 2), up_sib)
+    )
+    near_out, far_out = (
+        dot_rows(heads4[r], d_branch_b) + dot_rows(s, branch_sib)
+        for r, s in zip((0, 2), heads_sib)
+    )
+    far_up, far_out = far_up.astype(BF16), far_out.astype(BF16)
+    g_down = reduced(near_down, far_down)
+    da_own = tie(da_own, far_up, far_out, g_down)
     dq_chunks, dkv_mine, dkv_theirs = attend_back(
-        core, tables, q_own, kv_own, kv_sib, da_own, out_t, mass
+        core, tables, q_own, da_own, out_t, mass, kv_pack, kv_turned
     )
     dkv_chunks = (dkv_mine + to_sib(dkv_theirs).astype(F32)).astype(BF16)
-    d_q, d_k, d_v = unpack_qkv(who, exchange(dq_chunks), exchange(dkv_chunks))
-
-    inner_sib, down_sib, branch_sib, normed_sib = (
-        to_sib(inner), to_sib(d_down_b), to_sib(d_branch_b), to_sib(normed)
-    )
-
-    def paired(left4, right):
-        own = [left4[r] for r in (0, 2)]
-        sib = [to_sib(left4[r]) for r in (1, 3)]
-        near, far = (right(o, s) for o, s in zip(own, sib))
-        return near, far.astype(BF16)
-
-    def reduced(pair):
-        near, far = pair
-        return (near + to_tp(far).astype(F32)).astype(BF16)
-
-    g_down = reduced(paired(active4, lambda o, s: dot_rows(o, d_down_b) + dot_rows(s, down_sib)))
-    g_up = reduced(paired(d_up4, lambda o, s: dot_rows(inner, o) + dot_rows(inner_sib, s)))
-    g_out = reduced(paired(heads4, lambda o, s: dot_rows(o, d_branch_b) + dot_rows(s, branch_sib)))
-    g_down, g_up, g_out = lax.psum((g_down, g_up, g_out), "seq", axis_index_groups=chips)
+    near_all = jnp.concatenate([g_down, reduced(near_up, far_up), reduced(near_out, far_out)])
+    dq_home, dkv_home, sums = send_back(dq_chunks, dkv_chunks, near_all, CHUNKS)
+    d_q, d_k, d_v = unpack_qkv(who, dq_home, dkv_home)
 
     mixed4 = [
         jnp.concatenate([cols(d, r, 256) for d in (d_q, d_k, d_v)], axis=1) for r in range(4)
     ]
+    mixed_sib = [to_sib(mixed4[r]) for r in (1, 3)]
+    near_qkv, far_qkv = (
+        dot_rows(normed, mixed4[r]) + dot_rows(normed_sib, s) for r, s in zip((0, 2), mixed_sib)
+    )
+    far_qkv = far_qkv.astype(BF16)
+    mixed4 = tie(mixed4, far_qkv)
     d_normed = sum(dot_t(mixed4[r], wq4[r]) for r in range(4))
     d_first, gain_first, shift_first = norm_back(input_f32, norm_gains[0], d_normed)
     grad_x = d_hidden + d_first
-    g_qkv = reduced(paired(mixed4, lambda o, s: dot_rows(normed, o) + dot_rows(normed_sib, s)))
-    g_qkv = lax.psum(g_qkv, "seq", axis_index_groups=chips).reshape(width, 3, -1)
-
-    def joined(own, axis):
-        sib = to_sib(own)
+
+    def joined(pair, axis):
+        own, sib = pair
         first = jnp.concatenate([own, sib], axis=axis).astype(F32)
         second = jnp.concatenate([sib, own], axis=axis).astype(F32)
         return jnp.where(core == 0, first, second)
@@ -600,6 +870,11 @@
     )
     vectors = jnp.concatenate([vectors, absolute(bias_up_part).reshape(4, -1)])
     vectors = sum_all(vectors, seq_count)
+    near_qkv, vectors = tie((near_qkv.astype(BF16), vectors), vectors)
+    sums_qkv = reduce_last(near_qkv, far_qkv, CHUNKS_LAST).reshape(2, width, 3, -1)
+    hidden_rows = g_down.shape[0]
+    up_rows = slice(hidden_rows, hidden_rows + width)
+    out_rows = slice(hidden_rows + width, None)
     own_cols = bias_qv.shape[1]
     grad_bias_qv = lax.dynamic_slice_in_dim(vectors[10:12], tp * own_cols, own_cols, 1)
     grad_bias_up = lax.dynamic_slice_in_dim(
@@ -608,13 +883,13 @@
     return (
         result,
         grad_x,
-        joined(g_qkv, 2),
+        joined(sums_qkv, 2),
         grad_bias_qv,
-        joined(g_out, 0),
+        joined(sums[:, out_rows], 0),
         vectors[8],
-        joined(g_up, 1),
+        joined(sums[:, up_rows], 1),
         grad_bias_up,
-        joined(g_down, 0),
+        joined(sums[:, :hidden_rows], 0),
         vectors[9],
         vectors[0:4],
         vectors[4:8],

time: 949 us -> 845 us (0.89)
  waiting for transfers between devices: 482 us -> 113 us
  Pallas kernels: 172 us -> 429 us
  blocking collectives: 31 us -> 53.6 us
  local copies, waits for them, and re-layouts: 44.3 us -> 58.2 us
  between operations: 15.8 us -> 1.92 us
    pallas_call x0 -> x2, Pallas kernels: none -> 271 us  [the longest x1 198 us: send_back(): pl.pallas_call(functools.partial(send_back_kernel, chunks), out_shape=(ja...]
    psum x1 -> x0, waiting for transfers between devices: 201 us -> none  [fast_local(): lax.psum(g_qkv, 'seq', axis_index_groups=chips).reshape(width, 3, -1)]
    all_to_all x5 -> x3, waiting for transfers between devices: 109 us -> 16.6 us  [exchange(): return lax.all_to_all(chunks, ('seq', 'tp'), 0, 0, tiled=True)]
    ppermute x9 -> x8, waiting for transfers between devices: 170 us -> 95 us  [to_tp(): return lax.ppermute(values, 'tp', over_tp)]
    all_to_all x1, blocking collectives: 31 us -> 53.6 us  [exchange(): return lax.all_to_all(chunks, ('seq', 'tp'), 0, 0, tiled=True)]
    another operation x1 -> x6, local copies, waits for them, and re-layouts: 0.61 us -> 14.8 us  [the longest x5 14.2 us: joined(): own, sib = pair]
    pallas_call x1, Pallas kernels: 63.4 us -> 53.1 us  [attend(): pl.pallas_call(attend_kernel, out_shape=(jax.ShapeDtypeStruct((blocks, QU...]
    all_to_all x5 -> x3, starting transfers between devices: 20 us -> 12.6 us  [exchange(): return lax.all_to_all(chunks, ('seq', 'tp'), 0, 0, tiled=True)]
  transfers between devices with their start and end apart: 38 -> 30, of which waited for: 11 -> 6; matrix products, arithmetic and copies ran while one was open for 14% -> 17% of each run, Pallas kernels for 9% -> 39%
where the time goes in v2:
time: 845 us; the launch traced here: 838 us
  Pallas kernels  429 us (51%)
  waiting for transfers between devices  113 us (13%)
  matrix products  108 us (13%)
  local copies, waits for them, and re-layouts  58.2 us (7%)
  blocking collectives  53.6 us (6%)
  other arithmetic  44.9 us (5%)
  starting transfers between devices  29.7 us (4%)
    pallas_call x1, Pallas kernels, send_back(): pl.pallas_call(functools.partial(send_back_kernel, chunks), out_shape=(ja...  198 us
    ppermute x8, waiting for transfers between devices, to_tp(): return lax.ppermute(values, 'tp', over_tp)  95 us
    pallas_call x1, Pallas kernels, reduce_last(): pl.pallas_call(functools.partial(reduce_last_kernel, chunks), out_shape=j...  72.5 us
    pallas_call x1, Pallas kernels, attend_back(): pl.pallas_call(attend_back_kernel, out_shape=(jax.ShapeDtypeStruct((block...  62.5 us
    all_to_all x1, blocking collectives, exchange(): return lax.all_to_all(chunks, ('seq', 'tp'), 0, 0, tiled=True)  53.6 us
    pallas_call x1, Pallas kernels, attend(): pl.pallas_call(attend_kernel, out_shape=(jax.ShapeDtypeStruct((blocks, QU...  53.1 us
    dot_general x16, matrix products, dot_rows(): lax.dot_general(a, b, (((0,), (0,)), ((), ())), preferred_element_type=F32)  40.5 us
    dot_general x12, matrix products, dot_t(): lax.dot_general(a, b, (((1,), (1,)), ((), ())), preferred_element_type=F32)  38 us
  transfers between devices with their start and end apart: 30, of which 6 were waited for; matrix products, arithmetic and copies ran while one was open for 17% of the time, Pallas kernels for 39%

profile of v2, /device:TPU:0, one launch (start us, length us, event | category | flops | bytes accessed | tf_op | source)
XLA Modules:
  0.0 837.7 jit_solution(4472364579665837733)
XLA Ops:
  7.8 34.5 %collective-permute-done.2 = bf16[1024,3,256]{0,2,1:T(8,128)(2,1)} collective-permute-done((bf16[1024,3,256]{0,2,1:T(8,128)(2,1)S(1)}, bf16[1024,3,256]{0,2,1:T(8,128)(2,1)}, u32[]{:S(2)}, u32[]{:S(2)}) %collective-permute-start.2) | collective-permute-done | bytes 1572896 | tf_op jit(solution)/shard_map/ppermute | solution.py:730
  57.5 8.7 %project.1 = (bf16[512,1024]{1,0:T(8,128)(2,1)}, bf16[32,128,128]{2,1,0:T(8,128)(2,1)}, bf16[32,256,128]{2,1,0:T(8,128)(2,1)}) custom-call(s32[2]{0:T(128)} %pad_add_fusion.who_ref, bf16[512,1024]{1,0:T(8,128)(2,1)} %x_ref.1, f32[1,1024]{1,0:T(1,128)} %get-tuple-element.170.gain_ref, f32[1,1024]{1,0:T(1,128)} %get-tuple-element.197.shift_ref, ...), custom_call_target="tpu_custom_call" | custom-call | tf_op jit(solution)/shard_map/project/pallas_call | solution.py:339
  66.2 53.6 %all_to_all.20.own_ref = bf16[32,256,128]{2,1,0:T(8,128)(2,1)S(1)} all-to-all(bf16[32,256,128]{2,1,0:T(8,128)(2,1)} %get-tuple-element.41), channel_id=1, replica_groups=mesh['seq'=16,'tp'=2] {'seq','tp'}, dimensions={0} | all-to-all | bytes 4194304 | tf_op jit(solution)/shard_map/all_to_all | solution.py:736
  119.9 3.8 all-to-all-start
  133.2 16.6 %all-to-all-done.q_ref = bf16[32,128,128]{2,1,0:T(8,128)(2,1)S(1)} async-done(((bf16[32,128,128]{2,1,0:T(8,128)(2,1)}), bf16[32,128,128]{2,1,0:T(8,128)(2,1)S(1)}, u32[]{:S(2)}, u32[]{:S(2)}) %all-to-all-start) | async-done | bytes 1048608 | tf_op jit(solution)/shard_map/all_to_all | solution.py:736
  150.9 53.1 %attend.1 = (bf16[32,128,128]{2,1,0:T(8,128)(2,1)}, f32[32,64,256]{2,1,0:T(8,128)}, f32[32,1,256]{2,1,0:T(1,128)}, bf16[17408,128]{1,0:T(8,128)(2,1)}, bf16[128,17408]{1,0:T(8,128)(2,1)}) custom-call(s32[1]{0:T(128)} %bitcast.1.part_ref, s32[5,32]{1,0:T(8,128)} %stack.68.tab, s32[32,1,256]{2,1,0:T(1,128)} %broadcast_in_dim.123.low_ref, ...), custom_call_target="tpu_custom_call" | custom-call | flops 40000000000 | bytes 20971520 | tf_op jit(solution)/shard_map/attend/pallas_call | solution.py:227
  203.9 3.8 all-to-all-start.2
  211.3 38.9 %collective-permute-done.5.w2 = bf16[256,1024]{1,0:T(8,128)(2,1)} collective-permute-done((bf16[256,1024]{1,0:T(8,128)(2,1)S(1)}, bf16[256,1024]{1,0:T(8,128)(2,1)}, u32[]{:S(2)}, u32[]{:S(2)}) %collective-permute-start.5) | collective-permute-done | bytes 524320 | tf_op jit(solution)/shard_map/ppermute | solution.py:730
  293.2 4.0 fusion.17
  304.7 5.2 fusion.38
  310.3 3.6 fusion.73
  313.9 4.0 fusion.31
  331.8 4.1 multiply_reduce_fusion.1
  341.7 4.3 spread.1
  346.0 5.0 all-to-all-start.3
  355.6 4.2 add_convert_fusion.3
  366.2 13.0 %collective-permute-done.18 = bf16[1024,1024]{1,0:T(8,128)(2,1)} collective-permute-done((bf16[1024,1024]{1,0:T(8,128)(2,1)}, bf16[1024,1024]{1,0:T(8,128)(2,1)}, u32[]{:S(2)}, u32[]{:S(2)}) %collective-permute-start.18) | collective-permute-done | bytes 2097184 | tf_op jit(solution)/shard_map/ppermute | solution.py:730
  379.3 4.7 add_convert_fusion.2
  384.0 62.5 %attend_back.1 = (bf16[32,128,128]{2,1,0:T(8,128)(2,1)}, f32[32,256,128]{2,1,0:T(8,128)}, bf16[32,256,128]{2,1,0:T(8,128)(2,1)}) custom-call(s32[1]{0:T(128)} %bitcast.1.part_ref, s32[5,32]{1,0:T(8,128)} %stack.68.tab, s32[32,1,256]{2,1,0:T(1,128)} %broadcast_in_dim.123.low_ref, s32[32,1,256]{2,1,0:T(1,128)} %maximum_minimum_fusion.high_ref, ...), custom_call_target="tpu_custom_call" | custom-call | flops 60000002048 | bytes 31457280 | tf_op jit(solution)/shard_map/attend_back/pallas_call | solution.py:250
  452.5 8.6 %collective-permute-done.23 = bf16[256,1024]{1,0:T(8,128)(2,1)S(1)} collective-permute-done((bf16[256,1024]{1,0:T(8,128)(2,1)}, bf16[256,1024]{1,0:T(8,128)(2,1)S(1)}, u32[]{:S(2)}, u32[]{:S(2)}) %collective-permute-start.23) | collective-permute-done | bytes 524320 | tf_op jit(solution)/shard_map/ppermute | solution.py:730
  463.0 3.8 add_convert_fusion
  474.3 198.1 %send_back.1 = (bf16[32,128,128]{2,1,0:T(8,128)(2,1)}, bf16[32,256,128]{2,1,0:T(8,128)(2,1)}, bf16[2,2304,1024]{2,1,0:T(8,128)(2,1)}) custom-call(bf16[32,128,128]{2,1,0:T(8,128)(2,1)} %get-tuple-element.52.dq_ref, bf16[32,256,128]{2,1,0:T(8,128)(2,1)} %add_convert_fusion.1.dkv_ref, bf16[2304,1024]{1,0:T(8,128)(2,1)} %pad_maximum_fusion.near), custom_call_target="tpu_custom_call" | custom-call | tf_op jit(solution)/shard_map/send_back/pallas_call | solution.py:661
  672.4 4.8 unpack_qkv.1
  680.6 4.0 slice_bitcast_fusion.1
  687.3 4.1 convert_select_fusion.1
  691.5 4.4 convert_select_fusion
  707.7 4.5 fusion.9
  713.5 22.4 %sum_all.1 = f32[16,1024]{1,0:T(8,128)} custom-call(f32[16,1024]{1,0:T(8,128)} %concatenate.63.mine_ref), custom_call_target="tpu_custom_call" | custom-call | tf_op jit(solution)/shard_map/sum_all/pallas_call | solution.py:445
  739.6 72.5 %reduce_last.1 = bf16[2,1024,768]{2,1,0:T(8,128)(2,1)} custom-call(bf16[1024,768]{1,0:T(8,128)(2,1)} %add_convert_fusion.5.near, bf16[1024,768]{1,0:T(8,128)(2,1)} %add_convert_fusion.6.far), custom_call_target="tpu_custom_call" | custom-call | tf_op jit(solution)/shard_map/reduce_last/pallas_call | solution.py:687
  812.1 3.7 fusion.82
  821.1 5.1 convert_select_fusion.2
  826.2 6.6 copy.57
  (283 shorter events, 165.6 us)
Async XLA Ops:
  4.8 37.5 %collective-permute-start.2 = (bf16[1024,3,256]{0,2,1:T(8,128)(2,1)S(1)}, bf16[1024,3,256]{0,2,1:T(8,128)(2,1)}, u32[]{:S(2)}, u32[]{:S(2)}) collective-permute-start(bf16[1024,3,256]{0,2,1:T(8,128)(2,1)S(1)} %copy.58), channel_id=1, source_target_pairs={{0,1},{1,0},{2,3},{3,2},{4,5},{5,4},{6,7},{7,6},{8,9},{9,8},{10,11... | collective-permute-start | bytes 4718600 | tf_op jit(solution)/shard_map/ppermute | solution.py:730
  42.3 12.6 %collective-permute-start.3 = (bf16[1024,3,256]{0,2,1:T(8,128)(2,1)}, bf16[1024,3,256]{0,2,1:T(8,128)(2,1)}, u32[]{:S(2)}, u32[]{:S(2)}) collective-permute-start(bf16[1024,3,256]{0,2,1:T(8,128)(2,1)} %collective-permute-done.2), channel_id=1, source_target_pairs={{0,2},{2,0},{4,6},{6,4},{8,10},{10,8},{12,14},{14,12},{16,18},{18,... | collective-permute-start | bytes 4718600 | tf_op jit(solution)/shard_map/ppermute | solution.py:733
  42.4 8.2 collective-permute-start
  50.6 1.2 collective-permute-start.1
  119.8 30.0 %collective-permute-start.4 = (bf16[32,256,128]{2,1,0:T(8,128)(2,1)S(1)}, bf16[32,256,128]{2,1,0:T(8,128)(2,1)}, u32[]{:S(2)}, u32[]{:S(2)}) collective-permute-start(bf16[32,256,128]{2,1,0:T(8,128)(2,1)S(1)} %all_to_all.20.own_ref), channel_id=1, source_target_pairs={{0,2},{2,0},{4,6},{6,4},{8,10},{10,8},{12,14},{14,12},{16,18},{18,... | collective-permute-start | bytes 6291464 | tf_op jit(solution)/shard_map/ppermute | solution.py:733
  119.9 30.0 %all-to-all-start = ((bf16[32,128,128]{2,1,0:T(8,128)(2,1)}), bf16[32,128,128]{2,1,0:T(8,128)(2,1)S(1)}, u32[]{:S(2)}, u32[]{:S(2)}) async-start(bf16[32,128,128]{2,1,0:T(8,128)(2,1)} %get-tuple-element.40), calls=%async_computation | async-start | bytes 2097152 | tf_op jit(solution)/shard_map/all_to_all | solution.py:736
  126.9 123.3 %collective-permute-start.7 = (bf16[1024,1024]{1,0:T(8,128)(2,1)}, bf16[1024,1024]{1,0:T(8,128)(2,1)}, u32[]{:S(2)}, u32[]{:S(2)}) collective-permute-start(bf16[1024,1024]{1,0:T(8,128)(2,1)} %constant_dynamic-slice_fusion.2), channel_id=1, source_target_pairs={{0,1},{1,0},{2,3},{3,2},{4,5},{5,4},{6,7},{7,6},{8,9},{9,8},{10,11... | collective-permute-start | bytes 6291464 | tf_op jit(solution)/shard_map/ppermute | solution.py:730
  130.3 120.5 %collective-permute-start.8 = (bf16[1024,1024]{1,0:T(8,128)(2,1)}, bf16[1024,1024]{1,0:T(8,128)(2,1)}, u32[]{:S(2)}, u32[]{:S(2)}) collective-permute-start(bf16[1024,1024]{1,0:T(8,128)(2,1)} %constant_dynamic-slice_fusion.1), channel_id=1, source_target_pairs={{0,1},{1,0},{2,3},{3,2},{4,5},{5,4},{6,7},{7,6},{8,9},{9,8},{10,11... | collective-permute-start | bytes 6291464 | tf_op jit(solution)/shard_map/ppermute | solution.py:730
  203.9 46.9 %all-to-all-start.2 = ((bf16[32,128,128]{2,1,0:T(8,128)(2,1)}), bf16[32,128,128]{2,1,0:T(8,128)(2,1)S(1)}, u32[]{:S(2)}, u32[]{:S(2)}) async-start(bf16[32,128,128]{2,1,0:T(8,128)(2,1)} %get-tuple-element.42), calls=%async_computation.2 | async-start | bytes 2097152 | tf_op jit(solution)/shard_map/all_to_all | solution.py:736
  209.1 46.8 %copy-start.10 = (bf16[256,1024]{1,0:T(8,128)(2,1)}, bf16[256,1024]{1,0:T(8,128)(2,1)S(1)}, u32[]{:S(2)}) copy-start(bf16[256,1024]{1,0:T(8,128)(2,1)S(1)} %get-tuple-element.159.w0) | copy-start | bytes 1572868
  209.1 41.1 %collective-permute-start.5 = (bf16[256,1024]{1,0:T(8,128)(2,1)S(1)}, bf16[256,1024]{1,0:T(8,128)(2,1)}, u32[]{:S(2)}, u32[]{:S(2)}) collective-permute-start(bf16[256,1024]{1,0:T(8,128)(2,1)S(1)} %get-tuple-element.159.w0), channel_id=1, source_target_pairs={{0,1},{1,0},{2,3},{3,2},{4,5},{5,4},{6,7},{7,6},{8,9},{9,8},{10,11... | collective-permute-start | bytes 1572872 | tf_op jit(solution)/shard_map/ppermute | solution.py:730
  211.1 48.8 %copy-start.30 = (f32[512]{0:T(512)}, f32[512]{0:T(512)S(1)}, u32[]{:S(2)}) copy-start(f32[512]{0:T(512)S(1)} %broadcast_multiply_fusion.4) | copy-start | bytes 6148
  250.2 7.7 collective-permute-start.6
  250.2 24.2 %collective-permute-start.9 = (bf16[1024,1024]{1,0:T(8,128)(2,1)}, bf16[1024,1024]{1,0:T(8,128)(2,1)}, u32[]{:S(2)}, u32[]{:S(2)}) collective-permute-start(bf16[1024,1024]{1,0:T(8,128)(2,1)} %collective-permute-done.7), channel_id=1, source_target_pairs={{0,2},{2,0},{4,6},{6,4},{8,10},{10,8},{12,14},{14,12},{16,18},{18,... | collective-permute-start | bytes 6291464 | tf_op jit(solution)/shard_map/ppermute | solution.py:733
  250.7 33.7 %collective-permute-start.10 = (bf16[1024,1024]{1,0:T(8,128)(2,1)}, bf16[1024,1024]{1,0:T(8,128)(2,1)}, u32[]{:S(2)}, u32[]{:S(2)}) collective-permute-start(bf16[1024,1024]{1,0:T(8,128)(2,1)} %collective-permute-done.8), channel_id=1, source_target_pairs={{0,2},{2,0},{4,6},{6,4},{8,10},{10,8},{12,14},{14,12},{16,18},{18,... | collective-permute-start | bytes 6291464 | tf_op jit(solution)/shard_map/ppermute | solution.py:733
  298.8 19.0 %collective-permute-start.11 = (bf16[512,1024]{1,0:T(8,128)(2,1)S(1)}, bf16[512,1024]{1,0:T(8,128)(2,1)S(1)}, u32[]{:S(2)}, u32[]{:S(2)}) collective-permute-start(bf16[512,1024]{1,0:T(8,128)(2,1)S(1)} %get-tuple-element.188), channel_id=1, source_target_pairs={{0,2},{2,0},{4,6},{6,4},{8,10},{10,8},{12,14},{14,12},{16,18},{18,... | collective-permute-start | bytes 3145736 | tf_op jit(solution)/shard_map/ppermute | solution.py:733
  299.4 18.5 %collective-permute-start.12 = (bf16[512,1024]{1,0:T(8,128)(2,1)S(1)}, bf16[512,1024]{1,0:T(8,128)(2,1)S(1)}, u32[]{:S(2)}, u32[]{:S(2)}) collective-permute-start(bf16[512,1024]{1,0:T(8,128)(2,1)S(1)} %get-tuple-element.124), channel_id=1, source_target_pairs={{0,2},{2,0},{4,6},{6,4},{8,10},{10,8},{12,14},{14,12},{16,18},{18,... | collective-permute-start | bytes 3145736 | tf_op jit(solution)/shard_map/ppermute | solution.py:733
  299.4 55.6 %collective-permute-start.13 = (bf16[512,1024]{1,0:T(8,128)(2,1)S(1)}, bf16[512,1024]{1,0:T(8,128)(2,1)}, u32[]{:S(2)}, u32[]{:S(2)}) collective-permute-start(bf16[512,1024]{1,0:T(8,128)(2,1)S(1)} %add_convert_fusion.8), channel_id=1, source_target_pairs={{0,2},{2,0},{4,6},{6,4},{8,10},{10,8},{12,14},{14,12},{16,18},{18,... | collective-permute-start | bytes 3145736 | tf_op jit(solution)/shard_map/ppermute | solution.py:733
  300.6 65.6 %collective-permute-start.17 = (bf16[512,1024]{1,0:T(8,128)(2,1)}, bf16[512,1024]{1,0:T(8,128)(2,1)}, u32[]{:S(2)}, u32[]{:S(2)}) collective-permute-start(bf16[512,1024]{1,0:T(8,128)(2,1)} %get-tuple-element.186), channel_id=1, source_target_pairs={{0,2},{2,0},{4,6},{6,4},{8,10},{10,8},{12,14},{14,12},{16,18},{18,... | collective-permute-start | bytes 3145736 | tf_op jit(solution)/shard_map/ppermute | solution.py:733
  309.8 45.4 %collective-permute-start.14 = (bf16[512,1024]{1,0:T(8,128)(2,1)}, bf16[512,1024]{1,0:T(8,128)(2,1)}, u32[]{:S(2)}, u32[]{:S(2)}) collective-permute-start(bf16[512,1024]{1,0:T(8,128)(2,1)} %fusion.38), channel_id=1, source_target_pairs={{0,2},{2,0},{4,6},{6,4},{8,10},{10,8},{12,14},{14,12},{16,18},{18,... | collective-permute-start | bytes 3145736 | tf_op jit(solution)/shard_map/ppermute | solution.py:733
  320.6 58.6 %collective-permute-start.18 = (bf16[1024,1024]{1,0:T(8,128)(2,1)}, bf16[1024,1024]{1,0:T(8,128)(2,1)}, u32[]{:S(2)}, u32[]{:S(2)}) collective-permute-start(bf16[1024,1024]{1,0:T(8,128)(2,1)} %add_convert_fusion.4), channel_id=1, source_target_pairs={{0,1},{1,0},{2,3},{3,2},{4,5},{5,4},{6,7},{7,6},{8,9},{9,8},{10,11... | collective-permute-start | bytes 6291464 | tf_op jit(solution)/shard_map/ppermute | solution.py:730
  341.6 20.4 %collective-permute-start.16 = (bf16[512,1024]{1,0:T(8,128)(2,1)}, bf16[512,1024]{1,0:T(8,128)(2,1)}, u32[]{:S(2)}, u32[]{:S(2)}) collective-permute-start(bf16[512,1024]{1,0:T(8,128)(2,1)} %get-tuple-element.126.d_ref), channel_id=1, source_target_pairs={{0,2},{2,0},{4,6},{6,4},{8,10},{10,8},{12,14},{14,12},{16,18},{18,... | collective-permute-start | bytes 3145736 | tf_op jit(solution)/shard_map/ppermute | solution.py:733
  346.0 38.0 %all-to-all-start.3 = ((bf16[32,128,128]{2,1,0:T(8,128)(2,1)}), bf16[32,128,128]{2,1,0:T(8,128)(2,1)}, u32[]{:S(2)}, u32[]{:S(2)}) async-start(bf16[32,128,128]{2,1,0:T(8,128)(2,1)} %spread.1), calls=%async_computation.3 | async-start | bytes 2097152 | tf_op jit(solution)/shard_map/all_to_all | solution.py:736
  355.0 107.9 %collective-permute-start.20 = (bf16[512,1024]{1,0:T(8,128)(2,1)}, bf16[512,1024]{1,0:T(8,128)(2,1)}, u32[]{:S(2)}, u32[]{:S(2)}) collective-permute-start(bf16[512,1024]{1,0:T(8,128)(2,1)} %fusion.24), channel_id=1, source_target_pairs={{0,2},{2,0},{4,6},{6,4},{8,10},{10,8},{12,14},{14,12},{16,18},{18,... | collective-permute-start | bytes 3145736 | tf_op jit(solution)/shard_map/ppermute | solution.py:733
  355.3 6.5 collective-permute-start.15
  361.8 90.4 %collective-permute-start.22 = (bf16[512,256]{1,0:T(8,128)(2,1)S(1)}, bf16[512,256]{1,0:T(8,128)(2,1)}, u32[]{:S(2)}, u32[]{:S(2)}) collective-permute-start(bf16[512,256]{1,0:T(8,128)(2,1)S(1)} %get-tuple-element.156), channel_id=1, source_target_pairs={{0,2},{2,0},{4,6},{6,4},{8,10},{10,8},{12,14},{14,12},{16,18},{18,... | collective-permute-start | bytes 786440 | tf_op jit(solution)/shard_map/ppermute | solution.py:733
  362.0 100.9 %collective-permute-start.21 = (bf16[1024,1024]{1,0:T(8,128)(2,1)}, bf16[1024,1024]{1,0:T(8,128)(2,1)}, u32[]{:S(2)}, u32[]{:S(2)}) collective-permute-start(bf16[1024,1024]{1,0:T(8,128)(2,1)} %add_convert_fusion.3), channel_id=1, source_target_pairs={{0,1},{1,0},{2,3},{3,2},{4,5},{5,4},{6,7},{7,6},{8,9},{9,8},{10,11... | collective-permute-start | bytes 6291464 | tf_op jit(solution)/shard_map/ppermute | solution.py:730
  446.5 23.0 %collective-permute-start.19 = (bf16[32,256,128]{2,1,0:T(8,128)(2,1)}, bf16[32,256,128]{2,1,0:T(8,128)(2,1)}, u32[]{:S(2)}, u32[]{:S(2)}) collective-permute-start(bf16[32,256,128]{2,1,0:T(8,128)(2,1)} %get-tuple-element.54), channel_id=1, source_target_pairs={{0,2},{2,0},{4,6},{6,4},{8,10},{10,8},{12,14},{14,12},{16,18},{18,... | collective-permute-start | bytes 6291464 | tf_op jit(solution)/shard_map/ppermute | solution.py:733
  446.5 14.6 %collective-permute-start.23 = (bf16[256,1024]{1,0:T(8,128)(2,1)}, bf16[256,1024]{1,0:T(8,128)(2,1)S(1)}, u32[]{:S(2)}, u32[]{:S(2)}) collective-permute-start(bf16[256,1024]{1,0:T(8,128)(2,1)} %fusion.50), channel_id=1, source_target_pairs={{0,1},{1,0},{2,3},{3,2},{4,5},{5,4},{6,7},{7,6},{8,9},{9,8},{10,11... | collective-permute-start | bytes 1572872 | tf_op jit(solution)/shard_map/ppermute | solution.py:730
  452.2 243.7 %collective-permute-start.24 = (bf16[512,1024]{1,0:T(8,128)(2,1)S(1)}, bf16[512,1024]{1,0:T(8,128)(2,1)S(1)}, u32[]{:S(2)}, u32[]{:S(2)}) collective-permute-start(bf16[512,1024]{1,0:T(8,128)(2,1)S(1)} %copy-done.11), channel_id=1, source_target_pairs={{0,2},{2,0},{4,6},{6,4},{8,10},{10,8},{12,14},{14,12},{16,18},{18,... | collective-permute-start | bytes 3145736 | tf_op jit(solution)/shard_map/ppermute | solution.py:733
  684.7 11.2 %collective-permute-start.25 = (bf16[512,768]{1,0:T(8,128)(2,1)S(1)}, bf16[512,768]{1,0:T(8,128)(2,1)S(1)}, u32[]{:S(2)}, u32[]{:S(2)}) collective-permute-start(bf16[512,768]{1,0:T(8,128)(2,1)S(1)} %pad_maximum_fusion.4), channel_id=1, source_target_pairs={{0,2},{2,0},{4,6},{6,4},{8,10},{10,8},{12,14},{14,12},{16,18},{18,... | collective-permute-start | bytes 2359304 | tf_op jit(solution)/shard_map/ppermute | solution.py:733
  685.2 19.0 %collective-permute-start.26 = (bf16[512,768]{1,0:T(8,128)(2,1)S(1)}, bf16[512,768]{1,0:T(8,128)(2,1)S(1)}, u32[]{:S(2)}, u32[]{:S(2)}) collective-permute-start(bf16[512,768]{1,0:T(8,128)(2,1)S(1)} %pad_maximum_fusion.2), channel_id=1, source_target_pairs={{0,2},{2,0},{4,6},{6,4},{8,10},{10,8},{12,14},{14,12},{16,18},{18,... | collective-permute-start | bytes 2359304 | tf_op jit(solution)/shard_map/ppermute | solution.py:733
  (43 other events, 426.8 us)

commit v3 on v2

--- a/solution.py
+++ b/solution.py
@@ -15,8 +15,8 @@
 STEP_F = 1024
 STEP_B = 512
 UNROLL = 4
-CHUNKS = 9
-CHUNKS_LAST = 8
+CHUNK_ROWS = 256
+FIRST_TICKS = 6
 VMEM_LIMIT = 58 << 20
 
 EPS = 1e-05
@@ -298,14 +298,14 @@
             out_ref[chunk_of(who, quarter, 2 * pair + 1, half)] = odd.astype(BF16)
 
 
-def load_packed(who, quarter, ref, out_ref):
+def load_packed(who, quarter, ref, out_ref, base):
     low = low_lanes(QUART)
     for pair in range(2):
         for half in range(2):
             even = ref[chunk_of(who, quarter, 2 * pair, half)].astype(F32)
             odd = ref[chunk_of(who, quarter, 2 * pair + 1, half)].astype(F32)
             top = half * HALF
-            lanes = slice(quarter * 256 + pair * 128, quarter * 256 + pair * 128 + 128)
+            lanes = slice(base + pair * 128, base + pair * 128 + 128)
             out_ref[top : top + QUART, lanes] = jnp.where(low, even, swap_lanes(odd)).astype(BF16)
             out_ref[top + QUART : top + HALF, lanes] = jnp.where(low, swap_lanes(even), odd).astype(BF16)
 
@@ -353,7 +353,7 @@
 def unpack_heads_kernel(who_ref, ref, out_ref):
     who = (who_ref[0], who_ref[1])
     for quarter in range(4):
-        load_packed(who, quarter, ref, out_ref)
+        load_packed(who, quarter, ref, out_ref, quarter * 256)
 
 
 def unpack_heads(who, chunks):
@@ -388,75 +388,6 @@
     )(who, d_branch, *weights)
 
 
-def unpack_qkv_kernel(who_ref, dq_ref, dkv_ref, q_ref, k_ref, v_ref):
-    who = (who_ref[0], who_ref[1])
-    low = low_lanes(HALF)
-    for quarter in range(4):
-        load_packed(who, quarter, dq_ref, q_ref)
-        for pair in range(2):
-            lanes = slice(quarter * 256 + pair * 128, quarter * 256 + pair * 128 + 128)
-            for half in range(2):
-                rows = slice(half * HALF, half * HALF + HALF)
-                even = dkv_ref[chunk_of(who, quarter, 2 * pair, half)].astype(F32)
-                odd = dkv_ref[chunk_of(who, quarter, 2 * pair + 1, half)].astype(F32)
-                k_ref[rows, lanes] = jnp.where(low, even, swap_lanes(odd)).astype(BF16)
-                v_ref[rows, lanes] = jnp.where(low, swap_lanes(even), odd).astype(BF16)
-
-
-def unpack_qkv(who, dq_chunks, dkv_chunks):
-    shape = jax.ShapeDtypeStruct((BLK, 1024), BF16)
-    return pl.pallas_call(
-        unpack_qkv_kernel,
-        out_shape=(shape, shape, shape),
-        in_specs=smem(1) + vmem(2),
-        out_specs=tuple(vmem(3)),
-        compiler_params=pltpu.CompilerParams(vmem_limit_bytes=VMEM_LIMIT),
-        name="unpack_qkv",
-    )(who, dq_chunks, dkv_chunks)
-
-
-def sum_all_kernel(seq_bits, mine_ref, out_ref, slots, send, recv):
-    seq, tp = lax.axis_index("seq"), lax.axis_index("tp")
-    partners = [(seq ^ (1 << bit), tp) for bit in range(seq_bits)]
-    partners.insert(1, (seq, tp ^ 1))
-    barrier = pltpu.get_barrier_semaphore()
-    for partner in partners:
-        pl.semaphore_signal(barrier, inc=1, device_id=partner, device_id_type=MESH)
-    pl.semaphore_wait(barrier, len(partners))
-    out_ref[...] = mine_ref[...]
-    for step, partner in enumerate(partners):
-        slots[step] = out_ref[...]
-        copy = pltpu.make_async_remote_copy(
-            src_ref=slots.at[step],
-            dst_ref=slots.at[len(partners) + step],
-            send_sem=send.at[step],
-            recv_sem=recv.at[step],
-            device_id=partner,
-            device_id_type=MESH,
-        )
-        copy.start()
-        copy.wait()
-        out_ref[...] += slots[len(partners) + step]
-
-
-def sum_all(values, seq_count):
-    seq_bits = seq_count.bit_length() - 1
-    steps = seq_bits + 1
-    return pl.pallas_call(
-        functools.partial(sum_all_kernel, seq_bits),
-        out_shape=jax.ShapeDtypeStruct(values.shape, values.dtype),
-        in_specs=vmem(1),
-        out_specs=vmem(1)[0],
-        scratch_shapes=[
-            pltpu.VMEM((2 * steps,) + values.shape, values.dtype),
-            pltpu.SemaphoreType.DMA((steps,)),
-            pltpu.SemaphoreType.DMA((steps,)),
-        ],
-        compiler_params=pltpu.CompilerParams(collective_id=7, has_side_effects=True),
-        name="sum_all",
-    )(values)
-
-
 class Place:
     def __init__(self):
         self.seq, self.tp = lax.axis_index("seq"), lax.axis_index("tp")
@@ -500,78 +431,64 @@
     return remote(src.at[other], dst.at[me], send.at[k], recv.at[k], (other // 2, lax.rem(other, 2)))
 
 
-def reduce_ticks(place, chunks, near, far, out, xbuf, xsum, zbuf, ybuf, ysum, sems):
-    rows = near.shape[0] // chunks
+def rows_at(start, size):
+    return pl.ds(pl.multiple_of(start, size), size)
+
+
+def reduce_stages(place, chunks, base, out, sib, xbuf, xsum, zbuf, sems, arrived):
+    rows = base.shape[0] // chunks
     half, piece = rows // 2, rows // 8
     x, z = place.x, place.z
 
-    def at(start, size):
-        return pl.ds(pl.multiple_of(start, size), size)
-
-    def tp_copy(k):
+    def x_copy(k):
         return remote(
-            far.at[at(k * rows, rows)], ybuf.at[at(k * rows, rows)],
-            sems["ys"].at[k], sems["yr"].at[k], place.tp_partner,
-        )
-
-    def x_copy(k):
-        src = ysum if far is not None else near
-        return remote(
-            src.at[at(k * rows + (1 - x) * half, half)], xbuf.at[at(k * half, half)],
+            base.at[rows_at(k * rows + (1 - x) * half, half)], xbuf.at[rows_at(k * half, half)],
             sems["xs"].at[k], sems["xr"].at[k], place.x_partner,
         )
 
     def z_copy(k, d):
         return remote(
-            xsum.at[at(k * half + (z ^ d) * piece, piece)], zbuf.at[d - 1, at(k * piece, piece)],
+            xsum.at[rows_at(k * half + (z ^ d) * piece, piece)],
+            zbuf.at[d - 1, rows_at(k * piece, piece)],
             sems["zs"].at[d - 1, k], sems["zr"].at[d - 1, k], place.z_partners[d - 1],
         )
 
     def own_piece(k):
-        return at(k * rows + x * half + z * piece, piece)
+        return rows_at(k * rows + x * half + z * piece, piece)
 
     def zg_copy(k, d):
         return remote(
-            out.at[0, own_piece(k)], out.at[0, own_piece(k)],
+            out.at[own_piece(k)], out.at[own_piece(k)],
             sems["zgs"].at[d - 1, k], sems["zgr"].at[d - 1, k], place.z_partners[d - 1],
         )
 
     def xg_copy(k):
-        span = at(k * rows + x * half, half)
-        return remote(
-            out.at[0, span], out.at[0, span], sems["xgs"].at[k], sems["xgr"].at[k], place.x_partner
-        )
+        span = rows_at(k * rows + x * half, half)
+        return remote(out.at[span], out.at[span], sems["xgs"].at[k], sems["xgr"].at[k], place.x_partner)
 
     def core_copy(k):
-        span = at(k * rows, rows)
-        return remote(
-            out.at[0, span], out.at[1, span], sems["cs"].at[k], sems["cr"].at[k], place.core_partner
-        )
-
-    def stage_tp(k):
-        tp_copy(k).start()
+        span = rows_at(k * rows, rows)
+        return remote(out.at[span], sib.at[span], sems["cs"].at[k], sems["cr"].at[k], place.core_partner)
 
     def stage_x(k):
-        if far is not None:
-            tp_copy(k).wait_recv()
-            span = at(k * rows, rows)
-            ysum[span, :] = (near[span, :].astype(F32) + ybuf[span, :].astype(F32)).astype(BF16)
+        arrived(k)
         x_copy(k).start()
 
     def stage_z(k):
         x_copy(k).wait_recv()
-        src = ysum if far is not None else near
-        mine = src[at(k * rows + x * half, half), :].astype(F32)
-        xsum[at(k * half, half), :] = (mine + xbuf[at(k * half, half), :].astype(F32)).astype(BF16)
+        mine = base[rows_at(k * rows + x * half, half), :].astype(F32)
+        xsum[rows_at(k * half, half), :] = (
+            mine + xbuf[rows_at(k * half, half), :].astype(F32)
+        ).astype(BF16)
         for d in (3, 2, 1):
             z_copy(k, d).start()
 
     def stage_zg(k):
-        total = xsum[at(k * half + z * piece, piece), :].astype(F32)
+        total = xsum[rows_at(k * half + z * piece, piece), :].astype(F32)
         for d in (1, 2, 3):
             z_copy(k, d).wait_recv()
-            total = total + zbuf[d - 1, at(k * piece, piece), :].astype(F32)
-        out[0, own_piece(k), :] = total.astype(BF16)
+            total = total + zbuf[d - 1, rows_at(k * piece, piece), :].astype(F32)
+        out[own_piece(k), :] = total.astype(BF16)
         for d in (3, 2, 1):
             zg_copy(k, d).start()
 
@@ -585,21 +502,14 @@
         core_copy(k).start()
 
     stages = [stage_x, stage_z, stage_zg, stage_xg, stage_core]
-    if far is not None:
-        stages.insert(0, stage_tp)
-
-    def tick(t, carry):
+
+    def tick(t):
         for s, stage in reversed(list(enumerate(stages))):
             @pl.when((t >= s) & (t - s < chunks))
             def _():
                 stage(t - s)
-        return carry
-
-    lax.fori_loop(0, chunks + len(stages) - 1, tick, 0)
 
     def drain(k, carry):
-        if far is not None:
-            tp_copy(k).wait_send()
         x_copy(k).wait_send()
         for d in (1, 2, 3):
             z_copy(k, d).wait_send()
@@ -608,93 +518,233 @@
         core_copy(k).wait()
         return carry
 
-    lax.fori_loop(0, chunks, drain, 0)
-
-
-SEM_NAMES = ("xs", "xr", "zs", "zr", "zgs", "zgr", "xgs", "xgr", "cs", "cr", "ys", "yr")
-
-
-def reduce_scratch(rows, cols, chunks, with_tp):
-    spaces = [
-        pltpu.VMEM((rows // 2, cols), BF16),
-        pltpu.VMEM((rows // 2, cols), BF16),
-        pltpu.VMEM((3, rows // 8, cols), BF16),
-    ]
-    if with_tp:
-        spaces += [pltpu.VMEM((rows, cols), BF16)] * 2
-    names = SEM_NAMES if with_tp else SEM_NAMES[:-2]
-    for name in names:
-        spaces.append(pltpu.SemaphoreType.DMA((3, chunks) if name[0] == "z" else (chunks,)))
-    return spaces
-
-
-def send_back_kernel(chunks, dq_ref, dkv_ref, near, dq_out, dkv_out, out, xbuf, xsum, zbuf, *rest):
+    return tick, lambda: lax.fori_loop(0, chunks, drain, 0), chunks + len(stages) - 1
+
+
+SEM_NAMES = ("xs", "xr", "zs", "zr", "zgs", "zgr", "xgs", "xgr", "cs", "cr")
+VECTOR_STEPS = 5
+
+
+def finish_kernel(
+    chunks, first_ticks, gain_ref, dq_ref, dkv_ref, near_ref, normed_ref, normed_sib_ref, x_ref, dh_ref,
+    w0, w1, w2, w3, vec_ref, out, sib, gx_ref, vec_out,
+    base, far, ybuf, xbuf, xsum, zbuf, dq_in, dkv_in, mixed, mixed_sib, normed, normed_sib, x_s, dh_s, w_s, slots,
+    *rest,
+):
     place = Place()
     count = dq_ref.shape[0]
     me = place.seq * 2 + place.tp
-    names = SEM_NAMES[:-2]
-    sems = dict(zip(names, rest))
-    qs, qr, ks, kr = rest[len(names) :]
+    who = (place.tp, lax.rem(place.seq, 2))
+    sems = dict(zip(SEM_NAMES, rest))
+    qs, qr, ks, kr, ys, yr, ms, mr, vs, vr, loc = rest[len(SEM_NAMES) :]
+    early = near_ref.shape[0]
+    rows = base.shape[0] // chunks
+    settled = early // rows
     greet_all(count, me, place.seq, place.tp)
 
+    near_copy = pltpu.make_async_copy(near_ref, base.at[pl.ds(0, early)], loc.at[0])
+    near_copy.start()
+
     def start(k, carry):
-        chunk_copy(count, me, k, dkv_ref, dkv_out, ks, kr).start()
-        chunk_copy(count, me, k, dq_ref, dq_out, qs, qr).start()
+        chunk_copy(count, me, k, dkv_ref, dkv_in, ks, kr).start()
+        chunk_copy(count, me, k, dq_ref, dq_in, qs, qr).start()
         return carry
 
     lax.fori_loop(1, count, start, 0)
-    dq_out[me] = dq_ref[me]
-    dkv_out[me] = dkv_ref[me]
-    reduce_ticks(place, chunks, near, None, out, xbuf, xsum, zbuf, None, None, sems)
+    locals_ = [
+        pltpu.make_async_copy(src, dst, loc.at[1 + i])
+        for i, (src, dst) in enumerate(
+            [
+                (dq_ref.at[me], dq_in.at[me]),
+                (dkv_ref.at[me], dkv_in.at[me]),
+                (normed_ref, normed),
+                (normed_sib_ref, normed_sib),
+                (x_ref, x_s),
+                (dh_ref, dh_s),
+            ]
+            + [(w, w_s.at[r]) for r, w in enumerate((w0, w1, w2, w3))]
+        )
+    ]
+    near_copy.wait()
+    for copy in locals_:
+        copy.start()
+
+    def tp_copy(k):
+        span = rows_at(k * rows, rows)
+        return remote(far.at[span], ybuf.at[span], ys.at[k], yr.at[k], place.tp_partner)
+
+    def arrived(k):
+        @pl.when(k >= settled)
+        def _():
+            late = k - settled
+            tp_copy(late).wait_recv()
+            span = rows_at(k * rows, rows)
+            base[span, :] = (
+                base[span, :].astype(F32) + ybuf[rows_at(late * rows, rows), :].astype(F32)
+            ).astype(BF16)
+
+    tick, drain, ticks = reduce_stages(place, chunks, base, out, sib, xbuf, xsum, zbuf, sems, arrived)
+
+    def plain(t, carry):
+        tick(t)
+        return carry
+
+    lax.fori_loop(0, first_ticks, plain, 0)
 
     def wait(k, carry):
-        chunk_copy(count, me, k, dkv_ref, dkv_out, ks, kr).wait()
-        chunk_copy(count, me, k, dq_ref, dq_out, qs, qr).wait()
+        chunk_copy(count, me, k, dkv_ref, dkv_in, ks, kr).wait()
+        chunk_copy(count, me, k, dq_ref, dq_in, qs, qr).wait()
         return carry
 
     lax.fori_loop(1, count, wait, 0)
-
-
-def send_back(dq_chunks, dkv_chunks, near, chunks):
-    rows, cols = near.shape
+    for copy in locals_:
+        copy.wait()
+    vec_out[...] = vec_ref[...]
+    low = low_lanes(HALF)
+    for quarter in range(4):
+        load_packed(who, quarter, dq_in, mixed.at[quarter], 0)
+        for pair in range(2):
+            for half in range(2):
+                span = slice(half * HALF, half * HALF + HALF)
+                even = dkv_in[chunk_of(who, quarter, 2 * pair, half)].astype(F32)
+                odd = dkv_in[chunk_of(who, quarter, 2 * pair + 1, half)].astype(F32)
+                k_at = 256 + pair * 128
+                mixed[quarter, span, k_at : k_at + 128] = jnp.where(low, even, swap_lanes(odd)).astype(BF16)
+                mixed[quarter, span, k_at + 256 : k_at + 384] = jnp.where(low, swap_lanes(even), odd).astype(BF16)
+    mixed_copies = [
+        remote(mixed.at[2 * i + 1], mixed_sib.at[i], ms.at[i], mr.at[i], place.core_partner)
+        for i in range(2)
+    ]
+    for copy in mixed_copies:
+        copy.start()
+    tick(first_ticks)
+
+    for quarter in range(4):
+        absolute = (who[0] * 2 + who[1]) ^ quarter
+        lanes = pl.ds(pl.multiple_of(absolute * 256, 256), 256)
+        for row, col in ((10, 0), (11, 512)):
+            vec_out[row : row + 1, lanes] = jnp.sum(
+                mixed[quarter, :, col : col + 256].astype(F32), axis=0, keepdims=True
+            )
+    gains = jnp.zeros((1, base.shape[1]), F32)
+    shifts = jnp.zeros((1, base.shape[1]), F32)
+    for part in range(2):
+        span = slice(part * HALF, part * HALF + HALF)
+        d_normed = jnp.zeros((HALF, base.shape[1]), F32)
+        for quarter in range(4):
+            d_normed += lax.dot_general(
+                mixed[quarter, span, :], w_s[quarter], (((1,), (1,)), ((), ())), preferred_element_type=F32
+            )
+        xhat, rstd = norm_parts(x_s[span, :].astype(F32))
+        e = d_normed * gain_ref[...]
+        grad = rstd * (
+            e
+            - jnp.mean(e, axis=-1, keepdims=True)
+            - xhat * jnp.mean(e * xhat, axis=-1, keepdims=True)
+        )
+        gx_ref[span, :] = dh_s[span, :] + grad
+        gains += jnp.sum(d_normed * xhat, axis=0, keepdims=True)
+        shifts += jnp.sum(d_normed, axis=0, keepdims=True)
+        tick(first_ticks + 1 + part)
+    vec_out[0:1, :] = gains
+    vec_out[4:5, :] = shifts
+
+    for copy in mixed_copies:
+        copy.wait()
+    late = pl.ds(early, base.shape[0] - early)
+    for i, target in ((1, far), (0, base.at[late])):
+        for col in range(0, target.shape[0], 256):
+            span = slice(col, col + 256)
+            target[span, :] = (
+                lax.dot_general(
+                    mixed[2 * i, :, span], normed[...], (((0,), (0,)), ((), ())), preferred_element_type=F32
+                )
+                + lax.dot_general(
+                    mixed_sib[i, :, span], normed_sib[...], (((0,), (0,)), ((), ())),
+                    preferred_element_type=F32,
+                )
+            ).astype(BF16)
+            if i == 1:
+                tp_copy(col // rows).start()
+
+    partners = [place.core_partner, place.tp_partner, place.x_partner] + [
+        (place.seq ^ bit, place.tp) for bit in (4, 8)
+    ]
+
+    def vector_step(step):
+        slots[step] = vec_out[...]
+        copy = remote(
+            slots.at[step], slots.at[VECTOR_STEPS + step], vs.at[step], vr.at[step], partners[step]
+        )
+        copy.start()
+        copy.wait()
+        vec_out[...] += slots[VECTOR_STEPS + step]
+
+    def last(t, carry):
+        tick(t)
+        for step in range(VECTOR_STEPS):
+            @pl.when(t == first_ticks + 3 + step)
+            def _():
+                vector_step(step)
+        return carry
+
+    lax.fori_loop(first_ticks + 3, ticks, last, 0)
+
+    def sent(k, carry):
+        tp_copy(k).wait_send()
+        return carry
+
+    lax.fori_loop(0, chunks - settled, sent, 0)
+    drain()
+
+
+def finish(gain, dq_chunks, dkv_chunks, near, normed, normed_sib, x, d_hidden, weights, vectors):
+    early, cols = near.shape
+    late = weights[0].shape[1]
+    total = early + late
+    chunks = total // CHUNK_ROWS
+    late_chunks = late // CHUNK_ROWS
     count = dq_chunks.shape[0]
+    rows = x.shape[0]
+    dma = pltpu.SemaphoreType.DMA
+    anywhere = pl.BlockSpec(memory_space=pl.ANY)
+    scratch = [
+        pltpu.VMEM((total, cols), BF16),
+        pltpu.VMEM((late, cols), BF16),
+        pltpu.VMEM((late, cols), BF16),
+        pltpu.VMEM((total // 2, cols), BF16),
+        pltpu.VMEM((total // 2, cols), BF16),
+        pltpu.VMEM((3, total // 8, cols), BF16),
+        pltpu.VMEM(dq_chunks.shape, BF16),
+        pltpu.VMEM(dkv_chunks.shape, BF16),
+        pltpu.VMEM((4, rows, late), BF16),
+        pltpu.VMEM((2, rows, late), BF16),
+        pltpu.VMEM((rows, cols), BF16),
+        pltpu.VMEM((rows, cols), BF16),
+        pltpu.VMEM((rows, cols), BF16),
+        pltpu.VMEM((rows, cols), F32),
+        pltpu.VMEM((4,) + weights[0].shape, BF16),
+        pltpu.VMEM((2 * VECTOR_STEPS,) + vectors.shape, F32),
+    ]
+    scratch += [dma((3, chunks) if name[0] == "z" else (chunks,)) for name in SEM_NAMES]
+    scratch += [dma((count,))] * 4 + [dma((late_chunks,))] * 2 + [dma((2,))] * 2
+    scratch += [dma((VECTOR_STEPS,))] * 2 + [dma((11,))]
     return pl.pallas_call(
-        functools.partial(send_back_kernel, chunks),
+        functools.partial(finish_kernel, chunks, FIRST_TICKS),
         out_shape=(
-            jax.ShapeDtypeStruct(dq_chunks.shape, BF16),
-            jax.ShapeDtypeStruct(dkv_chunks.shape, BF16),
-            jax.ShapeDtypeStruct((2, rows, cols), BF16),
+            jax.ShapeDtypeStruct((total, cols), BF16),
+            jax.ShapeDtypeStruct((total, cols), BF16),
+            jax.ShapeDtypeStruct((rows, cols), F32),
+            jax.ShapeDtypeStruct(vectors.shape, F32),
         ),
-        in_specs=vmem(3),
-        out_specs=tuple(vmem(3)),
-        scratch_shapes=reduce_scratch(rows, cols, chunks, False)
-        + [pltpu.SemaphoreType.DMA((count,))] * 4,
+        in_specs=vmem(1) + [anywhere] * 11 + vmem(1),
+        out_specs=(vmem(1)[0], anywhere, vmem(1)[0], vmem(1)[0]),
+        scratch_shapes=scratch,
         compiler_params=pltpu.CompilerParams(
             collective_id=1, has_side_effects=True, vmem_limit_bytes=VMEM_LIMIT
         ),
-        name="send_back",
-    )(dq_chunks, dkv_chunks, near)
-
-
-def reduce_last_kernel(chunks, near, far, out, xbuf, xsum, zbuf, ybuf, ysum, *rest):
-    place = Place()
-    greet([place.tp_partner, place.x_partner, place.core_partner] + place.z_partners)
-    reduce_ticks(place, chunks, near, far, out, xbuf, xsum, zbuf, ybuf, ysum, dict(zip(SEM_NAMES, rest)))
-
-
-def reduce_last(near, far, chunks):
-    rows, cols = near.shape
-    return pl.pallas_call(
-        functools.partial(reduce_last_kernel, chunks),
-        out_shape=jax.ShapeDtypeStruct((2, rows, cols), BF16),
-        in_specs=vmem(2),
-        out_specs=vmem(1)[0],
-        scratch_shapes=reduce_scratch(rows, cols, chunks, True),
-        compiler_params=pltpu.CompilerParams(
-            collective_id=2, has_side_effects=True, vmem_limit_bytes=VMEM_LIMIT
-        ),
-        name="reduce_last",
-    )(near, far)
+        name="finish",
+    )(gain, dq_chunks, dkv_chunks, near, normed, normed_sib, x, d_hidden, *weights, vectors)
 
 
 def norm_parts(values):
@@ -833,21 +883,6 @@
     )
     dkv_chunks = (dkv_mine + to_sib(dkv_theirs).astype(F32)).astype(BF16)
     near_all = jnp.concatenate([g_down, reduced(near_up, far_up), reduced(near_out, far_out)])
-    dq_home, dkv_home, sums = send_back(dq_chunks, dkv_chunks, near_all, CHUNKS)
-    d_q, d_k, d_v = unpack_qkv(who, dq_home, dkv_home)
-
-    mixed4 = [
-        jnp.concatenate([cols(d, r, 256) for d in (d_q, d_k, d_v)], axis=1) for r in range(4)
-    ]
-    mixed_sib = [to_sib(mixed4[r]) for r in (1, 3)]
-    near_qkv, far_qkv = (
-        dot_rows(normed, mixed4[r]) + dot_rows(normed_sib, s) for r, s in zip((0, 2), mixed_sib)
-    )
-    far_qkv = far_qkv.astype(BF16)
-    mixed4 = tie(mixed4, far_qkv)
-    d_normed = sum(dot_t(mixed4[r], wq4[r]) for r in range(4))
-    d_first, gain_first, shift_first = norm_back(input_f32, norm_gains[0], d_normed)
-    grad_x = d_hidden + d_first
 
     def joined(pair, axis):
         own, sib = pair
@@ -861,20 +896,26 @@
             [sum(jnp.where((base ^ r) == a, parts[r], 0.0) for r in range(4)) for a in range(4)]
         )
 
-    bias_q_part = [jnp.sum(cols(d_q, r, 256).astype(F32), axis=0) for r in range(4)]
-    bias_v_part = [jnp.sum(cols(d_v, r, 256).astype(F32), axis=0) for r in range(4)]
+    blank = jnp.zeros_like(gain_last)
     vectors = jnp.stack(
-        [gain_first, gain_second, gain_third, gain_last]
-        + [shift_first, shift_second, shift_third, shift_last]
-        + [bias_out_part, bias_down_part, absolute(bias_q_part), absolute(bias_v_part)]
+        [blank, gain_second, gain_third, gain_last]
+        + [blank, shift_second, shift_third, shift_last]
+        + [bias_out_part, bias_down_part, blank, blank]
     )
     vectors = jnp.concatenate([vectors, absolute(bias_up_part).reshape(4, -1)])
-    vectors = sum_all(vectors, seq_count)
-    near_qkv, vectors = tie((near_qkv.astype(BF16), vectors), vectors)
-    sums_qkv = reduce_last(near_qkv, far_qkv, CHUNKS_LAST).reshape(2, width, 3, -1)
+    sums, sums_sib, grad_x, vectors = finish(
+        norm_gains[:1], dq_chunks, dkv_chunks, near_all, normed, normed_sib, tokens_in, d_hidden, wq4, vectors
+    )
+    pair = (sums, sums_sib)
     hidden_rows = g_down.shape[0]
-    up_rows = slice(hidden_rows, hidden_rows + width)
-    out_rows = slice(hidden_rows + width, None)
+    up_end = hidden_rows + width
+    out_end = near_all.shape[0]
+
+    def rows_of(start, stop):
+        return [part[start:stop] for part in pair]
+
+    g_qkv = joined([part.reshape(3, -1, width) for part in rows_of(out_end, None)], 1)
+    g_qkv = jnp.transpose(g_qkv, (2, 0, 1))
     own_cols = bias_qv.shape[1]
     grad_bias_qv = lax.dynamic_slice_in_dim(vectors[10:12], tp * own_cols, own_cols, 1)
     grad_bias_up = lax.dynamic_slice_in_dim(
@@ -883,13 +924,13 @@
     return (
         result,
         grad_x,
-        joined(sums_qkv, 2),
+        g_qkv,
         grad_bias_qv,
-        joined(sums[:, out_rows], 0),
+        joined(rows_of(up_end, out_end), 0),
         vectors[8],
-        joined(sums[:, up_rows], 1),
+        joined(rows_of(hidden_rows, up_end), 1),
         grad_bias_up,
-        joined(sums[:, :hidden_rows], 0),
+        joined(rows_of(0, hidden_rows), 0),
         vectors[9],
         vectors[0:4],
         vectors[4:8],

time: 845 us -> 756 us (0.89)
  Pallas kernels: 429 us -> 357 us
  matrix products: 108 us -> 88.5 us
  starting transfers between devices: 29.7 us -> 38.3 us
    pallas_call x4 -> x1, Pallas kernels: 298 us -> 238 us  [finish(): pl.pallas_call(functools.partial(finish_kernel, chunks, FIRST_TICKS), out...]
    another operation x5 -> x1, local copies, waits for them, and re-layouts: 14.2 us -> 0.01 us  [joined(): own, sib = pair]
    slice x0 -> x6, local copies, waits for them, and re-layouts: none -> 13.1 us  [rows_of(): return [part[start:stop] for part in pair]]
    dot_general x12 -> x8, matrix products: 38 us -> 27.6 us  [dot_t(): lax.dot_general(a, b, (((1,), (1,)), ((), ())), preferred_element_type=F32)]
    dot_general x16 -> x12, matrix products: 40.5 us -> 31.4 us  [dot_rows(): lax.dot_general(a, b, (((0,), (0,)), ((), ())), preferred_element_type=F32)]
  transfers between devices with their start and end apart: 30 -> 28, of which waited for: 6 -> 6; matrix products, arithmetic and copies ran while one was open for 17% -> 15% of each run, Pallas kernels for 39% -> 15%
where the time goes in v3:
time: 756 us; the launch traced here: 748 us
  Pallas kernels  357 us (47%)
  waiting for transfers between devices  117 us (15%)
  matrix products  88.5 us (12%)
  local copies, waits for them, and re-layouts  53.8 us (7%)
  blocking collectives  53.6 us (7%)
  starting transfers between devices  38.3 us (5%)
  other arithmetic  37.5 us (5%)
    pallas_call x1, Pallas kernels, finish(): pl.pallas_call(functools.partial(finish_kernel, chunks, FIRST_TICKS), out...  238 us
    ppermute x8, waiting for transfers between devices, to_tp(): return lax.ppermute(values, 'tp', over_tp)  99.5 us
    pallas_call x1, Pallas kernels, attend_back(): pl.pallas_call(attend_back_kernel, out_shape=(jax.ShapeDtypeStruct((block...  55.5 us
    all_to_all x1, blocking collectives, exchange(): return lax.all_to_all(chunks, ('seq', 'tp'), 0, 0, tiled=True)  53.6 us
    pallas_call x1, Pallas kernels, attend(): pl.pallas_call(attend_kernel, out_shape=(jax.ShapeDtypeStruct((blocks, QU...  48.5 us
    dot_general x12, matrix products, dot_rows(): lax.dot_general(a, b, (((0,), (0,)), ((), ())), preferred_element_type=F32)  31.4 us
    dot_general x12, matrix products, dot(): return jnp.dot(a, b, preferred_element_type=F32)  29.5 us
    dot_general x8, matrix products, dot_t(): lax.dot_general(a, b, (((1,), (1,)), ((), ())), preferred_element_type=F32)  27.6 us
  transfers between devices with their start and end apart: 28, of which 6 were waited for; matrix products, arithmetic and copies ran while one was open for 15% of the time, Pallas kernels for 15%

profile of v3, /device:TPU:0, one launch (start us, length us, event | category | flops | bytes accessed | tf_op | source)
XLA Modules:
  0.0 747.8 jit_solution(12198482330587539785)
XLA Ops:
  8.7 34.5 %collective-permute-done.2 = bf16[1024,3,256]{0,2,1:T(8,128)(2,1)} collective-permute-done((bf16[1024,3,256]{0,2,1:T(8,128)(2,1)S(1)}, bf16[1024,3,256]{0,2,1:T(8,128)(2,1)}, u32[]{:S(2)}, u32[]{:S(2)}) %collective-permute-start.2) | collective-permute-done | bytes 1572896 | tf_op jit(solution)/shard_map/ppermute | solution.py:780
  57.3 8.7 %project.1 = (bf16[512,1024]{1,0:T(8,128)(2,1)}, bf16[32,128,128]{2,1,0:T(8,128)(2,1)}, bf16[32,256,128]{2,1,0:T(8,128)(2,1)}) custom-call(s32[2]{0:T(128)} %pad_add_fusion.who_ref, bf16[512,1024]{1,0:T(8,128)(2,1)} %x_ref.3, f32[1,1024]{1,0:T(1,128)} %get-tuple-element.101.gain_ref, f32[1,1024]{1,0:T(1,128)} %get-tuple-element.121.shift_ref, ...), custom_call_target="tpu_custom_call" | custom-call | tf_op jit(solution)/shard_map/project/pallas_call | solution.py:339
  66.0 53.6 %all_to_all.20.own_ref = bf16[32,256,128]{2,1,0:T(8,128)(2,1)S(1)} all-to-all(bf16[32,256,128]{2,1,0:T(8,128)(2,1)} %get-tuple-element.33), channel_id=1, replica_groups=mesh['seq'=16,'tp'=2] {'seq','tp'}, dimensions={0} | all-to-all | bytes 4194304 | tf_op jit(solution)/shard_map/all_to_all | solution.py:786
  119.7 3.8 all-to-all-start
  133.1 16.6 %all-to-all-done.q_ref = bf16[32,128,128]{2,1,0:T(8,128)(2,1)S(1)} async-done(((bf16[32,128,128]{2,1,0:T(8,128)(2,1)}), bf16[32,128,128]{2,1,0:T(8,128)(2,1)S(1)}, u32[]{:S(2)}, u32[]{:S(2)}) %all-to-all-start) | async-done | bytes 1048608 | tf_op jit(solution)/shard_map/all_to_all | solution.py:786
  150.6 48.5 %attend.1 = (bf16[32,128,128]{2,1,0:T(8,128)(2,1)}, f32[32,64,256]{2,1,0:T(8,128)}, f32[32,1,256]{2,1,0:T(1,128)}, bf16[17408,128]{1,0:T(8,128)(2,1)}, bf16[128,17408]{1,0:T(8,128)(2,1)}) custom-call(s32[1]{0:T(128)} %bitcast.1.part_ref, s32[5,32]{1,0:T(8,128)} %stack.56.tab, s32[32,1,256]{2,1,0:T(1,128)} %broadcast_in_dim.84.low_ref, ...), custom_call_target="tpu_custom_call" | custom-call | flops 40000000000 | bytes 20971520 | tf_op jit(solution)/shard_map/attend/pallas_call | solution.py:227
  199.2 8.1 %all-to-all-start.2 = ((bf16[32,128,128]{2,1,0:T(8,128)(2,1)}), bf16[32,128,128]{2,1,0:T(8,128)(2,1)S(1)}, u32[]{:S(2)}, u32[]{:S(2)}) async-start(bf16[32,128,128]{2,1,0:T(8,128)(2,1)} %get-tuple-element.34), calls=%async_computation.2 | async-start | bytes 2097152 | tf_op jit(solution)/shard_map/all_to_all | solution.py:786
  209.4 40.5 %collective-permute-done.5.w2 = bf16[256,1024]{1,0:T(8,128)(2,1)S(1)} collective-permute-done((bf16[256,1024]{1,0:T(8,128)(2,1)S(1)}, bf16[256,1024]{1,0:T(8,128)(2,1)S(1)}, u32[]{:S(2)}, u32[]{:S(2)}) %collective-permute-start.5) | collective-permute-done | bytes 524320 | tf_op jit(solution)/shard_map/ppermute | solution.py:780
  261.9 4.0 multiply_convert_fusion.2
  274.8 3.6 multiply_convert_fusion
  281.6 3.5 fusion.65
  292.9 4.0 fusion.6
  300.3 3.5 fusion.13
  303.8 4.0 fusion.27
  308.5 3.6 fusion.62
  312.1 4.0 fusion.20
  328.8 3.8 multiply_reduce_fusion.1
  338.5 4.3 spread.1
  342.8 5.0 all-to-all-start.3
  352.8 4.3 add_convert_fusion.3
  362.1 15.4 %collective-permute-done.18 = bf16[1024,1024]{1,0:T(8,128)(2,1)} collective-permute-done((bf16[1024,1024]{1,0:T(8,128)(2,1)}, bf16[1024,1024]{1,0:T(8,128)(2,1)}, u32[]{:S(2)}, u32[]{:S(2)}) %collective-permute-start.18) | collective-permute-done | bytes 2097184 | tf_op jit(solution)/shard_map/ppermute | solution.py:780
  377.5 4.7 add_convert_fusion.2
  382.2 55.5 %attend_back.1 = (bf16[32,128,128]{2,1,0:T(8,128)(2,1)}, f32[32,256,128]{2,1,0:T(8,128)}, bf16[32,256,128]{2,1,0:T(8,128)(2,1)}) custom-call(s32[1]{0:T(128)} %bitcast.1.part_ref, s32[5,32]{1,0:T(8,128)} %stack.56.tab, s32[32,1,256]{2,1,0:T(1,128)} %broadcast_in_dim.84.low_ref, s32[32,1,256]{2,1,0:T(1,128)} %maximum_minimum_fusion.high_ref, ...), custom_call_target="tpu_custom_call" | custom-call | flops 60000002048 | bytes 31457280 | tf_op jit(solution)/shard_map/attend_back/pallas_call | solution.py:250
  437.7 4.9 collective-permute-start.19
  448.9 9.1 %collective-permute-done.23 = bf16[256,1024]{1,0:T(8,128)(2,1)S(1)} collective-permute-done((bf16[256,1024]{1,0:T(8,128)(2,1)}, bf16[256,1024]{1,0:T(8,128)(2,1)S(1)}, u32[]{:S(2)}, u32[]{:S(2)}) %collective-permute-start.23) | collective-permute-done | bytes 524320 | tf_op jit(solution)/shard_map/ppermute | solution.py:780
  459.9 3.8 add_convert_fusion
  467.6 3.6 add_convert_fusion.1.dkv_ref
  472.2 237.6 %finish.1 = (bf16[3072,1024]{1,0:T(8,128)(2,1)}, bf16[3072,1024]{1,0:T(8,128)(2,1)}, f32[512,1024]{1,0:T(8,128)}, f32[16,1024]{1,0:T(8,128)}) custom-call(f32[1,1024]{1,0:T(1,128)} %get-tuple-element.101.gain_ref, bf16[32,128,128]{2,1,0:T(8,128)(2,1)} %get-tuple-element.44.dq_ref, bf16[32,256,128]{2,1,0:T(8,128)(2,1)} %add_convert_fusion.1.dkv_ref, ...), custom_call_target="tpu_custom_call" | custom-call | tf_op jit(solution)/shard_map/finish/pallas_call | solution.py:732
  717.1 4.0 fusion.72
  729.9 5.2 select_bitcast_fusion
  737.1 4.2 convert_select_fusion.1
  741.9 4.4 convert_select_fusion
  (248 shorter events, 131.8 us)
Async XLA Ops:
  3.9 41.2 %copy-start.35 = (f32[4,1024]{1,0:T(4,128)S(1)}, f32[4,1024]{1,0:T(4,128)}, u32[]{:S(2)}) copy-start(f32[4,1024]{1,0:T(4,128)} %param.25) | copy-start | bytes 49156
  5.7 37.5 %collective-permute-start.2 = (bf16[1024,3,256]{0,2,1:T(8,128)(2,1)S(1)}, bf16[1024,3,256]{0,2,1:T(8,128)(2,1)}, u32[]{:S(2)}, u32[]{:S(2)}) collective-permute-start(bf16[1024,3,256]{0,2,1:T(8,128)(2,1)S(1)} %copy.68), channel_id=1, source_target_pairs={{0,1},{1,0},{2,3},{3,2},{4,5},{5,4},{6,7},{7,6},{8,9},{9,8},{10,11... | collective-permute-start | bytes 4718600 | tf_op jit(solution)/shard_map/ppermute | solution.py:780
  43.2 11.5 %collective-permute-start.3 = (bf16[1024,3,256]{0,2,1:T(8,128)(2,1)}, bf16[1024,3,256]{0,2,1:T(8,128)(2,1)}, u32[]{:S(2)}, u32[]{:S(2)}) collective-permute-start(bf16[1024,3,256]{0,2,1:T(8,128)(2,1)} %collective-permute-done.2), channel_id=1, source_target_pairs={{0,2},{2,0},{4,6},{6,4},{8,10},{10,8},{12,14},{14,12},{16,18},{18,... | collective-permute-start | bytes 4718600 | tf_op jit(solution)/shard_map/ppermute | solution.py:783
  43.3 7.1 collective-permute-start
  50.3 1.2 collective-permute-start.1
  119.7 30.0 %collective-permute-start.4 = (bf16[32,256,128]{2,1,0:T(8,128)(2,1)S(1)}, bf16[32,256,128]{2,1,0:T(8,128)(2,1)}, u32[]{:S(2)}, u32[]{:S(2)}) collective-permute-start(bf16[32,256,128]{2,1,0:T(8,128)(2,1)S(1)} %all_to_all.20.own_ref), channel_id=1, source_target_pairs={{0,2},{2,0},{4,6},{6,4},{8,10},{10,8},{12,14},{14,12},{16,18},{18,... | collective-permute-start | bytes 6291464 | tf_op jit(solution)/shard_map/ppermute | solution.py:783
  119.7 30.0 %all-to-all-start = ((bf16[32,128,128]{2,1,0:T(8,128)(2,1)}), bf16[32,128,128]{2,1,0:T(8,128)(2,1)S(1)}, u32[]{:S(2)}, u32[]{:S(2)}) async-start(bf16[32,128,128]{2,1,0:T(8,128)(2,1)} %get-tuple-element.32), calls=%async_computation | async-start | bytes 2097152 | tf_op jit(solution)/shard_map/all_to_all | solution.py:786
  126.8 123.2 %collective-permute-start.7 = (bf16[1024,1024]{1,0:T(8,128)(2,1)}, bf16[1024,1024]{1,0:T(8,128)(2,1)}, u32[]{:S(2)}, u32[]{:S(2)}) collective-permute-start(bf16[1024,1024]{1,0:T(8,128)(2,1)} %constant_dynamic-slice_fusion.2), channel_id=1, source_target_pairs={{0,1},{1,0},{2,3},{3,2},{4,5},{5,4},{6,7},{7,6},{8,9},{9,8},{10,11... | collective-permute-start | bytes 6291464 | tf_op jit(solution)/shard_map/ppermute | solution.py:780
  130.1 120.3 %collective-permute-start.8 = (bf16[1024,1024]{1,0:T(8,128)(2,1)}, bf16[1024,1024]{1,0:T(8,128)(2,1)}, u32[]{:S(2)}, u32[]{:S(2)}) collective-permute-start(bf16[1024,1024]{1,0:T(8,128)(2,1)} %constant_dynamic-slice_fusion.1), channel_id=1, source_target_pairs={{0,1},{1,0},{2,3},{3,2},{4,5},{5,4},{6,7},{7,6},{8,9},{9,8},{10,11... | collective-permute-start | bytes 6291464 | tf_op jit(solution)/shard_map/ppermute | solution.py:780
  199.2 51.3 %all-to-all-start.2 = ((bf16[32,128,128]{2,1,0:T(8,128)(2,1)}), bf16[32,128,128]{2,1,0:T(8,128)(2,1)S(1)}, u32[]{:S(2)}, u32[]{:S(2)}) async-start(bf16[32,128,128]{2,1,0:T(8,128)(2,1)} %get-tuple-element.34), calls=%async_computation.2 | async-start | bytes 2097152 | tf_op jit(solution)/shard_map/all_to_all | solution.py:786
  207.4 48.2 %copy-start.12 = (bf16[256,1024]{1,0:T(8,128)(2,1)}, bf16[256,1024]{1,0:T(8,128)(2,1)S(1)}, u32[]{:S(2)}) copy-start(bf16[256,1024]{1,0:T(8,128)(2,1)S(1)} %get-tuple-element.90.w0) | copy-start | bytes 1572868
  207.4 48.2 %copy-start.11 = (bf16[256,1024]{1,0:T(8,128)(2,1)}, bf16[256,1024]{1,0:T(8,128)(2,1)S(1)}, u32[]{:S(2)}) copy-start(bf16[256,1024]{1,0:T(8,128)(2,1)S(1)} %get-tuple-element.89.w1) | copy-start | bytes 1572868
  207.4 42.5 %collective-permute-start.5 = (bf16[256,1024]{1,0:T(8,128)(2,1)S(1)}, bf16[256,1024]{1,0:T(8,128)(2,1)S(1)}, u32[]{:S(2)}, u32[]{:S(2)}) collective-permute-start(bf16[256,1024]{1,0:T(8,128)(2,1)S(1)} %get-tuple-element.90.w0), channel_id=1, source_target_pairs={{0,1},{1,0},{2,3},{3,2},{4,5},{5,4},{6,7},{7,6},{8,9},{9,8},{10,11... | collective-permute-start | bytes 1572872 | tf_op jit(solution)/shard_map/ppermute | solution.py:780
  249.9 6.6 collective-permute-start.6
  249.9 24.9 %collective-permute-start.9 = (bf16[1024,1024]{1,0:T(8,128)(2,1)}, bf16[1024,1024]{1,0:T(8,128)(2,1)}, u32[]{:S(2)}, u32[]{:S(2)}) collective-permute-start(bf16[1024,1024]{1,0:T(8,128)(2,1)} %collective-permute-done.7), channel_id=1, source_target_pairs={{0,2},{2,0},{4,6},{6,4},{8,10},{10,8},{12,14},{14,12},{16,18},{18,... | collective-permute-start | bytes 6291464 | tf_op jit(solution)/shard_map/ppermute | solution.py:783
  250.4 34.7 %collective-permute-start.10 = (bf16[1024,1024]{1,0:T(8,128)(2,1)}, bf16[1024,1024]{1,0:T(8,128)(2,1)}, u32[]{:S(2)}, u32[]{:S(2)}) collective-permute-start(bf16[1024,1024]{1,0:T(8,128)(2,1)} %collective-permute-done.8), channel_id=1, source_target_pairs={{0,2},{2,0},{4,6},{6,4},{8,10},{10,8},{12,14},{14,12},{16,18},{18,... | collective-permute-start | bytes 6291464 | tf_op jit(solution)/shard_map/ppermute | solution.py:783
  298.5 17.6 %collective-permute-start.11 = (bf16[512,1024]{1,0:T(8,128)(2,1)S(1)}, bf16[512,1024]{1,0:T(8,128)(2,1)S(1)}, u32[]{:S(2)}, u32[]{:S(2)}) collective-permute-start(bf16[512,1024]{1,0:T(8,128)(2,1)S(1)} %get-tuple-element.113), channel_id=1, source_target_pairs={{0,2},{2,0},{4,6},{6,4},{8,10},{10,8},{12,14},{14,12},{16,18},{18,... | collective-permute-start | bytes 3145736 | tf_op jit(solution)/shard_map/ppermute | solution.py:783
  299.0 17.1 %collective-permute-start.12 = (bf16[512,1024]{1,0:T(8,128)(2,1)S(1)}, bf16[512,1024]{1,0:T(8,128)(2,1)S(1)}, u32[]{:S(2)}, u32[]{:S(2)}) collective-permute-start(bf16[512,1024]{1,0:T(8,128)(2,1)S(1)} %get-tuple-element.72), channel_id=1, source_target_pairs={{0,2},{2,0},{4,6},{6,4},{8,10},{10,8},{12,14},{14,12},{16,18},{18,... | collective-permute-start | bytes 3145736 | tf_op jit(solution)/shard_map/ppermute | solution.py:783
  299.1 53.0 %collective-permute-start.13 = (bf16[512,1024]{1,0:T(8,128)(2,1)}, bf16[512,1024]{1,0:T(8,128)(2,1)}, u32[]{:S(2)}, u32[]{:S(2)}) collective-permute-start(bf16[512,1024]{1,0:T(8,128)(2,1)} %add_convert_fusion.6), channel_id=1, source_target_pairs={{0,2},{2,0},{4,6},{6,4},{8,10},{10,8},{12,14},{14,12},{16,18},{18,... | collective-permute-start | bytes 3145736 | tf_op jit(solution)/shard_map/ppermute | solution.py:783
  300.2 61.9 %collective-permute-start.17 = (bf16[512,1024]{1,0:T(8,128)(2,1)}, bf16[512,1024]{1,0:T(8,128)(2,1)}, u32[]{:S(2)}, u32[]{:S(2)}) collective-permute-start(bf16[512,1024]{1,0:T(8,128)(2,1)} %get-tuple-element.111), channel_id=1, source_target_pairs={{0,2},{2,0},{4,6},{6,4},{8,10},{10,8},{12,14},{14,12},{16,18},{18,... | collective-permute-start | bytes 3145736 | tf_op jit(solution)/shard_map/ppermute | solution.py:783
  307.8 44.6 %collective-permute-start.14 = (bf16[512,1024]{1,0:T(8,128)(2,1)S(1)}, bf16[512,1024]{1,0:T(8,128)(2,1)}, u32[]{:S(2)}, u32[]{:S(2)}) collective-permute-start(bf16[512,1024]{1,0:T(8,128)(2,1)S(1)} %fusion.27), channel_id=1, source_target_pairs={{0,2},{2,0},{4,6},{6,4},{8,10},{10,8},{12,14},{14,12},{16,18},{18,... | collective-permute-start | bytes 3145736 | tf_op jit(solution)/shard_map/ppermute | solution.py:783
  318.8 58.6 %collective-permute-start.18 = (bf16[1024,1024]{1,0:T(8,128)(2,1)}, bf16[1024,1024]{1,0:T(8,128)(2,1)}, u32[]{:S(2)}, u32[]{:S(2)}) collective-permute-start(bf16[1024,1024]{1,0:T(8,128)(2,1)} %add_convert_fusion.4), channel_id=1, source_target_pairs={{0,1},{1,0},{2,3},{3,2},{4,5},{5,4},{6,7},{7,6},{8,9},{9,8},{10,11... | collective-permute-start | bytes 6291464 | tf_op jit(solution)/shard_map/ppermute | solution.py:780
  338.4 19.5 %collective-permute-start.16 = (bf16[512,1024]{1,0:T(8,128)(2,1)S(1)}, bf16[512,1024]{1,0:T(8,128)(2,1)}, u32[]{:S(2)}, u32[]{:S(2)}) collective-permute-start(bf16[512,1024]{1,0:T(8,128)(2,1)S(1)} %get-tuple-element.74.d_ref), channel_id=1, source_target_pairs={{0,2},{2,0},{4,6},{6,4},{8,10},{10,8},{12,14},{14,12},{16,18},{18,... | collective-permute-start | bytes 3145736 | tf_op jit(solution)/shard_map/ppermute | solution.py:783
  342.8 39.4 %all-to-all-start.3 = ((bf16[32,128,128]{2,1,0:T(8,128)(2,1)}), bf16[32,128,128]{2,1,0:T(8,128)(2,1)}, u32[]{:S(2)}, u32[]{:S(2)}) async-start(bf16[32,128,128]{2,1,0:T(8,128)(2,1)} %spread.1), calls=%async_computation.3 | async-start | bytes 2097152 | tf_op jit(solution)/shard_map/all_to_all | solution.py:786
  352.1 107.8 %collective-permute-start.20 = (bf16[512,1024]{1,0:T(8,128)(2,1)}, bf16[512,1024]{1,0:T(8,128)(2,1)}, u32[]{:S(2)}, u32[]{:S(2)}) collective-permute-start(bf16[512,1024]{1,0:T(8,128)(2,1)} %fusion.13), channel_id=1, source_target_pairs={{0,2},{2,0},{4,6},{6,4},{8,10},{10,8},{12,14},{14,12},{16,18},{18,... | collective-permute-start | bytes 3145736 | tf_op jit(solution)/shard_map/ppermute | solution.py:783
  352.4 5.1 collective-permute-start.15
  357.5 90.7 %collective-permute-start.22 = (bf16[512,256]{1,0:T(8,128)(2,1)S(1)}, bf16[512,256]{1,0:T(8,128)(2,1)}, u32[]{:S(2)}, u32[]{:S(2)}) collective-permute-start(bf16[512,256]{1,0:T(8,128)(2,1)S(1)} %get-tuple-element.87), channel_id=1, source_target_pairs={{0,2},{2,0},{4,6},{6,4},{8,10},{10,8},{12,14},{14,12},{16,18},{18,... | collective-permute-start | bytes 786440 | tf_op jit(solution)/shard_map/ppermute | solution.py:783
  357.9 102.0 %collective-permute-start.21 = (bf16[1024,1024]{1,0:T(8,128)(2,1)}, bf16[1024,1024]{1,0:T(8,128)(2,1)}, u32[]{:S(2)}, u32[]{:S(2)}) collective-permute-start(bf16[1024,1024]{1,0:T(8,128)(2,1)} %add_convert_fusion.3), channel_id=1, source_target_pairs={{0,1},{1,0},{2,3},{3,2},{4,5},{5,4},{6,7},{7,6},{8,9},{9,8},{10,11... | collective-permute-start | bytes 6291464 | tf_op jit(solution)/shard_map/ppermute | solution.py:780
  382.2 63.0 %copy-start.19 = (bf16[512,1024]{1,0:T(8,128)(2,1)S(1)}, bf16[512,1024]{1,0:T(8,128)(2,1)}, u32[]{:S(2)}) copy-start(bf16[512,1024]{1,0:T(8,128)(2,1)} %copy-done.18) | copy-start | bytes 3145732
  437.7 28.7 %collective-permute-start.19 = (bf16[32,256,128]{2,1,0:T(8,128)(2,1)}, bf16[32,256,128]{2,1,0:T(8,128)(2,1)}, u32[]{:S(2)}, u32[]{:S(2)}) collective-permute-start(bf16[32,256,128]{2,1,0:T(8,128)(2,1)} %get-tuple-element.46), channel_id=1, source_target_pairs={{0,2},{2,0},{4,6},{6,4},{8,10},{10,8},{12,14},{14,12},{16,18},{18,... | collective-permute-start | bytes 6291464 | tf_op jit(solution)/shard_map/ppermute | solution.py:783
  444.0 14.1 %collective-permute-start.23 = (bf16[256,1024]{1,0:T(8,128)(2,1)}, bf16[256,1024]{1,0:T(8,128)(2,1)S(1)}, u32[]{:S(2)}, u32[]{:S(2)}) collective-permute-start(bf16[256,1024]{1,0:T(8,128)(2,1)} %fusion.39), channel_id=1, source_target_pairs={{0,1},{1,0},{2,3},{3,2},{4,5},{5,4},{6,7},{7,6},{8,9},{9,8},{10,11... | collective-permute-start | bytes 1572872 | tf_op jit(solution)/shard_map/ppermute | solution.py:780
  448.9 22.3 %collective-permute-start.24 = (bf16[512,1024]{1,0:T(8,128)(2,1)S(1)}, bf16[512,1024]{1,0:T(8,128)(2,1)S(1)}, u32[]{:S(2)}, u32[]{:S(2)}) collective-permute-start(bf16[512,1024]{1,0:T(8,128)(2,1)S(1)} %copy-done.30), channel_id=1, source_target_pairs={{0,2},{2,0},{4,6},{6,4},{8,10},{10,8},{12,14},{14,12},{16,18},{18,... | collective-permute-start | bytes 3145736 | tf_op jit(solution)/shard_map/ppermute | solution.py:783
  (39 other events, 317.0 us)

commit v4 on v3

--- a/solution.py
+++ b/solution.py
@@ -18,6 +18,7 @@
 CHUNK_ROWS = 256
 FIRST_TICKS = 6
 VMEM_LIMIT = 58 << 20
+VMEM_MIDDLE = 62 << 20
 
 EPS = 1e-05
 F32 = jnp.float32
@@ -310,84 +311,6 @@
             out_ref[top + QUART : top + HALF, lanes] = jnp.where(low, swap_lanes(even), odd).astype(BF16)
 
 
-def project_kernel(who_ref, x_ref, gain_ref, shift_ref, bias_ref, w0, w1, w2, w3, normed_ref, q_ref, kv_ref):
-    who = (who_ref[0], who_ref[1])
-    normed = layer_norm(x_ref[...].astype(F32), gain_ref[...], shift_ref[...]).astype(BF16)
-    normed_ref[...] = normed
-    low = low_lanes(HALF)
-    for quarter, w in enumerate((w0, w1, w2, w3)):
-        def dot(col):
-            return jnp.dot(normed, w[:, col : col + 256], preferred_element_type=F32)
-
-        bias = bias_ref[quarter : quarter + 1, :].astype(F32)
-        store_packed(who, quarter, dot(0) + bias[:, :256], q_ref)
-        keys = dot(256)
-        values = dot(512) + bias[:, 256:]
-        for pair in range(2):
-            lanes = slice(pair * 128, pair * 128 + 128)
-            for half in range(2):
-                rows = slice(half * HALF, half * HALF + HALF)
-                k, v = keys[rows, lanes], values[rows, lanes]
-                even = jnp.where(low, k, swap_lanes(v))
-                odd = jnp.where(low, swap_lanes(k), v)
-                kv_ref[chunk_of(who, quarter, 2 * pair, half)] = even.astype(BF16)
-                kv_ref[chunk_of(who, quarter, 2 * pair + 1, half)] = odd.astype(BF16)
-
-
-def project(who, x, gain, shift, bias, weights):
-    rows, width = x.shape
-    return pl.pallas_call(
-        project_kernel,
-        out_shape=(
-            jax.ShapeDtypeStruct((rows, width), BF16),
-            jax.ShapeDtypeStruct((32, QUART, 2 * HEAD), BF16),
-            jax.ShapeDtypeStruct((32, HALF, 2 * HEAD), BF16),
-        ),
-        in_specs=smem(1) + vmem(8),
-        out_specs=tuple(vmem(3)),
-        compiler_params=pltpu.CompilerParams(vmem_limit_bytes=VMEM_LIMIT),
-        name="project",
-    )(who, x, gain, shift, bias, *weights)
-
-
-def unpack_heads_kernel(who_ref, ref, out_ref):
-    who = (who_ref[0], who_ref[1])
-    for quarter in range(4):
-        load_packed(who, quarter, ref, out_ref, quarter * 256)
-
-
-def unpack_heads(who, chunks):
-    return pl.pallas_call(
-        unpack_heads_kernel,
-        out_shape=jax.ShapeDtypeStruct((BLK, 1024), BF16),
-        in_specs=smem(1) + vmem(1),
-        out_specs=vmem(1)[0],
-        compiler_params=pltpu.CompilerParams(vmem_limit_bytes=VMEM_LIMIT),
-        name="unpack_heads",
-    )(who, chunks)
-
-
-def spread_kernel(who_ref, d_ref, w0, w1, w2, w3, out_ref):
-    who = (who_ref[0], who_ref[1])
-    d_rows = d_ref[...]
-    for quarter, w in enumerate((w0, w1, w2, w3)):
-        values = lax.dot_general(
-            d_rows, w[...], (((1,), (1,)), ((), ())), preferred_element_type=F32
-        )
-        store_packed(who, quarter, values, out_ref)
-
-
-def spread(who, d_branch, weights):
-    return pl.pallas_call(
-        spread_kernel,
-        out_shape=jax.ShapeDtypeStruct((32, QUART, 2 * HEAD), BF16),
-        in_specs=smem(1) + vmem(5),
-        out_specs=vmem(1)[0],
-        compiler_params=pltpu.CompilerParams(vmem_limit_bytes=VMEM_LIMIT),
-        name="spread",
-    )(who, d_branch, *weights)
-
-
 class Place:
     def __init__(self):
         self.seq, self.tp = lax.axis_index("seq"), lax.axis_index("tp")
@@ -526,7 +449,7 @@
 
 
 def finish_kernel(
-    chunks, first_ticks, gain_ref, dq_ref, dkv_ref, near_ref, normed_ref, normed_sib_ref, x_ref, dh_ref,
+    chunks, first_ticks, gain_ref, dq_ref, dkv_ref, near_ref, far_ref, normed_ref, normed_sib_ref, x_ref, dh_ref,
     w0, w1, w2, w3, vec_ref, out, sib, gx_ref, vec_out,
     base, far, ybuf, xbuf, xsum, zbuf, dq_in, dkv_in, mixed, mixed_sib, normed, normed_sib, x_s, dh_s, w_s, slots,
     *rest,
@@ -540,10 +463,14 @@
     early = near_ref.shape[0]
     rows = base.shape[0] // chunks
     settled = early // rows
+    crossed = far_ref.shape[0]
+    summed = (early - crossed) // rows
     greet_all(count, me, place.seq, place.tp)
 
     near_copy = pltpu.make_async_copy(near_ref, base.at[pl.ds(0, early)], loc.at[0])
     near_copy.start()
+    far_copy = pltpu.make_async_copy(far_ref, ybuf.at[pl.ds(0, crossed)], loc.at[11])
+    far_copy.start()
 
     def start(k, carry):
         chunk_copy(count, me, k, dkv_ref, dkv_in, ks, kr).start()
@@ -562,25 +489,30 @@
                 (x_ref, x_s),
                 (dh_ref, dh_s),
             ]
-            + [(w, w_s.at[r]) for r, w in enumerate((w0, w1, w2, w3))]
+            + [(w.at[pl.ds(0, w_s.shape[1])], w_s.at[r]) for r, w in enumerate((w0, w1, w2, w3))]
         )
     ]
     near_copy.wait()
+    far_copy.wait()
     for copy in locals_:
         copy.start()
 
     def tp_copy(k):
-        span = rows_at(k * rows, rows)
-        return remote(far.at[span], ybuf.at[span], ys.at[k], yr.at[k], place.tp_partner)
+        return remote(
+            far.at[rows_at(k * rows, rows)], ybuf.at[rows_at(crossed + k * rows, rows)],
+            ys.at[k], yr.at[k], place.tp_partner,
+        )
 
     def arrived(k):
         @pl.when(k >= settled)
         def _():
-            late = k - settled
-            tp_copy(late).wait_recv()
+            tp_copy(k - settled).wait_recv()
+
+        @pl.when(k >= summed)
+        def _():
             span = rows_at(k * rows, rows)
             base[span, :] = (
-                base[span, :].astype(F32) + ybuf[rows_at(late * rows, rows), :].astype(F32)
+                base[span, :].astype(F32) + ybuf[rows_at((k - summed) * rows, rows), :].astype(F32)
             ).astype(BF16)
 
     tick, drain, ticks = reduce_stages(place, chunks, base, out, sib, xbuf, xsum, zbuf, sems, arrived)
@@ -698,7 +630,7 @@
     drain()
 
 
-def finish(gain, dq_chunks, dkv_chunks, near, normed, normed_sib, x, d_hidden, weights, vectors):
+def finish(gain, dq_chunks, dkv_chunks, near, far, normed, normed_sib, x, d_hidden, weights, vectors):
     early, cols = near.shape
     late = weights[0].shape[1]
     total = early + late
@@ -711,7 +643,7 @@
     scratch = [
         pltpu.VMEM((total, cols), BF16),
         pltpu.VMEM((late, cols), BF16),
-        pltpu.VMEM((late, cols), BF16),
+        pltpu.VMEM((far.shape[0] + late, cols), BF16),
         pltpu.VMEM((total // 2, cols), BF16),
         pltpu.VMEM((total // 2, cols), BF16),
         pltpu.VMEM((3, total // 8, cols), BF16),
@@ -723,12 +655,12 @@
         pltpu.VMEM((rows, cols), BF16),
         pltpu.VMEM((rows, cols), BF16),
         pltpu.VMEM((rows, cols), F32),
-        pltpu.VMEM((4,) + weights[0].shape, BF16),
+        pltpu.VMEM((4, cols, late), BF16),
         pltpu.VMEM((2 * VECTOR_STEPS,) + vectors.shape, F32),
     ]
     scratch += [dma((3, chunks) if name[0] == "z" else (chunks,)) for name in SEM_NAMES]
     scratch += [dma((count,))] * 4 + [dma((late_chunks,))] * 2 + [dma((2,))] * 2
-    scratch += [dma((VECTOR_STEPS,))] * 2 + [dma((11,))]
+    scratch += [dma((VECTOR_STEPS,))] * 2 + [dma((12,))]
     return pl.pallas_call(
         functools.partial(finish_kernel, chunks, FIRST_TICKS),
         out_shape=(
@@ -737,14 +669,161 @@
             jax.ShapeDtypeStruct((rows, cols), F32),
             jax.ShapeDtypeStruct(vectors.shape, F32),
         ),
-        in_specs=vmem(1) + [anywhere] * 11 + vmem(1),
+        in_specs=vmem(1) + [anywhere] * 12 + vmem(1),
         out_specs=(vmem(1)[0], anywhere, vmem(1)[0], vmem(1)[0]),
         scratch_shapes=scratch,
         compiler_params=pltpu.CompilerParams(
             collective_id=1, has_side_effects=True, vmem_limit_bytes=VMEM_LIMIT
         ),
         name="finish",
-    )(gain, dq_chunks, dkv_chunks, near, normed, normed_sib, x, d_hidden, *weights, vectors)
+    )(gain, dq_chunks, dkv_chunks, near, far, normed, normed_sib, x, d_hidden, *weights, vectors)
+
+
+def begin_kernel(
+    x_ref, gain_ref, shift_ref, w0, w1, wo_ref,
+    normed_ref, q_in, kv_own, kv_sib, w2, w3, wo2, wo3,
+    q_st, kv_st, *sems,
+):
+    place = Place()
+    count = q_in.shape[0]
+    width = x_ref.shape[1]
+    me = place.seq * 2 + place.tp
+    who = (place.tp, lax.rem(place.seq, 2))
+    ks, kr, qs, qr, fs, fr, ws, wr = sems
+    greet_all(count, me, place.seq, place.tp)
+    w_far = remote(w0, w2, ws.at[0], wr.at[0], place.tp_partner)
+    w_far.start()
+    wo_far = remote(wo_ref, wo2, ws.at[1], wr.at[1], place.tp_partner)
+    wo_far.start()
+    w_last = remote(w2, w3, ws.at[2], wr.at[2], place.core_partner)
+    wo_last = remote(wo2, wo3, ws.at[3], wr.at[3], place.core_partner)
+
+    def norm(part, carry):
+        span = rows_at(part * 64, 64)
+        normed_ref[span, :] = layer_norm(
+            x_ref[span, :].astype(F32), gain_ref[...], shift_ref[...]
+        ).astype(BF16)
+        return carry
+
+    lax.fori_loop(0, x_ref.shape[0] // 64, norm, 0)
+
+    def kv_copy(other):
+        return remote(kv_st.at[other], kv_own.at[me], ks.at[other], kr.at[me], (other // 2, lax.rem(other, 2)))
+
+    def q_copy(other):
+        return remote(q_st.at[other], q_in.at[me], qs.at[other], qr.at[me], (other // 2, lax.rem(other, 2)))
+
+    def kv_came(other):
+        return remote(kv_st.at[other], kv_own.at[other], ks.at[other], kr.at[other], (other // 2, lax.rem(other, 2)))
+
+    def q_came(other):
+        return remote(q_st.at[other], q_in.at[other], qs.at[other], qr.at[other], (other // 2, lax.rem(other, 2)))
+
+    def forward(other):
+        return remote(kv_own.at[other], kv_sib.at[other], fs.at[other], fr.at[other], place.core_partner)
+
+    low = low_lanes(HALF)
+
+    def project(quarter, w):
+        def dot(col):
+            return (
+                jnp.dot(normed_ref[...], w[:width, col : col + 256], preferred_element_type=F32)
+                + w[width : width + 1, col : col + 256].astype(F32)
+            )
+
+        keys, values = dot(256), dot(512)
+        for pair in range(2):
+            lanes = slice(pair * 128, pair * 128 + 128)
+            for half in range(2):
+                rows = slice(half * HALF, half * HALF + HALF)
+                k, v = keys[rows, lanes], values[rows, lanes]
+                kv_st[chunk_of(who, quarter, 2 * pair, half)] = jnp.where(low, k, swap_lanes(v)).astype(BF16)
+                kv_st[chunk_of(who, quarter, 2 * pair + 1, half)] = jnp.where(low, swap_lanes(k), v).astype(BF16)
+        store_packed(who, quarter, dot(0), q_st)
+
+        def send(i, carry):
+            other = chunk_of(who, quarter, i // 2, lax.rem(i, 2))
+
+            @pl.when(other != me)
+            def _():
+                kv_copy(other).start()
+                q_copy(other).start()
+
+            @pl.when(other == me)
+            def _():
+                kv_own[me] = kv_st[me]
+                q_in[me] = q_st[me]
+
+            return carry
+
+        lax.fori_loop(0, 8, send, 0)
+
+    project(0, w0)
+    project(1, w1)
+    w_far.wait()
+    w_last.start()
+    project(2, w2)
+    w_last.wait()
+    project(3, w3)
+    wo_far.wait()
+    wo_last.start()
+    forward(me).start()
+
+    def receive(i, carry):
+        other = lax.rem(place.seq + lax.rem(i, count // 2), count // 2) * 2 + lax.rem(
+            place.tp + i // (count // 2), 2
+        )
+        kv_came(other).wait_recv()
+        forward(other).start()
+        return carry
+
+    lax.fori_loop(1, count, receive, 0)
+
+    def rest(k, carry):
+        other = lax.rem(me + k, count)
+        q_came(other).wait_recv()
+        kv_copy(other).wait_send()
+        q_copy(other).wait_send()
+        return carry
+
+    lax.fori_loop(1, count, rest, 0)
+
+    def forwarded(k, carry):
+        forward(k).wait()
+        return carry
+
+    lax.fori_loop(0, count, forwarded, 0)
+    wo_last.wait()
+
+
+def begin(x, gain, shift, w0, w1, wo0):
+    rows, width = x.shape
+    count = 32
+    dma = pltpu.SemaphoreType.DMA
+    anywhere = pl.BlockSpec(memory_space=pl.ANY)
+    q_shape, kv_shape = (count, QUART, 2 * HEAD), (count, HALF, 2 * HEAD)
+    return pl.pallas_call(
+        begin_kernel,
+        out_shape=(
+            jax.ShapeDtypeStruct((rows, width), BF16),
+            jax.ShapeDtypeStruct(q_shape, BF16),
+            jax.ShapeDtypeStruct(kv_shape, BF16),
+            jax.ShapeDtypeStruct(kv_shape, BF16),
+            jax.ShapeDtypeStruct(w0.shape, BF16),
+            jax.ShapeDtypeStruct(w0.shape, BF16),
+            jax.ShapeDtypeStruct(wo0.shape, BF16),
+            jax.ShapeDtypeStruct(wo0.shape, BF16),
+        ),
+        in_specs=vmem(5) + [anywhere],
+        out_specs=tuple(vmem(6) + [anywhere] * 2),
+        scratch_shapes=[pltpu.VMEM(q_shape, BF16), pltpu.VMEM(kv_shape, BF16)]
+        + [dma((count,))] * 6
+        + [dma((4,))] * 2,
+        compiler_params=pltpu.CompilerParams(
+            collective_id=3, has_side_effects=True, vmem_limit_bytes=VMEM_LIMIT
+        ),
+        name="begin",
+    )(x, gain, shift, w0, w1, wo0)
 
 
 def norm_parts(values):
@@ -754,15 +833,379 @@
     return centred * rstd, rstd
 
 
-def norm_back(values, gain, upstream):
-    xhat, rstd = norm_parts(values)
+GELU_A = 0.7978845608028654
+GELU_B = 0.044715
+
+
+def gelu_parts(u):
+    square = u * u
+    t = jnp.tanh(GELU_A * u * (1.0 + GELU_B * square))
+    rise = 0.5 * (1.0 + t)
+    return u * rise, rise + 0.5 * u * (1.0 - t * t) * (GELU_A * (1.0 + 3.0 * GELU_B * square))
+
+
+def col_sum(values):
+    return jnp.sum(values, axis=0, keepdims=True)
+
+
+def back_rows(xhat, rstd, gain, upstream):
     e = upstream * gain
-    grad = rstd * (
-        e
-        - jnp.mean(e, axis=-1, keepdims=True)
-        - xhat * jnp.mean(e * xhat, axis=-1, keepdims=True)
-    )
-    return grad, jnp.sum(upstream * xhat, axis=0), jnp.sum(upstream, axis=0)
+    return rstd * (
+        e - jnp.mean(e, axis=-1, keepdims=True) - xhat * jnp.mean(e * xhat, axis=-1, keepdims=True)
+    )
+
+
+def dot_nn(a, b):
+    return jnp.dot(a, b, preferred_element_type=F32)
+
+
+def dot_nt(a, b):
+    return lax.dot_general(a, b, (((1,), (1,)), ((), ())), preferred_element_type=F32)
+
+
+def dot_tn(a, b):
+    return lax.dot_general(a, b, (((0,), (0,)), ((), ())), preferred_element_type=F32)
+
+
+def middle_kernel(
+    gains, shifts, bias_out, bias_down, bias_up, att_ref, x_ref, og_ref,
+    wo0, wo1, wo2, wo3, wu0, wu1, wu2, wd0, wd1,
+    result, da_in, dh, vec, near_ref, far_ref,
+    att_in, att_s, att_sib, wo_s, wu_s, wd_s, x_s, branch_s, hidden_s, inner_s, inner_sib, act_s, act_sib,
+    dg_s, dup_sib, down_s, dd_s, dd_sib, db_s, db_sib, da_st, fd_s, fd_in,
+    ats, atr, das, dar, ws, wr, cs, cr, fs, fr, loc,
+):
+    place = Place()
+    count = att_in.shape[0]
+    me = place.seq * 2 + place.tp
+    who = (place.tp, lax.rem(place.seq, 2))
+    rows, width = x_s.shape
+    hid = wd_s.shape[1]
+    greet_all(count, me, place.seq, place.tp)
+
+    def start(k, carry):
+        chunk_copy(count, me, k, att_ref, att_in, ats, atr).start()
+        return carry
+
+    lax.fori_loop(1, count, start, 0)
+    wd_far = remote(wd0, wd_s.at[2], ws.at[0], wr.at[0], place.tp_partner)
+    wd_far.start()
+    wu_last = remote(wu2, wu_s.at[3], ws.at[1], wr.at[1], place.core_partner)
+    wu_last.start()
+    wd_last = remote(wd_s.at[2], wd_s.at[3], ws.at[2], wr.at[2], place.core_partner)
+    loads = [(att_ref.at[me], att_in.at[me]), (x_ref, x_s), (og_ref, dh)]
+    loads += [(w, wo_s.at[r]) for r, w in enumerate((wo0, wo1, wo2, wo3))]
+    loads += [(w, wu_s.at[r]) for r, w in enumerate((wu0, wu1, wu2))]
+    loads += [(w, wd_s.at[r]) for r, w in enumerate((wd0, wd1))]
+    loads = [pltpu.make_async_copy(src, dst, loc.at[i]) for i, (src, dst) in enumerate(loads)]
+    for copy in loads:
+        copy.start()
+
+    def to_core(i, src, dst):
+        return remote(src, dst, cs.at[i], cr.at[i], place.core_partner)
+
+    att_pair = [to_core(i, att_s.at[2 * i + 1], att_sib.at[i]) for i in range(2)]
+    act_pair = [to_core(2 + i, act_s.at[2 * i + 1], act_sib.at[i]) for i in range(2)]
+    dup_pair = [to_core(4 + i, dg_s.at[2 * i + 1], dup_sib.at[i]) for i in range(2)]
+    inner_pair = to_core(6, inner_s, inner_sib)
+    dd_pair = to_core(7, dd_s, dd_sib)
+    db_pair = to_core(8, db_s, db_sib)
+
+    def came(k, carry):
+        chunk_copy(count, me, k, att_ref, att_in, ats, atr).wait()
+        return carry
+
+    lax.fori_loop(1, count, came, 0)
+    for copy in loads:
+        copy.wait()
+    for quarter in range(4):
+        load_packed(who, quarter, att_in, att_s.at[quarter], 0)
+    for copy in att_pair:
+        copy.start()
+
+    def cols(i):
+        return rows_at(i * 256, 256)
+
+    def project(i, carry):
+        span = cols(i)
+        branch_s[:, span] = (
+            dot_nn(att_s[0], wo_s[0, :, span])
+            + dot_nn(att_s[1], wo_s[1, :, span])
+            + dot_nn(att_s[2], wo_s[2, :, span])
+            + dot_nn(att_s[3], wo_s[3, :, span])
+            + bias_out[:, span]
+        )
+        return carry
+
+    lax.fori_loop(0, width // 256, project, 0)
+
+    def into(i, carry):
+        span = rows_at(i * 64, 64)
+        hidden = x_s[span, :].astype(F32) + layer_norm(branch_s[span, :], gains[1:2, :], shifts[1:2, :])
+        hidden_s[span, :] = hidden
+        inner_s[span, :] = layer_norm(hidden, gains[2:3, :], shifts[2:3, :]).astype(BF16)
+        return carry
+
+    lax.fori_loop(0, rows // 64, into, 0)
+    inner_pair.start()
+    for quarter in range(4):
+        if quarter == 3:
+            wu_last.wait()
+
+        def up(i, carry, quarter=quarter):
+            span = cols(i)
+            act, slope = gelu_parts(
+                dot_nn(inner_s[...], wu_s[quarter, :, span]) + bias_up[quarter : quarter + 1, span]
+            )
+            act_s[quarter, :, span] = act.astype(BF16)
+            dg_s[quarter, :, span] = slope.astype(BF16)
+            return carry
+
+        lax.fori_loop(0, hid // 256, up, 0)
+        if quarter % 2 == 1:
+            act_pair[quarter // 2].start()
+
+    def down_own(i, carry):
+        span = cols(i)
+        down_s[:, span] = (
+            dot_nn(act_s[0], wd_s[0, :, span]) + dot_nn(act_s[1], wd_s[1, :, span]) + bias_down[:, span]
+        )
+        return carry
+
+    lax.fori_loop(0, width // 256, down_own, 0)
+    wd_far.wait()
+    wd_last.start()
+    for quarter in (2, 3):
+        if quarter == 3:
+            wd_last.wait()
+
+        def down_far(i, carry, quarter=quarter):
+            span = cols(i)
+            down_s[:, span] += dot_nn(act_s[quarter], wd_s[quarter, :, span])
+            return carry
+
+        lax.fori_loop(0, width // 256, down_far, 0)
+
+    none = jnp.zeros((1, width), F32)
+
+    def turn(i, carry):
+        gain, shift, bias = carry
+        span = rows_at(i * 64, 64)
+        xhat, rstd = norm_parts(down_s[span, :])
+        result[span, :] = (hidden_s[span, :] + xhat * gains[3:4, :] + shifts[3:4, :]).astype(BF16)
+        upstream = dh[span, :]
+        d_down = back_rows(xhat, rstd, gains[3:4, :], upstream)
+        dd_s[span, :] = d_down.astype(BF16)
+        return gain + col_sum(upstream * xhat), shift + col_sum(upstream), bias + col_sum(d_down)
+
+    gain, shift, bias = lax.fori_loop(0, rows // 64, turn, (none,) * 3)
+    vec[...] = jnp.zeros_like(vec)
+    vec[3:4, :] = gain
+    vec[7:8, :] = shift
+    vec[9:10, :] = bias
+    dd_pair.start()
+    act_pair[1].wait_recv()
+    dd_pair.wait_recv()
+
+    def far_copy(i):
+        return remote(fd_s.at[cols(i)], fd_in.at[cols(i)], fs.at[i], fr.at[i], place.tp_partner)
+
+    def far_down(i, carry):
+        span = cols(i)
+        fd_s[span, :] = (
+            dot_tn(act_s[2, :, span], dd_s[...]) + dot_tn(act_sib[1, :, span], dd_sib[...])
+        ).astype(BF16)
+        far_copy(i).start()
+        return carry
+
+    lax.fori_loop(0, hid // 256, far_down, 0)
+    for quarter in range(4):
+        absolute = (who[0] * 2 + who[1]) ^ quarter
+
+        def back_up(i, carry, quarter=quarter, absolute=absolute):
+            span = cols(i)
+            d_up = dot_nt(dd_s[...], wd_s[quarter, span, :]) * dg_s[quarter, :, span].astype(F32)
+            d_up = d_up.astype(BF16)
+            dg_s[quarter, :, span] = d_up
+            vec[pl.ds(12 + absolute, 1), span] = col_sum(d_up.astype(F32))
+            return carry
+
+        lax.fori_loop(0, hid // 256, back_up, 0)
+        if quarter % 2 == 1:
+            dup_pair[quarter // 2].start()
+
+    def back_inner(i, carry):
+        span = cols(i)
+        down_s[:, span] = (
+            dot_nt(dg_s[0], wu_s[0, span, :])
+            + dot_nt(dg_s[1], wu_s[1, span, :])
+            + dot_nt(dg_s[2], wu_s[2, span, :])
+            + dot_nt(dg_s[3], wu_s[3, span, :])
+        )
+        return carry
+
+    lax.fori_loop(0, width // 256, back_inner, 0)
+
+    def out_of(i, carry):
+        gain3, shift3, gain2, shift2, bias = carry
+        span = rows_at(i * 64, 64)
+        d_inner = down_s[span, :]
+        xhat, rstd = norm_parts(hidden_s[span, :])
+        gain3 = gain3 + col_sum(d_inner * xhat)
+        shift3 = shift3 + col_sum(d_inner)
+        d_hidden = dh[span, :] + back_rows(xhat, rstd, gains[2:3, :], d_inner)
+        dh[span, :] = d_hidden
+        xhat, rstd = norm_parts(branch_s[span, :])
+        d_branch = back_rows(xhat, rstd, gains[1:2, :], d_hidden)
+        db_s[span, :] = d_branch.astype(BF16)
+        return (
+            gain3, shift3, gain2 + col_sum(d_hidden * xhat), shift2 + col_sum(d_hidden),
+            bias + col_sum(d_branch),
+        )
+
+    sums = lax.fori_loop(0, rows // 64, out_of, (none,) * 5)
+    for row, value in zip((2, 6, 1, 5, 8), sums):
+        vec[row : row + 1, :] = value
+    db_pair.start()
+
+    def da_copy(other):
+        return remote(
+            da_st.at[other], da_in.at[me], das.at[other], dar.at[me], (other // 2, lax.rem(other, 2))
+        )
+
+    def da_came(other):
+        return remote(
+            da_st.at[other], da_in.at[other], das.at[other], dar.at[other], (other // 2, lax.rem(other, 2))
+        )
+
+    for quarter in range(4):
+        store_packed(who, quarter, dot_nt(db_s[...], wo_s[quarter]), da_st)
+
+        def send(i, carry, quarter=quarter):
+            other = chunk_of(who, quarter, i // 2, lax.rem(i, 2))
+
+            @pl.when(other != me)
+            def _():
+                da_copy(other).start()
+
+            @pl.when(other == me)
+            def _():
+                da_in[me] = da_st[me]
+
+            return carry
+
+        lax.fori_loop(0, 8, send, 0)
+
+    for copy in dup_pair + [inner_pair]:
+        copy.wait()
+
+    def grad_up(i, carry):
+        span = cols(i)
+        for near, slot in ((0, 0), (2, 1)):
+            wu_s[near, :, span] = (
+                dot_tn(inner_s[...], dg_s[near, :, span]) + dot_tn(inner_sib[...], dup_sib[slot, :, span])
+            ).astype(BF16)
+        return carry
+
+    lax.fori_loop(0, hid // 256, grad_up, 0)
+    for copy in att_pair + [db_pair]:
+        copy.wait()
+    for near, slot in ((0, 0), (2, 1)):
+        wo_s[near] = (dot_tn(att_s[near], db_s[...]) + dot_tn(att_sib[slot], db_sib[...])).astype(BF16)
+    up_rows, out_rows = wu_s.shape[1], wo_s.shape[1]
+    stores = [
+        (wu_s.at[0], near_ref.at[pl.ds(hid, up_rows)]),
+        (wo_s.at[0], near_ref.at[pl.ds(hid + up_rows, out_rows)]),
+        (wu_s.at[2], far_ref.at[pl.ds(0, up_rows)]),
+        (wo_s.at[2], far_ref.at[pl.ds(up_rows, out_rows)]),
+    ]
+    stores = [pltpu.make_async_copy(src, dst, loc.at[i]) for i, (src, dst) in enumerate(stores)]
+    for copy in stores:
+        copy.start()
+    act_pair[0].wait()
+    act_pair[1].wait_send()
+    dd_pair.wait_send()
+
+    def near_down(i, carry):
+        span = cols(i)
+        far_copy(i).wait()
+        wd_s[0, span, :] = (
+            dot_tn(act_s[0, :, span], dd_s[...])
+            + dot_tn(act_sib[0, :, span], dd_sib[...])
+            + fd_in[span, :].astype(F32)
+        ).astype(BF16)
+        return carry
+
+    lax.fori_loop(0, hid // 256, near_down, 0)
+    last = pltpu.make_async_copy(wd_s.at[0], near_ref.at[pl.ds(0, hid)], loc.at[4])
+    last.start()
+
+    def da_wait(k, carry):
+        other = lax.rem(me + k, count)
+        da_came(other).wait_recv()
+        da_copy(other).wait_send()
+        return carry
+
+    lax.fori_loop(1, count, da_wait, 0)
+    for copy in stores + [last]:
+        copy.wait()
+
+
+def middle(gains, shifts, bias_out, bias_down, bias_up, att, x, out_grad, wo4, wu3, wd2):
+    rows, width = x.shape
+    count = att.shape[0]
+    hid = wd2[0].shape[0]
+    out_rows = wo4[0].shape[0]
+    dma = pltpu.SemaphoreType.DMA
+    anywhere = pl.BlockSpec(memory_space=pl.ANY)
+
+    def held(*shape, dtype=BF16):
+        return pltpu.VMEM(shape, dtype)
+
+    scratch = [
+        held(*att.shape),
+        held(4, rows, out_rows),
+        held(2, rows, out_rows),
+        held(4, out_rows, width),
+        held(4, width, hid),
+        held(4, hid, width),
+        held(rows, width),
+        held(rows, width, dtype=F32),
+        held(rows, width, dtype=F32),
+        held(rows, width),
+        held(rows, width),
+        held(4, rows, hid),
+        held(2, rows, hid),
+        held(4, rows, hid),
+        held(2, rows, hid),
+        held(rows, width, dtype=F32),
+        held(rows, width),
+        held(rows, width),
+        held(rows, width),
+        held(rows, width),
+        held(*att.shape),
+        held(hid, width),
+        held(hid, width),
+    ]
+    scratch += [dma((count,))] * 4 + [dma((3,))] * 2 + [dma((9,))] * 2 + [dma((4,))] * 2 + [dma((12,))]
+    return pl.pallas_call(
+        middle_kernel,
+        out_shape=(
+            jax.ShapeDtypeStruct((rows, width), BF16),
+            jax.ShapeDtypeStruct(att.shape, BF16),
+            jax.ShapeDtypeStruct((rows, width), F32),
+            jax.ShapeDtypeStruct((16, width), F32),
+            jax.ShapeDtypeStruct((hid + width + out_rows, width), BF16),
+            jax.ShapeDtypeStruct((width + out_rows, width), BF16),
+        ),
+        in_specs=vmem(5) + [anywhere] * 12,
+        out_specs=tuple(vmem(4) + [anywhere] * 2),
+        scratch_shapes=scratch,
+        compiler_params=pltpu.CompilerParams(
+            collective_id=4, has_side_effects=True, vmem_limit_bytes=VMEM_MIDDLE
+        ),
+        name="middle",
+    )(gains, shifts, bias_out, bias_down, bias_up, att, x, out_grad, *wo4, *wu3, *wd2)
 
 
 def fast_local(
@@ -793,96 +1236,44 @@
         return [own, sib, far, to_sib(far)]
 
     width = w_qkv.shape[0]
-    wq4 = [w.reshape(width, -1) for w in quarters(w_qkv, 2)]
-    small = jnp.concatenate([bias_qv.reshape(2, 2, -1), bias_up.reshape(2, 2, -1).transpose(1, 0, 2)], axis=2)
-    small = small.transpose(1, 0, 2)
-    small4 = [s.reshape(2, -1) for s in quarters(small, 0)]
-    split = bias_qv.shape[1] // 2
-    bias_qv4 = jnp.stack([s[:, :split].reshape(-1) for s in small4])
-    bias_up4 = [s[:, split:].reshape(-1).astype(F32) for s in small4]
-    wo4 = quarters(w_out, 0)
-    wu4 = quarters(w_up, 1)
-    wd4 = quarters(w_down, 0)
+
+    def halves(values, axis):
+        size = values.shape[axis] // 2
+        return [
+            lax.dynamic_slice_in_dim(values, which * size, size, axis) for which in (core, 1 - core)
+        ]
+
+    bias3 = jnp.stack([bias_qv[0], jnp.zeros_like(bias_qv[0]), bias_qv[1]])
+    bias3 = jnp.broadcast_to(bias3[None], (16,) + bias3.shape)
+    w_ext = jnp.concatenate([w_qkv, bias3])
+    wq0, wq1 = [w.reshape(w.shape[0], -1) for w in halves(w_ext, 2)]
+    wo0, wo1 = halves(w_out, 0)
+    bias_up4 = jnp.concatenate([b.astype(F32).reshape(1, -1) for b in quarters(bias_up.reshape(2, 1, -1), 0)])
 
     tables = block_tables(lengths, prefixes, placement, core)
-    normed, q_chunks, kv_chunks = project(
-        who, tokens_in, norm_gains[:1], norm_shifts[:1], bias_qv4, wq4
-    )
-    kv_own = exchange(kv_chunks)
-    kv_sib = to_sib(kv_own)
-    q_own = exchange(q_chunks)
+    normed, q_own, kv_own, kv_sib, wq2, wq3, wo2, wo3 = begin(
+        tokens_in, norm_gains[:1], norm_shifts[:1], wq0, wq1, wo0
+    )
+    wq4 = [wq0, wq1, wq2, wq3]
+    wo4 = [wo0, wo1, wo2, wo3]
+    w_up, w_down, normed = lax.optimization_barrier((w_up, w_down, normed))
+    wu0, wu1 = halves(w_up, 1)
+    wd0, wd1 = halves(w_down, 0)
+    wu2 = to_tp(wu0)
     att_chunks, out_t, mass, kv_pack, kv_turned = attend(core, tables, q_own, kv_own, kv_sib)
-    attended = unpack_heads(who, exchange(att_chunks))
-
-    input_f32 = tokens_in.astype(F32)
-
-    def cols(values, quarter, count):
-        return values[:, quarter * count : (quarter + 1) * count]
-
-    def dot(a, b):
-        return jnp.dot(a, b, preferred_element_type=F32)
-
-    def dot_t(a, b):
-        return lax.dot_general(a, b, (((1,), (1,)), ((), ())), preferred_element_type=F32)
-
-    def dot_rows(a, b):
-        return lax.dot_general(a, b, (((0,), (0,)), ((), ())), preferred_element_type=F32)
-
-    heads4 = [cols(attended, r, 256) for r in range(4)]
-    branch = sum(dot(heads4[r], wo4[r]) for r in range(4)) + bias_out.astype(F32)
-    hidden = input_f32 + layer_norm(branch, norm_gains[1], norm_shifts[1])
-    inner = layer_norm(hidden, norm_gains[2], norm_shifts[2]).astype(BF16)
-    active4, gate4 = [], []
-    for r in range(4):
-        act, back_gate = jax.vjp(smooth_gate, dot(inner, wu4[r]) + bias_up4[r])
-        active4.append(act.astype(BF16))
-        gate4.append(back_gate)
-    down = sum(dot(active4[r], wd4[r]) for r in range(4)) + bias_down.astype(F32)
-    result = (hidden + layer_norm(down, norm_gains[3], norm_shifts[3])).astype(BF16)
-    d_down, gain_last, shift_last = norm_back(down, norm_gains[3], out_grad)
-    bias_down_part = jnp.sum(d_down, axis=0)
-    d_down_b = d_down.astype(BF16)
-    inner_sib, down_sib = to_sib(inner), to_sib(d_down_b)
-    active_sib = [to_sib(active4[r]) for r in (1, 3)]
-
-    def tie(values, *others):
-        return lax.optimization_barrier((values,) + others)[0]
-
-    def reduced(near, far):
-        return (near + to_tp(far).astype(F32)).astype(BF16)
-
-    d_up4 = [gate4[r](dot_t(d_down_b, wd4[r]))[0].astype(BF16) for r in range(4)]
-    up_sib = [to_sib(d_up4[r]) for r in (1, 3)]
-    near_down, far_down = (
-        dot_rows(active4[r], d_down_b) + dot_rows(s, down_sib) for r, s in zip((0, 2), active_sib)
-    )
-    far_down = far_down.astype(BF16)
-    d_up4 = tie(d_up4, far_down)
-    bias_up_part = [jnp.sum(d.astype(F32), axis=0) for d in d_up4]
-    d_inner = sum(dot_t(d_up4[r], wu4[r]) for r in range(4))
-    d_third, gain_third, shift_third = norm_back(hidden, norm_gains[2], d_inner)
-    d_hidden = out_grad + d_third
-    d_branch, gain_second, shift_second = norm_back(branch, norm_gains[1], d_hidden)
-    bias_out_part = jnp.sum(d_branch, axis=0)
-    d_branch_b = d_branch.astype(BF16)
-    branch_sib, normed_sib = to_sib(d_branch_b), to_sib(normed)
-    heads_sib = [to_sib(heads4[r]) for r in (1, 3)]
-    da_own = exchange(spread(who, d_branch_b, wo4))
-    near_up, far_up = (
-        dot_rows(inner, d_up4[r]) + dot_rows(inner_sib, s) for r, s in zip((0, 2), up_sib)
-    )
-    near_out, far_out = (
-        dot_rows(heads4[r], d_branch_b) + dot_rows(s, branch_sib)
-        for r, s in zip((0, 2), heads_sib)
-    )
-    far_up, far_out = far_up.astype(BF16), far_out.astype(BF16)
-    g_down = reduced(near_down, far_down)
-    da_own = tie(da_own, far_up, far_out, g_down)
+    normed_sib = to_sib(normed)
+    result, da_own, d_hidden, vectors, near, far = middle(
+        norm_gains, norm_shifts, bias_out.astype(F32)[None], bias_down.astype(F32)[None], bias_up4,
+        att_chunks, tokens_in, out_grad, wo4, [wu0, wu1, wu2], [wd0, wd1],
+    )
+    far = to_tp(far)
     dq_chunks, dkv_mine, dkv_theirs = attend_back(
         core, tables, q_own, da_own, out_t, mass, kv_pack, kv_turned
     )
     dkv_chunks = (dkv_mine + to_sib(dkv_theirs).astype(F32)).astype(BF16)
-    near_all = jnp.concatenate([g_down, reduced(near_up, far_up), reduced(near_out, far_out)])
+    sums, sums_sib, grad_x, vectors = finish(
+        norm_gains[:1], dq_chunks, dkv_chunks, near, far, normed, normed_sib, tokens_in, d_hidden, wq4, vectors
+    )
 
     def joined(pair, axis):
         own, sib = pair
@@ -890,26 +1281,10 @@
         second = jnp.concatenate([sib, own], axis=axis).astype(F32)
         return jnp.where(core == 0, first, second)
 
-    def absolute(parts):
-        base = tp * 2 + core
-        return jnp.concatenate(
-            [sum(jnp.where((base ^ r) == a, parts[r], 0.0) for r in range(4)) for a in range(4)]
-        )
-
-    blank = jnp.zeros_like(gain_last)
-    vectors = jnp.stack(
-        [blank, gain_second, gain_third, gain_last]
-        + [blank, shift_second, shift_third, shift_last]
-        + [bias_out_part, bias_down_part, blank, blank]
-    )
-    vectors = jnp.concatenate([vectors, absolute(bias_up_part).reshape(4, -1)])
-    sums, sums_sib, grad_x, vectors = finish(
-        norm_gains[:1], dq_chunks, dkv_chunks, near_all, normed, normed_sib, tokens_in, d_hidden, wq4, vectors
-    )
     pair = (sums, sums_sib)
-    hidden_rows = g_down.shape[0]
+    hidden_rows = wd0.shape[0]
     up_end = hidden_rows + width
-    out_end = near_all.shape[0]
+    out_end = near.shape[0]
 
     def rows_of(start, stop):
         return [part[start:stop] for part in pair]

time: 756 us -> 677 us (0.90)
  Pallas kernels: 357 us -> 580 us
  waiting for transfers between devices: 117 us -> 4.08 us
  matrix products: 88.5 us -> 0 us
  blocking collectives: 53.6 us -> 0 us
  starting transfers between devices: 38.3 us -> 6.47 us
  other arithmetic: 37.5 us -> 26.9 us
    pallas_call x3 -> x2, Pallas kernels: 15.7 us -> 237 us  [the longest x1 140 us: middle(): pl.pallas_call(middle_kernel, out_shape=(jax.ShapeDtypeStruct((rows, widt...]
    ppermute x8 -> x3, waiting for transfers between devices: 99.5 us -> 0.01 us  [to_tp(): return lax.ppermute(values, 'tp', over_tp)]
    dot_general x32 -> x0, matrix products: 88.5 us -> none  [the longest x12 31.4 us: dot_rows(): lax.dot_general(a, b, (((0,), (0,)), ((), ())), preferred_element_type=F32)]
    all_to_all x1 -> x0, blocking collectives: 53.6 us -> none  [exchange(): return lax.all_to_all(chunks, ('seq', 'tp'), 0, 0, tiled=True)]
    all_to_all x3 -> x0, starting transfers between devices: 16.9 us -> none  [exchange(): return lax.all_to_all(chunks, ('seq', 'tp'), 0, 0, tiled=True)]
    all_to_all x3 -> x0, waiting for transfers between devices: 16.6 us -> none  [exchange(): return lax.all_to_all(chunks, ('seq', 'tp'), 0, 0, tiled=True)]
    reduce_sum x12 -> x0, other arithmetic: 11.5 us -> none  [the longest x2 3.61 us: norm_back(): return (grad, jnp.sum(upstream * xhat, axis=0), jnp.sum(upstream, axis=0))]
    ppermute x8 -> x3, starting transfers between devices: 12.8 us -> 3.62 us  [to_tp(): return lax.ppermute(values, 'tp', over_tp)]
  transfers between devices with their start and end apart: 28 -> 6, of which waited for: 6 -> 1; matrix products, arithmetic and copies ran while one was open for 15% -> 2% of each run, Pallas kernels for 15% -> 16%
where the time goes in v4:
time: 677 us; the launch traced here: 666 us
  Pallas kernels  580 us (86%)
  local copies, waits for them, and re-layouts  46.7 us (7%)
  other arithmetic  26.9 us (4%)
    pallas_call x1, Pallas kernels, finish(): pl.pallas_call(functools.partial(finish_kernel, chunks, FIRST_TICKS), out...  236 us
    pallas_call x1, Pallas kernels, middle(): pl.pallas_call(middle_kernel, out_shape=(jax.ShapeDtypeStruct((rows, widt...  140 us
    pallas_call x1, Pallas kernels, begin(): pl.pallas_call(begin_kernel, out_shape=(jax.ShapeDtypeStruct((rows, width...  96.4 us
    pallas_call x1, Pallas kernels, attend_back(): pl.pallas_call(attend_back_kernel, out_shape=(jax.ShapeDtypeStruct((block...  57.7 us
    pallas_call x1, Pallas kernels, attend(): pl.pallas_call(attend_kernel, out_shape=(jax.ShapeDtypeStruct((blocks, QU...  50 us
  transfers between devices with their start and end apart: 6, of which 1 were waited for; matrix products, arithmetic and copies ran while one was open for 2% of the time, Pallas kernels for 16%

profile of v4, /device:TPU:0, one launch (start us, length us, event | category | flops | bytes accessed | tf_op | source)
XLA Modules:
  0.0 665.5 jit_solution(3534840882892558212)
XLA Ops:
  1.6 3.3 fusion
  4.9 2.7 copy.45
  7.6 2.3 copy.47.w0
  10.9 2.2 copy.48.w1
  14.2 1.3 slice.55.gain_ref
  15.5 1.3 slice.56.shift_ref
  16.8 96.4 %begin.1 = (bf16[512,1024]{1,0:T(8,128)(2,1)}, bf16[32,128,128]{2,1,0:T(8,128)(2,1)}, bf16[32,256,128]{2,1,0:T(8,128)(2,1)}, bf16[32,256,128]{2,1,0:T(8,128)(2,1...) custom-call(bf16[512,1024]{1,0:T(8,128)(2,1)} %x_ref.5, ...), custom_call_target="tpu_custom_call" | custom-call | tf_op jit(solution)/shard_map/begin/pallas_call | solution.py:805
  113.3 4.0 constant_dynamic-slice_fusion.2
  117.3 1.5 collective-permute-start.2
  122.1 50.0 %attend.1 = (bf16[32,128,128]{2,1,0:T(8,128)(2,1)}, f32[32,64,256]{2,1,0:T(8,128)}, f32[32,1,256]{2,1,0:T(1,128)}, bf16[17408,128]{1,0:T(8,128)(2,1)}, bf16[128,17408]{1,0:T(8,128)(2,1)}) custom-call(s32[1]{0:T(128)} %bitcast.6.part_ref, s32[5,32]{1,0:T(8,128)} %stack.20.tab, s32[32,1,256]{2,1,0:T(1,128)} %broadcast_in_dim.61.low_ref, ...), custom_call_target="tpu_custom_call" | custom-call | flops 40000000000 | bytes 20971520 | tf_op jit(solution)/shard_map/attend/pallas_call | solution.py:228
  172.2 1.3 collective-permute-start.1
  173.5 4.7 constant_dynamic-slice_fusion
  180.0 140.4 %middle.1 = (bf16[512,1024]{1,0:T(8,128)(2,1)}, bf16[32,128,128]{2,1,0:T(8,128)(2,1)}, f32[512,1024]{1,0:T(8,128)}, f32[16,1024]{1,0:T(8,128)}, bf16[2304,1024]{1,0:T(8,128)(2,1)}, /*index=5*/bf16[1280,1024]{1,0:T(8,128)(2,1)}) custom-call(f32[4,1024]{1,0:T(4,128)} %gains.1, f32[4,1024]{1,0:T(4,128)} %shifts.1, f32[1,1024]{1,0:T(1,128)} %bitcast.48, ...), custom_call_target="tpu_custom_call" | custom-call | tf_op jit(solution)/shard_map/middle/pallas_call | solution.py:1191
  320.3 1.5 collective-permute-start.4
  321.9 57.7 %attend_back.1 = (bf16[32,128,128]{2,1,0:T(8,128)(2,1)}, f32[32,256,128]{2,1,0:T(8,128)}, bf16[32,256,128]{2,1,0:T(8,128)(2,1)}) custom-call(s32[1]{0:T(128)} %bitcast.6.part_ref, s32[5,32]{1,0:T(8,128)} %stack.20.tab, s32[32,1,256]{2,1,0:T(1,128)} %broadcast_in_dim.61.low_ref, s32[32,1,256]{2,1,0:T(1,128)} %maximum_minimum_fusion.high_ref, ...), custom_call_target="tpu_custom_call" | custom-call | flops 60000002048 | bytes 31457280 | tf_op jit(solution)/shard_map/attend_back/pallas_call | solution.py:251
  379.6 1.5 collective-permute-start.3
  381.1 4.1 collective-permute-done.3
  385.2 4.8 add_convert_fusion.dkv_ref
  390.1 1.5 copy-done.5
  391.6 235.5 %finish.1 = (bf16[3072,1024]{1,0:T(8,128)(2,1)}, bf16[3072,1024]{1,0:T(8,128)(2,1)}, f32[512,1024]{1,0:T(8,128)}, f32[16,1024]{1,0:T(8,128)}) custom-call(f32[1,1024]{1,0:T(1,128)} %slice.55.gain_ref, bf16[32,128,128]{2,1,0:T(8,128)(2,1)} %get-tuple-element.56.dq_ref, bf16[32,256,128]{2,1,0:T(8,128)(2,1)} %add_convert_fusion.dkv_ref, ...), custom_call_target="tpu_custom_call" | custom-call | tf_op jit(solution)/shard_map/finish/pallas_call | solution.py:664
  627.1 4.2 fusion.7
  631.3 1.1 slice.62
  632.4 2.4 fusion.8
  634.9 2.7 slice.59
  637.6 1.3 slice.60
  640.1 2.6 copy.51
  642.6 2.6 copy.52
  645.2 6.3 convert_select_fusion
  651.6 4.2 convert_select_fusion.1
  655.7 1.8 convert_select_fusion.2
  658.4 3.2 select_bitcast_fusion
  663.7 1.3 copy.61
  (69 shorter events, 12.6 us)
Async XLA Ops:
  10.9 2.3 copy-start.8
  113.2 5.5 copy-start.10
  113.2 6.2 copy-start.15
  113.2 6.2 copy-start.14
  113.3 6.3 copy-start.13
  117.3 54.9 %copy-start = (bf16[1024,1024]{1,0:T(8,128)(2,1)}, bf16[1024,1024]{1,0:T(8,128)(2,1)S(1)}, u32[]{:S(2)}) copy-start(bf16[1024,1024]{1,0:T(8,128)(2,1)S(1)} %get-tuple-element.86.wu0) | copy-start | bytes 6291460
  117.3 62.7 %collective-permute-start.2 = (bf16[1024,1024]{1,0:T(8,128)(2,1)S(1)}, bf16[1024,1024]{1,0:T(8,128)(2,1)}, u32[]{:S(2)}, u32[]{:S(2)}) collective-permute-start(bf16[1024,1024]{1,0:T(8,128)(2,1)S(1)} %get-tuple-element.86.wu0), channel_id=1, source_target_pairs={{0,1},{1,0},{2,3},{3,2},{4,5},{5,4},{6,7},{7,6},{8,9},{9,8},{10,11... | collective-permute-start | bytes 6291464 | tf_op jit(solution)/shard_map/ppermute | solution.py:1223
  118.8 53.4 %collective-permute-start = (bf16[1,1,1024]{2,0,1:T(2,128)(2,1)S(1)}, bf16[1,1,1024]{2,0,1:T(2,128)(2,1)S(1)}, u32[]{:S(2)}, u32[]{:S(2)}) collective-permute-start(bf16[1,1,1024]{2,0,1:T(2,128)(2,1)S(1)} %get-tuple-element.97), channel_id=1, source_target_pairs={{0,1},{1,0},{2,3},{3,2},{4,5},{5,4},{6,7},{7,6},{8,9},{9,8},{10,11... | collective-permute-start | bytes 6152 | tf_op jit(solution)/shard_map/ppermute | solution.py:1223
  172.1 6.0 copy-start.11
  172.1 6.6 copy-start.12
  172.2 7.2 %collective-permute-start.1 = (bf16[1,1,1024]{2,0,1:T(2,128)(2,1)S(1)}, bf16[1,1,1024]{2,0,1:T(2,128)(2,1)S(1)}, u32[]{:S(2)}, u32[]{:S(2)}) collective-permute-start(bf16[1,1,1024]{2,0,1:T(2,128)(2,1)S(1)} %collective-permute-done), channel_id=1, source_target_pairs={{0,2},{2,0},{4,6},{6,4},{8,10},{10,8},{12,14},{14,12},{16,18},{18,... | collective-permute-start | bytes 6152 | tf_op jit(solution)/shard_map/ppermute | solution.py:1226
  320.3 69.7 %collective-permute-start.4 = (bf16[1280,1024]{1,0:T(8,128)(2,1)}, bf16[1280,1024]{1,0:T(8,128)(2,1)S(1)}, u32[]{:S(2)}, u32[]{:S(2)}) collective-permute-start(bf16[1280,1024]{1,0:T(8,128)(2,1)} %get-tuple-element.60), channel_id=1, source_target_pairs={{0,1},{1,0},{2,3},{3,2},{4,5},{5,4},{6,7},{7,6},{8,9},{9,8},{10,11... | collective-permute-start | bytes 7864328 | tf_op jit(solution)/shard_map/ppermute | solution.py:1223
  379.6 5.6 collective-permute-start.3
  381.1 9.0 %collective-permute-start.5 = (bf16[512,1024]{1,0:T(8,128)(2,1)}, bf16[512,1024]{1,0:T(8,128)(2,1)}, u32[]{:S(2)}, u32[]{:S(2)}) collective-permute-start(bf16[512,1024]{1,0:T(8,128)(2,1)} %get-tuple-element.61.normed_ref), channel_id=1, source_target_pairs={{0,2},{2,0},{4,6},{6,4},{8,10},{10,8},{12,14},{14,12},{16,18},{18,... | collective-permute-start | bytes 3145736 | tf_op jit(solution)/shard_map/ppermute | solution.py:1226
  390.1 1.5 copy-start.5
  627.1 5.2 copy-start.4
  634.8 4.0 copy-start.9
  645.2 6.3 copy-start.1
  655.7 1.8 copy-start.2
  655.7 2.6 copy-start.3
  658.4 4.4 copy-start.7
  661.6 2.2 copy-start.6

commit v5 on v4

--- a/solution.py
+++ b/solution.py
@@ -17,6 +17,7 @@
 UNROLL = 4
 CHUNK_ROWS = 256
 FIRST_TICKS = 6
+SLACK = 1
 VMEM_LIMIT = 58 << 20
 VMEM_MIDDLE = 62 << 20
 
@@ -206,7 +207,7 @@
     def finish(b, carry):
         dq_ref[b] = pack_t(dqt_s[b] * scale).astype(BF16)
         base = tab[4, b] * BLK
-        mine_ref[b] = dkv[pl.ds(pl.multiple_of(base + part * HALF, HALF), HALF), :]
+        mine_ref[b] = dkv[pl.ds(pl.multiple_of(base + part * HALF, HALF), HALF), :].astype(BF16)
         theirs_ref[b] = dkv[pl.ds(pl.multiple_of(base + (1 - part) * HALF, HALF), HALF), :].astype(BF16)
         return carry
 
@@ -252,7 +253,7 @@
         attend_back_kernel,
         out_shape=(
             jax.ShapeDtypeStruct((blocks, QUART, 2 * HEAD), BF16),
-            jax.ShapeDtypeStruct((blocks, HALF, 2 * HEAD), F32),
+            jax.ShapeDtypeStruct((blocks, HALF, 2 * HEAD), BF16),
             jax.ShapeDtypeStruct((blocks, HALF, 2 * HEAD), BF16),
         ),
         in_specs=smem(2) + vmem(8),
@@ -318,7 +319,7 @@
         self.z = self.seq // 4
         self.core_partner = (self.seq ^ 1, self.tp)
         self.x_partner = (self.seq ^ 2, self.tp)
-        self.z_partners = [(self.seq ^ (4 * d), self.tp) for d in (1, 2, 3)]
+        self.z_partners = [(self.seq ^ (4 * d), self.tp) for d in (1, 2)]
         self.tp_partner = (self.seq, self.tp ^ 1)
 
 
@@ -358,10 +359,11 @@
     return pl.ds(pl.multiple_of(start, size), size)
 
 
-def reduce_stages(place, chunks, base, out, sib, xbuf, xsum, zbuf, sems, arrived):
+def reduce_stages(place, chunks, base, out, both, kept, xbuf, xsum, zbuf, zsum, fbuf, sems, arrived):
     rows = base.shape[0] // chunks
     half, piece = rows // 2, rows // 8
-    x, z = place.x, place.z
+    x, odd, upper = place.x, lax.rem(place.z, 2), place.z // 2
+    pair = half // 2
 
     def x_copy(k):
         return remote(
@@ -369,20 +371,34 @@
             sems["xs"].at[k], sems["xr"].at[k], place.x_partner,
         )
 
-    def z_copy(k, d):
+    def z_copy(k):
         return remote(
-            xsum.at[rows_at(k * half + (z ^ d) * piece, piece)],
-            zbuf.at[d - 1, rows_at(k * piece, piece)],
-            sems["zs"].at[d - 1, k], sems["zr"].at[d - 1, k], place.z_partners[d - 1],
-        )
+            xsum.at[rows_at(k * half + (1 - odd) * pair, pair)], zbuf.at[rows_at(k * pair, pair)],
+            sems["zs"].at[0, k], sems["zr"].at[0, k], place.z_partners[0],
+        )
+
+    def far_z_copy(k):
+        return remote(
+            zsum.at[rows_at(k * pair + (1 - upper) * piece, piece)], fbuf.at[rows_at(k * piece, piece)],
+            sems["zs"].at[1, k], sems["zr"].at[1, k], place.z_partners[1],
+        )
+
+    def own_pair(k):
+        return rows_at(k * rows + x * half + odd * pair, pair)
 
     def own_piece(k):
-        return rows_at(k * rows + x * half + z * piece, piece)
-
-    def zg_copy(k, d):
+        return rows_at(k * rows + x * half + odd * pair + upper * piece, piece)
+
+    def far_zg_copy(k):
         return remote(
             out.at[own_piece(k)], out.at[own_piece(k)],
-            sems["zgs"].at[d - 1, k], sems["zgr"].at[d - 1, k], place.z_partners[d - 1],
+            sems["zgs"].at[1, k], sems["zgr"].at[1, k], place.z_partners[1],
+        )
+
+    def zg_copy(k):
+        return remote(
+            out.at[own_pair(k)], out.at[own_pair(k)],
+            sems["zgs"].at[0, k], sems["zgr"].at[0, k], place.z_partners[0],
         )
 
     def xg_copy(k):
@@ -391,7 +407,7 @@
 
     def core_copy(k):
         span = rows_at(k * rows, rows)
-        return remote(out.at[span], sib.at[span], sems["cs"].at[k], sems["cr"].at[k], place.core_partner)
+        return remote(out.at[span], both.at[1, span], sems["cs"].at[k], sems["cr"].at[k], place.core_partner)
 
     def stage_x(k):
         arrived(k)
@@ -403,45 +419,59 @@
         xsum[rows_at(k * half, half), :] = (
             mine + xbuf[rows_at(k * half, half), :].astype(F32)
         ).astype(BF16)
-        for d in (3, 2, 1):
-            z_copy(k, d).start()
+        z_copy(k).start()
+
+    def stage_far_z(k):
+        z_copy(k).wait_recv()
+        span = rows_at(k * pair, pair)
+        zsum[span, :] = (
+            xsum[rows_at(k * half + odd * pair, pair), :].astype(F32) + zbuf[span, :].astype(F32)
+        ).astype(BF16)
+        far_z_copy(k).start()
+
+    def stage_far_zg(k):
+        far_z_copy(k).wait_recv()
+        out[own_piece(k), :] = (
+            zsum[rows_at(k * pair + upper * piece, piece), :].astype(F32)
+            + fbuf[rows_at(k * piece, piece), :].astype(F32)
+        ).astype(BF16)
+        far_zg_copy(k).start()
 
     def stage_zg(k):
-        total = xsum[rows_at(k * half + z * piece, piece), :].astype(F32)
-        for d in (1, 2, 3):
-            z_copy(k, d).wait_recv()
-            total = total + zbuf[d - 1, rows_at(k * piece, piece), :].astype(F32)
-        out[own_piece(k), :] = total.astype(BF16)
-        for d in (3, 2, 1):
-            zg_copy(k, d).start()
+        far_zg_copy(k).wait_recv()
+        zg_copy(k).start()
 
     def stage_xg(k):
-        for d in (1, 2, 3):
-            zg_copy(k, d).wait_recv()
+        zg_copy(k).wait_recv()
         xg_copy(k).start()
 
     def stage_core(k):
         xg_copy(k).wait_recv()
         core_copy(k).start()
 
-    stages = [stage_x, stage_z, stage_zg, stage_xg, stage_core]
+    stages = [stage_x, stage_z, stage_far_z, stage_far_zg, stage_zg, stage_xg, stage_core]
 
     def tick(t):
         for s, stage in reversed(list(enumerate(stages))):
-            @pl.when((t >= s) & (t - s < chunks))
+            k = t - SLACK * s
+
+            @pl.when((k >= 0) & (k < chunks))
             def _():
-                stage(t - s)
+                stage(k)
 
     def drain(k, carry):
-        x_copy(k).wait_send()
-        for d in (1, 2, 3):
-            z_copy(k, d).wait_send()
-            zg_copy(k, d).wait_send()
-        xg_copy(k).wait_send()
+        for copy in (x_copy, z_copy, far_z_copy, far_zg_copy, zg_copy, xg_copy):
+            copy(k).wait_send()
         core_copy(k).wait()
         return carry
 
-    return tick, lambda: lax.fori_loop(0, chunks, drain, 0), chunks + len(stages) - 1
+    def finale():
+        keep = pltpu.make_async_copy(out, both.at[0], kept)
+        keep.start()
+        lax.fori_loop(0, chunks, drain, 0)
+        keep.wait()
+
+    return tick, finale, chunks + SLACK * (len(stages) - 1)
 
 
 SEM_NAMES = ("xs", "xr", "zs", "zr", "zgs", "zgr", "xgs", "xgr", "cs", "cr")
@@ -449,10 +479,11 @@
 
 
 def finish_kernel(
-    chunks, first_ticks, gain_ref, dq_ref, dkv_ref, near_ref, far_ref, normed_ref, normed_sib_ref, x_ref, dh_ref,
-    w0, w1, w2, w3, vec_ref, out, sib, gx_ref, vec_out,
-    base, far, ybuf, xbuf, xsum, zbuf, dq_in, dkv_in, mixed, mixed_sib, normed, normed_sib, x_s, dh_s, w_s, slots,
-    *rest,
+    chunks, first_ticks, gain_ref, dq_ref, mine_ref, theirs_ref, near_ref, far_up_ref, far_ref,
+    normed_ref, normed_sib_ref, x_ref, dh_ref, w_ref, w2, w3, vec_ref,
+    both, gx_ref, vec_out,
+    out, base, far, ybuf, xbuf, xsum, zbuf, zsum, fbuf, dq_in, dkv_in, dkv_st, dkv_sib, mixed, mixed_sib,
+    normed, normed_sib, x_s, w_s, slots, *rest,
 ):
     place = Place()
     count = dq_ref.shape[0]
@@ -460,62 +491,80 @@
     who = (place.tp, lax.rem(place.seq, 2))
     sems = dict(zip(SEM_NAMES, rest))
     qs, qr, ks, kr, ys, yr, ms, mr, vs, vr, loc = rest[len(SEM_NAMES) :]
+    rows = base.shape[0] // chunks
     early = near_ref.shape[0]
-    rows = base.shape[0] // chunks
+    crossed = far_up_ref.shape[0] // rows
+    greet_all(count, me, place.seq, place.tp)
+    dkv_pair = remote(theirs_ref, dkv_sib, ms.at[2], mr.at[2], place.core_partner)
+    dkv_pair.start()
+    mine_copy = pltpu.make_async_copy(mine_ref, dkv_st, loc.at[0])
+    mine_copy.start()
+
+    def dq_copy(k):
+        return chunk_copy(count, me, k, dq_ref, dq_in, qs, qr)
+
+    def dkv_copy(k):
+        return chunk_copy(count, me, k, dkv_st, dkv_in, ks, kr)
+
+    def start_q(k, carry):
+        dq_copy(k).start()
+        return carry
+
+    lax.fori_loop(1, count, start_q, 0)
+    near_copy = pltpu.make_async_copy(near_ref, base.at[pl.ds(0, early)], loc.at[1])
+    near_copy.start()
+    far_copy = pltpu.make_async_copy(far_up_ref, ybuf.at[pl.ds(0, far_up_ref.shape[0])], loc.at[2])
+    far_copy.start()
+    locals_ = [(dq_ref.at[me], dq_in.at[me]), (normed_ref, normed), (normed_sib_ref, normed_sib)]
+    locals_ += [(x_ref, x_s), (dh_ref, gx_ref)]
+    col = w_s.shape[3]
+    halves = [w_ref.at[:, :, rows_at(c * col, col)] for c in (who[1], 1 - who[1])]
+    locals_ += [(w, w_s.at[r]) for r, w in enumerate(halves + [w2, w3])]
+    locals_ = [pltpu.make_async_copy(src, dst, loc.at[3 + i]) for i, (src, dst) in enumerate(locals_)]
+
+    def tp_copy(k, src, first):
+        return remote(
+            src.at[rows_at((k - first) * rows, rows)], ybuf.at[rows_at(k * rows, rows)],
+            ys.at[k], yr.at[k], place.tp_partner,
+        )
+
+    def cross(k, carry):
+        tp_copy(k, far_ref, crossed).start()
+        return carry
+
     settled = early // rows
-    crossed = far_ref.shape[0]
-    summed = (early - crossed) // rows
-    greet_all(count, me, place.seq, place.tp)
-
-    near_copy = pltpu.make_async_copy(near_ref, base.at[pl.ds(0, early)], loc.at[0])
-    near_copy.start()
-    far_copy = pltpu.make_async_copy(far_ref, ybuf.at[pl.ds(0, crossed)], loc.at[11])
-    far_copy.start()
-
-    def start(k, carry):
-        chunk_copy(count, me, k, dkv_ref, dkv_in, ks, kr).start()
-        chunk_copy(count, me, k, dq_ref, dq_in, qs, qr).start()
-        return carry
-
-    lax.fori_loop(1, count, start, 0)
-    locals_ = [
-        pltpu.make_async_copy(src, dst, loc.at[1 + i])
-        for i, (src, dst) in enumerate(
-            [
-                (dq_ref.at[me], dq_in.at[me]),
-                (dkv_ref.at[me], dkv_in.at[me]),
-                (normed_ref, normed),
-                (normed_sib_ref, normed_sib),
-                (x_ref, x_s),
-                (dh_ref, dh_s),
-            ]
-            + [(w.at[pl.ds(0, w_s.shape[1])], w_s.at[r]) for r, w in enumerate((w0, w1, w2, w3))]
-        )
-    ]
+    lax.fori_loop(crossed, settled, cross, 0)
+    mine_copy.wait()
+    dkv_pair.wait()
+
+    def add(b, carry):
+        dkv_st[b] = (dkv_st[b].astype(F32) + dkv_sib[b].astype(F32)).astype(BF16)
+        return carry
+
+    lax.fori_loop(0, count, add, 0)
+
+    def start_kv(k, carry):
+        dkv_copy(k).start()
+        return carry
+
+    lax.fori_loop(1, count, start_kv, 0)
+    dkv_in[me] = dkv_st[me]
     near_copy.wait()
     far_copy.wait()
     for copy in locals_:
         copy.start()
 
-    def tp_copy(k):
-        return remote(
-            far.at[rows_at(k * rows, rows)], ybuf.at[rows_at(crossed + k * rows, rows)],
-            ys.at[k], yr.at[k], place.tp_partner,
-        )
-
     def arrived(k):
-        @pl.when(k >= settled)
+        @pl.when(k >= crossed)
         def _():
-            tp_copy(k - settled).wait_recv()
-
-        @pl.when(k >= summed)
-        def _():
-            span = rows_at(k * rows, rows)
-            base[span, :] = (
-                base[span, :].astype(F32) + ybuf[rows_at((k - summed) * rows, rows), :].astype(F32)
-            ).astype(BF16)
-
-    tick, drain, ticks = reduce_stages(place, chunks, base, out, sib, xbuf, xsum, zbuf, sems, arrived)
+            tp_copy(k, base, 0).wait_recv()
+
+        span = rows_at(k * rows, rows)
+        base[span, :] = (base[span, :].astype(F32) + ybuf[span, :].astype(F32)).astype(BF16)
+
+    tick, drain, ticks = reduce_stages(
+        place, chunks, base, out, both, loc.at[12], xbuf, xsum, zbuf, zsum, fbuf, sems, arrived
+    )
 
     def plain(t, carry):
         tick(t)
@@ -524,8 +573,8 @@
     lax.fori_loop(0, first_ticks, plain, 0)
 
     def wait(k, carry):
-        chunk_copy(count, me, k, dkv_ref, dkv_in, ks, kr).wait()
-        chunk_copy(count, me, k, dq_ref, dq_in, qs, qr).wait()
+        dq_copy(k).wait()
+        dkv_copy(k).wait()
         return carry
 
     lax.fori_loop(1, count, wait, 0)
@@ -554,9 +603,9 @@
     for quarter in range(4):
         absolute = (who[0] * 2 + who[1]) ^ quarter
         lanes = pl.ds(pl.multiple_of(absolute * 256, 256), 256)
-        for row, col in ((10, 0), (11, 512)):
+        for row, left in ((10, 0), (11, 512)):
             vec_out[row : row + 1, lanes] = jnp.sum(
-                mixed[quarter, :, col : col + 256].astype(F32), axis=0, keepdims=True
+                mixed[quarter, :, left : left + 256].astype(F32), axis=0, keepdims=True
             )
     gains = jnp.zeros((1, base.shape[1]), F32)
     shifts = jnp.zeros((1, base.shape[1]), F32)
@@ -564,17 +613,17 @@
         span = slice(part * HALF, part * HALF + HALF)
         d_normed = jnp.zeros((HALF, base.shape[1]), F32)
         for quarter in range(4):
-            d_normed += lax.dot_general(
-                mixed[quarter, span, :], w_s[quarter], (((1,), (1,)), ((), ())), preferred_element_type=F32
-            )
+            for which in range(3):
+                lanes = slice(which * col, which * col + col)
+                d_normed += dot_nt(mixed[quarter, span, lanes], w_s[quarter, which])
         xhat, rstd = norm_parts(x_s[span, :].astype(F32))
-        e = d_normed * gain_ref[...]
+        e = d_normed * gain_ref[0:1, :]
         grad = rstd * (
             e
             - jnp.mean(e, axis=-1, keepdims=True)
             - xhat * jnp.mean(e * xhat, axis=-1, keepdims=True)
         )
-        gx_ref[span, :] = dh_s[span, :] + grad
+        gx_ref[span, :] += grad
         gains += jnp.sum(d_normed * xhat, axis=0, keepdims=True)
         shifts += jnp.sum(d_normed, axis=0, keepdims=True)
         tick(first_ticks + 1 + part)
@@ -585,8 +634,8 @@
         copy.wait()
     late = pl.ds(early, base.shape[0] - early)
     for i, target in ((1, far), (0, base.at[late])):
-        for col in range(0, target.shape[0], 256):
-            span = slice(col, col + 256)
+        for row in range(0, target.shape[0], 256):
+            span = slice(row, row + 256)
             target[span, :] = (
                 lax.dot_general(
                     mixed[2 * i, :, span], normed[...], (((0,), (0,)), ((), ())), preferred_element_type=F32
@@ -597,7 +646,8 @@
                 )
             ).astype(BF16)
             if i == 1:
-                tp_copy(col // rows).start()
+                for k in range(settled + row // rows, settled + (row + 256) // rows):
+                    tp_copy(k, far, settled).start()
 
     partners = [place.core_partner, place.tp_partner, place.x_partner] + [
         (place.seq ^ bit, place.tp) for bit in (4, 8)
@@ -623,77 +673,117 @@
     lax.fori_loop(first_ticks + 3, ticks, last, 0)
 
     def sent(k, carry):
-        tp_copy(k).wait_send()
-        return carry
-
-    lax.fori_loop(0, chunks - settled, sent, 0)
+        tp_copy(k, base, 0).wait_send()
+        return carry
+
+    lax.fori_loop(crossed, chunks, sent, 0)
     drain()
 
 
-def finish(gain, dq_chunks, dkv_chunks, near, far, normed, normed_sib, x, d_hidden, weights, vectors):
+def finish(gain, dq_chunks, mine, theirs, near, far_up, far, normed, normed_sib, x, d_hidden, weights, vectors):
     early, cols = near.shape
-    late = weights[0].shape[1]
+    late = 3 * weights[1].shape[2]
     total = early + late
     chunks = total // CHUNK_ROWS
-    late_chunks = late // CHUNK_ROWS
     count = dq_chunks.shape[0]
     rows = x.shape[0]
     dma = pltpu.SemaphoreType.DMA
     anywhere = pl.BlockSpec(memory_space=pl.ANY)
     scratch = [
         pltpu.VMEM((total, cols), BF16),
+        pltpu.VMEM((total, cols), BF16),
         pltpu.VMEM((late, cols), BF16),
-        pltpu.VMEM((far.shape[0] + late, cols), BF16),
+        pltpu.VMEM((total, cols), BF16),
         pltpu.VMEM((total // 2, cols), BF16),
         pltpu.VMEM((total // 2, cols), BF16),
-        pltpu.VMEM((3, total // 8, cols), BF16),
+        pltpu.VMEM((total // 4, cols), BF16),
+        pltpu.VMEM((total // 4, cols), BF16),
+        pltpu.VMEM((total // 8, cols), BF16),
         pltpu.VMEM(dq_chunks.shape, BF16),
-        pltpu.VMEM(dkv_chunks.shape, BF16),
+        pltpu.VMEM(mine.shape, BF16),
+        pltpu.VMEM(mine.shape, BF16),
+        pltpu.VMEM(mine.shape, BF16),
         pltpu.VMEM((4, rows, late), BF16),
         pltpu.VMEM((2, rows, late), BF16),
         pltpu.VMEM((rows, cols), BF16),
         pltpu.VMEM((rows, cols), BF16),
         pltpu.VMEM((rows, cols), BF16),
-        pltpu.VMEM((rows, cols), F32),
-        pltpu.VMEM((4, cols, late), BF16),
+        pltpu.VMEM((4,) + weights[1].shape, BF16),
         pltpu.VMEM((2 * VECTOR_STEPS,) + vectors.shape, F32),
     ]
-    scratch += [dma((3, chunks) if name[0] == "z" else (chunks,)) for name in SEM_NAMES]
-    scratch += [dma((count,))] * 4 + [dma((late_chunks,))] * 2 + [dma((2,))] * 2
-    scratch += [dma((VECTOR_STEPS,))] * 2 + [dma((12,))]
+    scratch += [dma((2, chunks) if name[0] == "z" else (chunks,)) for name in SEM_NAMES]
+    scratch += [dma((count,))] * 4 + [dma((chunks,))] * 2 + [dma((3,))] * 2
+    scratch += [dma((VECTOR_STEPS,))] * 2 + [dma((13,))]
     return pl.pallas_call(
         functools.partial(finish_kernel, chunks, FIRST_TICKS),
         out_shape=(
-            jax.ShapeDtypeStruct((total, cols), BF16),
-            jax.ShapeDtypeStruct((total, cols), BF16),
+            jax.ShapeDtypeStruct((2, total, cols), BF16),
             jax.ShapeDtypeStruct((rows, cols), F32),
             jax.ShapeDtypeStruct(vectors.shape, F32),
         ),
-        in_specs=vmem(1) + [anywhere] * 12 + vmem(1),
-        out_specs=(vmem(1)[0], anywhere, vmem(1)[0], vmem(1)[0]),
+        in_specs=vmem(1) + [anywhere] * 13 + vmem(1),
+        out_specs=(anywhere, vmem(1)[0], vmem(1)[0]),
         scratch_shapes=scratch,
         compiler_params=pltpu.CompilerParams(
-            collective_id=1, has_side_effects=True, vmem_limit_bytes=VMEM_LIMIT
+            collective_id=1, has_side_effects=True, vmem_limit_bytes=VMEM_MIDDLE
         ),
         name="finish",
-    )(gain, dq_chunks, dkv_chunks, near, far, normed, normed_sib, x, d_hidden, *weights, vectors)
+    )(
+        gain, dq_chunks, mine, theirs, near, far_up, far, normed, normed_sib, x, d_hidden, *weights, vectors
+    )
+
+
+def join_kernel(core_ref, in_ref, out_ref):
+    out_ref[...] = in_ref[0].astype(F32)
+
+
+def join_turned_kernel(core_ref, in_ref, out_ref):
+    out_ref[0] = in_ref[0].astype(F32).T
+
+
+def join(core, both, size, first, count, shape, place, turned=False):
+    cols = both.shape[2]
+    block = (1, cols, size) if turned else (size, cols)
+    return pl.pallas_call(
+        join_turned_kernel if turned else join_kernel,
+        grid_spec=pltpu.PrefetchScalarGridSpec(
+            num_scalar_prefetch=1,
+            grid=(2, count),
+            in_specs=[pl.BlockSpec((1, size, cols), lambda p, i, c: ((p + c[0]) % 2, first + i, 0))],
+            out_specs=pl.BlockSpec(block, lambda p, i, c: place(p, i)),
+        ),
+        out_shape=jax.ShapeDtypeStruct(shape, F32),
+        compiler_params=pltpu.CompilerParams(vmem_limit_bytes=VMEM_LIMIT),
+        name="join",
+    )(core.reshape(1).astype(jnp.int32), both)
 
 
 def begin_kernel(
-    x_ref, gain_ref, shift_ref, w0, w1, wo_ref,
-    normed_ref, q_in, kv_own, kv_sib, w2, w3, wo2, wo3,
-    q_st, kv_st, *sems,
+    x_ref, gain_ref, shift_ref, bias_ref, w_ref, wo_ref,
+    normed_ref, normed_sib, q_in, kv_own, kv_sib, bias_far, w2, w3, wo2, wo3,
+    w0, w1, q_st, kv_st, *sems,
 ):
     place = Place()
     count = q_in.shape[0]
     width = x_ref.shape[1]
     me = place.seq * 2 + place.tp
     who = (place.tp, lax.rem(place.seq, 2))
-    ks, kr, qs, qr, fs, fr, ws, wr = sems
+    ks, kr, qs, qr, fs, fr, ws, wr, ls = sems
     greet_all(count, me, place.seq, place.tp)
-    w_far = remote(w0, w2, ws.at[0], wr.at[0], place.tp_partner)
+    core = who[1]
+    col, wo_rows = w0.shape[2], wo2.shape[0]
+    w_own = w_ref.at[:, :, rows_at(core * col, col)]
+    w_far = remote(w_own, w2, ws.at[0], wr.at[0], place.tp_partner)
     w_far.start()
-    wo_far = remote(wo_ref, wo2, ws.at[1], wr.at[1], place.tp_partner)
+    bias_pair = remote(bias_ref, bias_far, ws.at[5], wr.at[5], place.tp_partner)
+    bias_pair.start()
+    w_loads = [
+        pltpu.make_async_copy(w_own, w0, ls.at[0]),
+        pltpu.make_async_copy(w_ref.at[:, :, rows_at((1 - core) * col, col)], w1, ls.at[1]),
+    ]
+    for copy in w_loads:
+        copy.start()
+    wo_far = remote(wo_ref.at[rows_at(core * wo_rows, wo_rows)], wo2, ws.at[1], wr.at[1], place.tp_partner)
     wo_far.start()
     w_last = remote(w2, w3, ws.at[2], wr.at[2], place.core_partner)
     wo_last = remote(wo2, wo3, ws.at[3], wr.at[3], place.core_partner)
@@ -701,11 +791,14 @@
     def norm(part, carry):
         span = rows_at(part * 64, 64)
         normed_ref[span, :] = layer_norm(
-            x_ref[span, :].astype(F32), gain_ref[...], shift_ref[...]
+            x_ref[span, :].astype(F32), gain_ref[0:1, :], shift_ref[0:1, :]
         ).astype(BF16)
         return carry
 
     lax.fori_loop(0, x_ref.shape[0] // 64, norm, 0)
+
+    normed_pair = remote(normed_ref, normed_sib, ws.at[4], wr.at[4], place.core_partner)
+    normed_pair.start()
 
     def kv_copy(other):
         return remote(kv_st.at[other], kv_own.at[me], ks.at[other], kr.at[me], (other // 2, lax.rem(other, 2)))
@@ -725,13 +818,16 @@
     low = low_lanes(HALF)
 
     def project(quarter, w):
-        def dot(col):
-            return (
-                jnp.dot(normed_ref[...], w[:width, col : col + 256], preferred_element_type=F32)
-                + w[width : width + 1, col : col + 256].astype(F32)
-            )
-
-        keys, values = dot(256), dot(512)
+        bias = bias_ref if quarter < 2 else bias_far
+        side = core if quarter % 2 == 0 else 1 - core
+
+        def bias_at(which):
+            return bias[2:3, rows_at(which * 2 * col + side * col, col)]
+
+        def dot(which):
+            return dot_nn(normed_ref[...], w[which])
+
+        keys, values = dot(1), dot(2) + bias_at(1)
         for pair in range(2):
             lanes = slice(pair * 128, pair * 128 + 128)
             for half in range(2):
@@ -739,7 +835,7 @@
                 k, v = keys[rows, lanes], values[rows, lanes]
                 kv_st[chunk_of(who, quarter, 2 * pair, half)] = jnp.where(low, k, swap_lanes(v)).astype(BF16)
                 kv_st[chunk_of(who, quarter, 2 * pair + 1, half)] = jnp.where(low, swap_lanes(k), v).astype(BF16)
-        store_packed(who, quarter, dot(0), q_st)
+        store_packed(who, quarter, dot(0) + bias_at(0), q_st)
 
         def send(i, carry):
             other = chunk_of(who, quarter, i // 2, lax.rem(i, 2))
@@ -758,9 +854,12 @@
 
         lax.fori_loop(0, 8, send, 0)
 
+    for copy in w_loads:
+        copy.wait()
     project(0, w0)
     project(1, w1)
     w_far.wait()
+    bias_pair.wait()
     w_last.start()
     project(2, w2)
     w_last.wait()
@@ -794,36 +893,43 @@
 
     lax.fori_loop(0, count, forwarded, 0)
     wo_last.wait()
-
-
-def begin(x, gain, shift, w0, w1, wo0):
+    normed_pair.wait()
+
+
+def begin(x, gains, shifts, bias, w, wo):
     rows, width = x.shape
     count = 32
     dma = pltpu.SemaphoreType.DMA
     anywhere = pl.BlockSpec(memory_space=pl.ANY)
     q_shape, kv_shape = (count, QUART, 2 * HEAD), (count, HALF, 2 * HEAD)
+    w_quarter = (3, width, w.shape[2] // 2)
+    wo_quarter = (wo.shape[0] // 2, wo.shape[1])
     return pl.pallas_call(
         begin_kernel,
         out_shape=(
             jax.ShapeDtypeStruct((rows, width), BF16),
+            jax.ShapeDtypeStruct((rows, width), BF16),
             jax.ShapeDtypeStruct(q_shape, BF16),
             jax.ShapeDtypeStruct(kv_shape, BF16),
             jax.ShapeDtypeStruct(kv_shape, BF16),
-            jax.ShapeDtypeStruct(w0.shape, BF16),
-            jax.ShapeDtypeStruct(w0.shape, BF16),
-            jax.ShapeDtypeStruct(wo0.shape, BF16),
-            jax.ShapeDtypeStruct(wo0.shape, BF16),
+            jax.ShapeDtypeStruct(bias.shape, F32),
+            jax.ShapeDtypeStruct(w_quarter, BF16),
+            jax.ShapeDtypeStruct(w_quarter, BF16),
+            jax.ShapeDtypeStruct(wo_quarter, BF16),
+            jax.ShapeDtypeStruct(wo_quarter, BF16),
         ),
-        in_specs=vmem(5) + [anywhere],
-        out_specs=tuple(vmem(6) + [anywhere] * 2),
-        scratch_shapes=[pltpu.VMEM(q_shape, BF16), pltpu.VMEM(kv_shape, BF16)]
+        in_specs=vmem(4) + [anywhere] * 2,
+        out_specs=tuple(vmem(1) + [anywhere] + vmem(6) + [anywhere] * 2),
+        scratch_shapes=[pltpu.VMEM(w_quarter, BF16)] * 2
+        + [pltpu.VMEM(q_shape, BF16), pltpu.VMEM(kv_shape, BF16)]
         + [dma((count,))] * 6
-        + [dma((4,))] * 2,
+        + [dma((6,))] * 2
+        + [dma((2,))],
         compiler_params=pltpu.CompilerParams(
             collective_id=3, has_side_effects=True, vmem_limit_bytes=VMEM_LIMIT
         ),
         name="begin",
-    )(x, gain, shift, w0, w1, wo0)
+    )(x, gains, shifts, bias, w, wo)
 
 
 def norm_parts(values):
@@ -868,12 +974,12 @@
 
 
 def middle_kernel(
-    gains, shifts, bias_out, bias_down, bias_up, att_ref, x_ref, og_ref,
-    wo0, wo1, wo2, wo3, wu0, wu1, wu2, wd0, wd1,
-    result, da_in, dh, vec, near_ref, far_ref,
+    gains, shifts, bias_out, bias_down, bias_own, bias_far, att_ref, x_ref, og_ref,
+    wo_ref, wo2, wo3, wu_ref, wu2, wd_ref,
+    result, da_in, dh, vec, near_ref, far_up_ref, far_ref,
     att_in, att_s, att_sib, wo_s, wu_s, wd_s, x_s, branch_s, hidden_s, inner_s, inner_sib, act_s, act_sib,
-    dg_s, dup_sib, down_s, dd_s, dd_sib, db_s, db_sib, da_st, fd_s, fd_in,
-    ats, atr, das, dar, ws, wr, cs, cr, fs, fr, loc,
+    dg_s, dup_sib, down_s, dd_s, dd_sib, db_s, db_sib, da_st,
+    ats, atr, das, dar, ws, wr, cs, cr, loc,
 ):
     place = Place()
     count = att_in.shape[0]
@@ -881,6 +987,9 @@
     who = (place.tp, lax.rem(place.seq, 2))
     rows, width = x_s.shape
     hid = wd_s.shape[1]
+    wu0, wu1 = (wu_ref.at[:, rows_at(c * hid, hid)] for c in (who[1], 1 - who[1]))
+    wo0, wo1 = (wo_ref.at[rows_at(c * wo2.shape[0], wo2.shape[0])] for c in (who[1], 1 - who[1]))
+    wd0, wd1 = (wd_ref.at[rows_at(c * hid, hid)] for c in (who[1], 1 - who[1]))
     greet_all(count, me, place.seq, place.tp)
 
     def start(k, carry):
@@ -952,10 +1061,13 @@
         if quarter == 3:
             wu_last.wait()
 
-        def up(i, carry, quarter=quarter):
+        bias = bias_own if quarter < 2 else bias_far
+        side = who[1] if quarter % 2 == 0 else 1 - who[1]
+
+        def up(i, carry, quarter=quarter, bias=bias, side=side):
             span = cols(i)
             act, slope = gelu_parts(
-                dot_nn(inner_s[...], wu_s[quarter, :, span]) + bias_up[quarter : quarter + 1, span]
+                dot_nn(inner_s[...], wu_s[quarter, :, span]) + bias[pl.ds(side, 1), span]
             )
             act_s[quarter, :, span] = act.astype(BF16)
             dg_s[quarter, :, span] = slope.astype(BF16)
@@ -1004,21 +1116,6 @@
     vec[7:8, :] = shift
     vec[9:10, :] = bias
     dd_pair.start()
-    act_pair[1].wait_recv()
-    dd_pair.wait_recv()
-
-    def far_copy(i):
-        return remote(fd_s.at[cols(i)], fd_in.at[cols(i)], fs.at[i], fr.at[i], place.tp_partner)
-
-    def far_down(i, carry):
-        span = cols(i)
-        fd_s[span, :] = (
-            dot_tn(act_s[2, :, span], dd_s[...]) + dot_tn(act_sib[1, :, span], dd_sib[...])
-        ).astype(BF16)
-        far_copy(i).start()
-        return carry
-
-    lax.fori_loop(0, hid // 256, far_down, 0)
     for quarter in range(4):
         absolute = (who[0] * 2 + who[1]) ^ quarter
 
@@ -1114,31 +1211,30 @@
         wo_s[near] = (dot_tn(att_s[near], db_s[...]) + dot_tn(att_sib[slot], db_sib[...])).astype(BF16)
     up_rows, out_rows = wu_s.shape[1], wo_s.shape[1]
     stores = [
-        (wu_s.at[0], near_ref.at[pl.ds(hid, up_rows)]),
-        (wo_s.at[0], near_ref.at[pl.ds(hid + up_rows, out_rows)]),
-        (wu_s.at[2], far_ref.at[pl.ds(0, up_rows)]),
-        (wo_s.at[2], far_ref.at[pl.ds(up_rows, out_rows)]),
+        (wu_s.at[0], near_ref.at[pl.ds(0, up_rows)]),
+        (wo_s.at[0], near_ref.at[pl.ds(up_rows + hid, out_rows)]),
+        (wu_s.at[2], far_up_ref),
+        (wo_s.at[2], far_ref.at[pl.ds(hid, out_rows)]),
+        (wd_s.at[0], near_ref.at[pl.ds(up_rows, hid)]),
+        (wd_s.at[2], far_ref.at[pl.ds(0, hid)]),
     ]
     stores = [pltpu.make_async_copy(src, dst, loc.at[i]) for i, (src, dst) in enumerate(stores)]
-    for copy in stores:
+    for copy in stores[:4]:
         copy.start()
-    act_pair[0].wait()
-    act_pair[1].wait_send()
-    dd_pair.wait_send()
-
-    def near_down(i, carry):
+    for copy in act_pair + [dd_pair]:
+        copy.wait()
+
+    def grad_down(i, carry):
         span = cols(i)
-        far_copy(i).wait()
-        wd_s[0, span, :] = (
-            dot_tn(act_s[0, :, span], dd_s[...])
-            + dot_tn(act_sib[0, :, span], dd_sib[...])
-            + fd_in[span, :].astype(F32)
-        ).astype(BF16)
-        return carry
-
-    lax.fori_loop(0, hid // 256, near_down, 0)
-    last = pltpu.make_async_copy(wd_s.at[0], near_ref.at[pl.ds(0, hid)], loc.at[4])
-    last.start()
+        for near, slot in ((0, 0), (2, 1)):
+            wd_s[near, span, :] = (
+                dot_tn(act_s[near, :, span], dd_s[...]) + dot_tn(act_sib[slot, :, span], dd_sib[...])
+            ).astype(BF16)
+        return carry
+
+    lax.fori_loop(0, hid // 256, grad_down, 0)
+    for copy in stores[4:]:
+        copy.start()
 
     def da_wait(k, carry):
         other = lax.rem(me + k, count)
@@ -1147,15 +1243,15 @@
         return carry
 
     lax.fori_loop(1, count, da_wait, 0)
-    for copy in stores + [last]:
+    for copy in stores:
         copy.wait()
 
 
-def middle(gains, shifts, bias_out, bias_down, bias_up, att, x, out_grad, wo4, wu3, wd2):
+def middle(gains, shifts, bias_out, bias_down, bias, bias_far, att, x, out_grad, wo3, w_up, wu2, w_down):
     rows, width = x.shape
     count = att.shape[0]
-    hid = wd2[0].shape[0]
-    out_rows = wo4[0].shape[0]
+    hid = wu2.shape[1]
+    out_rows = wo3[1].shape[0]
     dma = pltpu.SemaphoreType.DMA
     anywhere = pl.BlockSpec(memory_space=pl.ANY)
 
@@ -1184,10 +1280,8 @@
         held(rows, width),
         held(rows, width),
         held(*att.shape),
-        held(hid, width),
-        held(hid, width),
     ]
-    scratch += [dma((count,))] * 4 + [dma((3,))] * 2 + [dma((9,))] * 2 + [dma((4,))] * 2 + [dma((12,))]
+    scratch += [dma((count,))] * 4 + [dma((3,))] * 2 + [dma((9,))] * 2 + [dma((12,))]
     return pl.pallas_call(
         middle_kernel,
         out_shape=(
@@ -1196,16 +1290,19 @@
             jax.ShapeDtypeStruct((rows, width), F32),
             jax.ShapeDtypeStruct((16, width), F32),
             jax.ShapeDtypeStruct((hid + width + out_rows, width), BF16),
-            jax.ShapeDtypeStruct((width + out_rows, width), BF16),
+            jax.ShapeDtypeStruct((width, hid), BF16),
+            jax.ShapeDtypeStruct((hid + out_rows, width), BF16),
         ),
-        in_specs=vmem(5) + [anywhere] * 12,
-        out_specs=tuple(vmem(4) + [anywhere] * 2),
+        in_specs=vmem(6) + [anywhere] * 9,
+        out_specs=tuple(vmem(4) + [anywhere] * 3),
         scratch_shapes=scratch,
         compiler_params=pltpu.CompilerParams(
             collective_id=4, has_side_effects=True, vmem_limit_bytes=VMEM_MIDDLE
         ),
         name="middle",
-    )(gains, shifts, bias_out, bias_down, bias_up, att, x, out_grad, *wo4, *wu3, *wd2)
+    )(
+        gains, shifts, bias_out, bias_down, bias, bias_far, att, x, out_grad, *wo3, w_up, wu2, w_down
+    )
 
 
 def fast_local(
@@ -1215,82 +1312,41 @@
     seq_count = lax.axis_size("seq")
     seq, tp = lax.axis_index("seq"), lax.axis_index("tp")
     core = seq % 2
-    who = jnp.stack([tp, core]).astype(jnp.int32)
     over_tp = [(0, 1), (1, 0)]
-    over_core = [(i, i ^ 1) for i in range(seq_count)]
 
     def to_tp(values):
         return lax.ppermute(values, "tp", over_tp)
 
-    def to_sib(values):
-        return lax.ppermute(values, "seq", over_core)
-
-    def exchange(chunks):
-        return lax.all_to_all(chunks, ("seq", "tp"), 0, 0, tiled=True)
-
-    def quarters(values, axis):
-        size = values.shape[axis] // 2
-        own = lax.dynamic_slice_in_dim(values, core * size, size, axis)
-        sib = lax.dynamic_slice_in_dim(values, (1 - core) * size, size, axis)
-        far = to_tp(own)
-        return [own, sib, far, to_sib(far)]
-
     width = w_qkv.shape[0]
-
-    def halves(values, axis):
-        size = values.shape[axis] // 2
-        return [
-            lax.dynamic_slice_in_dim(values, which * size, size, axis) for which in (core, 1 - core)
-        ]
-
-    bias3 = jnp.stack([bias_qv[0], jnp.zeros_like(bias_qv[0]), bias_qv[1]])
-    bias3 = jnp.broadcast_to(bias3[None], (16,) + bias3.shape)
-    w_ext = jnp.concatenate([w_qkv, bias3])
-    wq0, wq1 = [w.reshape(w.shape[0], -1) for w in halves(w_ext, 2)]
-    wo0, wo1 = halves(w_out, 0)
-    bias_up4 = jnp.concatenate([b.astype(F32).reshape(1, -1) for b in quarters(bias_up.reshape(2, 1, -1), 0)])
-
+    w3 = jnp.transpose(w_qkv, (1, 0, 2))
+    bias = jnp.concatenate([bias_up.reshape(2, width), bias_qv.reshape(1, width)]).astype(F32)
+    bias = jnp.pad(bias, ((0, 5), (0, 0)))
     tables = block_tables(lengths, prefixes, placement, core)
-    normed, q_own, kv_own, kv_sib, wq2, wq3, wo2, wo3 = begin(
-        tokens_in, norm_gains[:1], norm_shifts[:1], wq0, wq1, wo0
-    )
-    wq4 = [wq0, wq1, wq2, wq3]
-    wo4 = [wo0, wo1, wo2, wo3]
-    w_up, w_down, normed = lax.optimization_barrier((w_up, w_down, normed))
-    wu0, wu1 = halves(w_up, 1)
-    wd0, wd1 = halves(w_down, 0)
-    wu2 = to_tp(wu0)
+    normed, normed_sib, q_own, kv_own, kv_sib, bias_far, wq2, wq3, wo2, wo3 = begin(
+        tokens_in, norm_gains, norm_shifts, bias, w3, w_out
+    )
+    w_up, normed = lax.optimization_barrier((w_up, normed))
+    half = w_up.shape[1] // 2
+    wu2 = to_tp(lax.dynamic_slice_in_dim(w_up, core * half, half, 1))
     att_chunks, out_t, mass, kv_pack, kv_turned = attend(core, tables, q_own, kv_own, kv_sib)
-    normed_sib = to_sib(normed)
-    result, da_own, d_hidden, vectors, near, far = middle(
-        norm_gains, norm_shifts, bias_out.astype(F32)[None], bias_down.astype(F32)[None], bias_up4,
-        att_chunks, tokens_in, out_grad, wo4, [wu0, wu1, wu2], [wd0, wd1],
-    )
-    far = to_tp(far)
-    dq_chunks, dkv_mine, dkv_theirs = attend_back(
-        core, tables, q_own, da_own, out_t, mass, kv_pack, kv_turned
-    )
-    dkv_chunks = (dkv_mine + to_sib(dkv_theirs).astype(F32)).astype(BF16)
-    sums, sums_sib, grad_x, vectors = finish(
-        norm_gains[:1], dq_chunks, dkv_chunks, near, far, normed, normed_sib, tokens_in, d_hidden, wq4, vectors
-    )
-
-    def joined(pair, axis):
-        own, sib = pair
-        first = jnp.concatenate([own, sib], axis=axis).astype(F32)
-        second = jnp.concatenate([sib, own], axis=axis).astype(F32)
-        return jnp.where(core == 0, first, second)
-
-    pair = (sums, sums_sib)
-    hidden_rows = wd0.shape[0]
-    up_end = hidden_rows + width
-    out_end = near.shape[0]
-
-    def rows_of(start, stop):
-        return [part[start:stop] for part in pair]
-
-    g_qkv = joined([part.reshape(3, -1, width) for part in rows_of(out_end, None)], 1)
-    g_qkv = jnp.transpose(g_qkv, (2, 0, 1))
+    result, da_own, d_hidden, vectors, near, far_up, far = middle(
+        norm_gains, norm_shifts, bias_out.astype(F32)[None], bias_down.astype(F32)[None], bias, bias_far,
+        att_chunks, tokens_in, out_grad, [w_out, wo2, wo3], w_up, wu2, w_down,
+    )
+    far_up = to_tp(far_up)
+    dq_chunks, mine, theirs = attend_back(core, tables, q_own, da_own, out_t, mass, kv_pack, kv_turned)
+    both, grad_x, vectors = finish(
+        norm_gains, dq_chunks, mine, theirs, near, far_up, far, normed, normed_sib, tokens_in, d_hidden,
+        [w3, wq2, wq3], vectors,
+    )
+    up, down, out = (n // 256 for n in (width, wu2.shape[1], wo2.shape[0]))
+    g_up = join(core, both, 512, 0, up // 2, w_up.shape, lambda p, i: (i, p))
+    g_down = join(core, both, 512, up // 2, down // 2, w_down.shape, lambda p, i: (p * (down // 2) + i, 0))
+    g_out = join(core, both, 256, up + down, out, w_out.shape, lambda p, i: (p * out + i, 0))
+    g_qkv = join(
+        core, both, 256, up + down + out, 3, (3, width, w_qkv.shape[2]), lambda p, i: (i, 0, p), turned=True
+    )
+    g_qkv = jnp.transpose(g_qkv, (1, 0, 2))
     own_cols = bias_qv.shape[1]
     grad_bias_qv = lax.dynamic_slice_in_dim(vectors[10:12], tp * own_cols, own_cols, 1)
     grad_bias_up = lax.dynamic_slice_in_dim(
@@ -1301,11 +1357,11 @@
         grad_x,
         g_qkv,
         grad_bias_qv,
-        joined(rows_of(up_end, out_end), 0),
+        g_out,
         vectors[8],
-        joined(rows_of(hidden_rows, up_end), 1),
+        g_up,
         grad_bias_up,
-        joined(rows_of(0, hidden_rows), 0),
+        g_down,
         vectors[9],
         vectors[0:4],
         vectors[4:8],

time: 677 us -> 584 us (0.86)
  local copies, waits for them, and re-layouts: 46.7 us -> 11.6 us
  other arithmetic: 26.9 us -> 3.23 us
  Pallas kernels: 580 us -> 559 us
    pallas_call x1, Pallas kernels: 140 us -> 118 us  [middle(): pl.pallas_call(middle_kernel, out_shape=(jax.ShapeDtypeStruct((rows, widt...]
    pallas_call x0 -> x4, Pallas kernels: none -> 20.6 us  [join(): pl.pallas_call(join_turned_kernel if turned else join_kernel, grid_spec=p...]
    slice x9 -> x0, local copies, waits for them, and re-layouts: 15.1 us -> none  [the longest x6 11.7 us: rows_of(): return [part[start:stop] for part in pair]]
    pallas_call x1, Pallas kernels: 236 us -> 223 us  [finish(): pl.pallas_call(functools.partial(finish_kernel, chunks, FIRST_TICKS), out...]
    select_n x3 -> x0, other arithmetic: 12.2 us -> none  [joined(): return jnp.where(core == 0, first, second)]
    dynamic_slice x5 -> x1, local copies, waits for them, and re-layouts: 13.4 us -> 1.78 us  [fast_local(): wu2 = to_tp(lax.dynamic_slice_in_dim(w_up, core * half, half, 1))]
    reshape x6 -> x1, local copies, waits for them, and re-layouts: 9.71 us -> 0.7 us  [fast_local(): bias_up.reshape(2, width)]
  transfers between devices with their start and end apart: 6 -> 2, of which waited for: 1 -> 0; matrix products, arithmetic and copies ran while one was open for 2% -> 1% of each run, Pallas kernels for 16% -> 18%
where the time goes in v5:
time: 584 us; the launch traced here: 577 us
  Pallas kernels  559 us (96%)
  local copies, waits for them, and re-layouts  11.6 us (2%)
    pallas_call x1, Pallas kernels, finish(): pl.pallas_call(functools.partial(finish_kernel, chunks, FIRST_TICKS), out...  223 us
    pallas_call x1, Pallas kernels, middle(): pl.pallas_call(middle_kernel, out_shape=(jax.ShapeDtypeStruct((rows, widt...  118 us
    pallas_call x1, Pallas kernels, begin(): pl.pallas_call(begin_kernel, out_shape=(jax.ShapeDtypeStruct((rows, width...  95.7 us
    pallas_call x1, Pallas kernels, attend_back(): pl.pallas_call(attend_back_kernel, out_shape=(jax.ShapeDtypeStruct((block...  54.1 us
    pallas_call x1, Pallas kernels, attend(): pl.pallas_call(attend_kernel, out_shape=(jax.ShapeDtypeStruct((blocks, QU...  48.2 us
    pallas_call x4, Pallas kernels, join(): pl.pallas_call(join_turned_kernel if turned else join_kernel, grid_spec=p...  20.6 us
  transfers between devices with their start and end apart: 2, of which 0 were waited for; matrix products, arithmetic and copies ran while one was open for 1% of the time, Pallas kernels for 18%

profile of v5, /device:TPU:0, one launch (start us, length us, event | category | flops | bytes accessed | tf_op | source)
XLA Modules:
  0.0 577.2 jit_solution(13809526825420003933)
XLA Ops:
  0.7 0.7 copy.28
  1.3 0.7 reshape.237
  2.0 0.6 fusion.3.bias_ref.bias_own
  2.7 95.7 %begin.1 = (bf16[512,1024]{1,0:T(8,128)(2,1)}, bf16[512,1024]{1,0:T(8,128)(2,1)}, bf16[32,128,128]{2,1,0:T(8,128)(2,1)}, bf16[32,256,128]{2,1,0:T(8,128)(2,1)}, ...) custom-call(bf16[512,1024]{1,0:T(8,128)(2,1)} %x_ref.5, ...), custom_call_target="tpu_custom_call" | custom-call | tf_op jit(solution)/shard_map/begin/pallas_call | solution.py:907
  98.4 1.8 constant_dynamic-slice_fusion
  100.2 1.5 collective-permute-start
  101.8 0.1 select_reduce_fusion.3
  101.9 0.1 broadcast_add_fusion
  102.0 0.2 select_reduce_fusion
  102.2 0.2 fusion.4
  102.4 0.7 maximum_minimum_fusion.high_ref
  103.1 0.1 fusion.7
  103.2 0.6 broadcast_in_dim.55.low_ref
  103.8 0.6 broadcast_in_dim.56
  104.4 0.6 broadcast_in_dim.57
  105.0 0.6 stack.17.tab
  105.6 48.2 %attend.1 = (bf16[32,128,128]{2,1,0:T(8,128)(2,1)}, f32[32,64,256]{2,1,0:T(8,128)}, f32[32,1,256]{2,1,0:T(1,128)}, bf16[17408,128]{1,0:T(8,128)(2,1)}, bf16[128,17408]{1,0:T(8,128)(2,1)}) custom-call(s32[1]{0:T(128)} %bitcast.3.part_ref.core_ref, s32[5,32]{1,0:T(8,128)} %stack.17.tab, s32[32,1,256]{2,1,0:T(1,128)} %broadcast_in_dim.55.low_ref, ...), custom_call_target="tpu_custom_call" | custom-call | flops 40000000000 | bytes 20971520 | tf_op jit(solution)/shard_map/attend/pallas_call | solution.py:229
  153.8 117.7 %middle.1 = (bf16[512,1024]{1,0:T(8,128)(2,1)}, bf16[32,128,128]{2,1,0:T(8,128)(2,1)}, f32[512,1024]{1,0:T(8,128)}, f32[16,1024]{1,0:T(8,128)}, bf16[2304,1024]{...) custom-call(f32[4,1024]{1,0:T(4,128)} %gain_ref.3, f32[4,1024]{1,0:T(4,128)} %shifts.1, ...), custom_call_target="tpu_custom_call" | custom-call | tf_op jit(solution)/shard_map/middle/pallas_call | solution.py:1285
  271.5 1.2 collective-permute-start.1
  272.8 54.1 %attend_back.1 = (bf16[32,128,128]{2,1,0:T(8,128)(2,1)}, bf16[32,256,128]{2,1,0:T(8,128)(2,1)}, bf16[32,256,128]{2,1,0:T(8,128)(2,1)}) custom-call(s32[1]{0:T(128)} %bitcast.3.part_ref.core_ref, s32[5,32]{1,0:T(8,128)} %stack.17.tab, s32[32,1,256]{2,1,0:T(1,128)} %broadcast_in_dim.55.low_ref, s32[32,1,256]{2,1,0:T(1,128)} %maximum_minimum_fusion.high_ref, ...), custom_call_target="tpu_custom_call" | custom-call | flops 60000002048 | bytes 31457280 | tf_op jit(solution)/shard_map/attend_back/pallas_call | solution.py:252
  326.9 222.7 %finish.1 = (bf16[2,3072,1024]{2,1,0:T(8,128)(2,1)}, f32[512,1024]{1,0:T(8,128)}, f32[16,1024]{1,0:T(8,128)}) custom-call(f32[4,1024]{1,0:T(4,128)} %gain_ref.3, bf16[32,128,128]{2,1,0:T(8,128)(2,1)} %get-tuple-element.57.dq_ref, bf16[32,256,128]{2,1,0:T(8,128)(2,1)} %get-tuple-element.58.mine_ref, bf16[32,256,128]{2,1,0:T(8,128)(2,1)} %get-tuple-element.59.theirs_ref, ...), custom_call_target="tpu_custom_call" | custom-call | tf_op jit(solution)/shard_map/finish/pallas_call | solution.py:717
  549.5 0.8 slice.18
  550.3 1.4 fusion.10
  551.7 1.5 fusion.9
  553.2 2.4 join.5
  555.6 6.1 %join.4 = f32[3,1024,512]{2,1,0:T(8,128)} custom-call(s32[1]{0:T(128)} %bitcast.3.part_ref.core_ref, bf16[2,3072,1024]{2,1,0:T(8,128)(2,1)} %get-tuple-element.70.in_ref), custom_call_target="tpu_custom_call" | custom-call | tf_op jit(solution)/shard_map/join/pallas_call | solution.py:747
  561.8 6.0 %join.7 = f32[2048,1024]{1,0:T(8,128)} custom-call(s32[1]{0:T(128)} %bitcast.3.part_ref.core_ref, bf16[2,3072,1024]{2,1,0:T(8,128)(2,1)} %get-tuple-element.70.in_ref), custom_call_target="tpu_custom_call" | custom-call | tf_op jit(solution)/shard_map/join/pallas_call | solution.py:747
  567.7 6.0 %join.6 = f32[1024,2048]{1,0:T(8,128)} custom-call(s32[1]{0:T(128)} %bitcast.3.part_ref.core_ref, bf16[2,3072,1024]{2,1,0:T(8,128)(2,1)} %get-tuple-element.70.in_ref), custom_call_target="tpu_custom_call" | custom-call | tf_op jit(solution)/shard_map/join/pallas_call | solution.py:747
  573.8 0.6 constant_dynamic-slice_fusion.1
  574.3 0.6 dynamic_slice.11
  574.9 1.0 copy.34
  575.9 1.3 copy.35
  (21 shorter events, 0.1 us)
Async XLA Ops:
  98.4 3.4 copy-start.6
  98.4 3.4 copy-start.5
  98.4 3.5 copy-start.4
  98.4 5.4 copy-start.2
  98.4 6.0 %copy-start.3 = (bf16[1024]{0:T(1024)(128)(2,1)S(1)}, bf16[1024]{0:T(1024)(128)(2,1)}, u32[]{:S(2)}) copy-start(bf16[1024]{0:T(1024)(128)(2,1)} %param.23) | copy-start | bytes 6148
  100.2 53.6 %collective-permute-start = (bf16[1024,1024]{1,0:T(8,128)(2,1)S(1)}, bf16[1024,1024]{1,0:T(8,128)(2,1)}, u32[]{:S(2)}, u32[]{:S(2)}) collective-permute-start(bf16[1024,1024]{1,0:T(8,128)(2,1)S(1)} %constant_dynamic-slice_fusion), channel_id=1, source_target_pairs={{0,1},{1,0},{2,3},{3,2},{4,5},{5,4},{6,7},{7,6},{8,9},{9,8},{10,11... | collective-permute-start | bytes 6291464 | tf_op jit(solution)/shard_map/ppermute | solution.py:1318
  271.5 55.3 %collective-permute-start.1 = (bf16[1024,1024]{1,0:T(8,128)(2,1)}, bf16[1024,1024]{1,0:T(8,128)(2,1)}, u32[]{:S(2)}, u32[]{:S(2)}) collective-permute-start(bf16[1024,1024]{1,0:T(8,128)(2,1)} %get-tuple-element.61), channel_id=1, source_target_pairs={{0,1},{1,0},{2,3},{3,2},{4,5},{5,4},{6,7},{7,6},{8,9},{9,8},{10,11... | collective-permute-start | bytes 6291464 | tf_op jit(solution)/shard_map/ppermute | solution.py:1318
  567.7 7.2 %copy-start.1 = (bf16[512,1024]{1,0:T(8,128)(2,1)S(1)}, bf16[512,1024]{1,0:T(8,128)(2,1)}, u32[]{:S(2)}) copy-start(bf16[512,1024]{1,0:T(8,128)(2,1)} %get-tuple-element.100) | copy-start | bytes 3145732
  573.7 2.2 copy-start

commit v6 on v5

--- a/solution.py
+++ b/solution.py
@@ -14,10 +14,9 @@
 LONGEST = 4096
 STEP_F = 1024
 STEP_B = 512
-UNROLL = 4
+UNROLL = 8
 CHUNK_ROWS = 256
 FIRST_TICKS = 6
-SLACK = 1
 VMEM_LIMIT = 58 << 20
 VMEM_MIDDLE = 62 << 20
 
@@ -83,6 +82,28 @@
     return jnp.concatenate([turned[:, :QUART], turned[:, QUART:]], axis=0).T
 
 
+def pieces_two(tab, b, keys, step, start):
+    count = keys // HALF
+    first, last = tab[0, b], tab[1, b]
+    total = last - first
+    short = lax.rem(total, count)
+    many = total // count + (short > count // 2).astype(jnp.int32)
+
+    def visit(size):
+        def at_piece(i, state):
+            at = pl.multiple_of((first + i * count) * HALF, HALF)
+            whole = (at >= tab[2, b]) & (at + size <= tab[3, b])
+            return lax.cond(
+                whole, lambda st: step(at, st, False, size), lambda st: step(at, st, True, size), state
+            )
+
+        return at_piece
+
+    state = lax.fori_loop(0, many, visit(keys), start)
+    half_step = ((short > 0) & (short <= count // 2)).astype(jnp.int32)
+    return lax.fori_loop(many, many + half_step, visit(keys // 2), state)
+
+
 def pieces(tab, b, keys, step, start):
     count = keys // HALF
     first = tab[0, b]
@@ -122,17 +143,18 @@
     def one(b, carry):
         low, high = low_ref[b], high_ref[b]
 
-        def step(at, state, masked):
+        def step(at, state, masked, size):
             top, total, acc = state
-            sc = jnp.dot(kv[pl.ds(at, STEP_F), :], rhs_s[b], preferred_element_type=F32)
+            sc = jnp.dot(kv[pl.ds(at, size), :], rhs_s[b], preferred_element_type=F32)
             if masked:
-                sc = jnp.where((depth >= low - at) & (depth < high - at), sc, -1e30)
+                rows_of = depth[:size]
+                sc = jnp.where((rows_of >= low - at) & (rows_of < high - at), sc, -1e30)
             new = jnp.maximum(top, jnp.max(sc, axis=0, keepdims=True))
             alpha = jnp.exp(top - new)
             pr = jnp.exp(sc - new)
             total = total * alpha + jnp.sum(pr, axis=0, keepdims=True)
             acc = acc * alpha + jnp.dot(
-                kvt[HEAD:, pl.ds(at, STEP_F)], pr.astype(BF16), preferred_element_type=F32
+                kvt[HEAD:, pl.ds(at, size)], pr.astype(BF16), preferred_element_type=F32
             )
             return new, total, acc
 
@@ -141,7 +163,7 @@
             jnp.zeros((1, HALF), F32),
             jnp.zeros((HEAD, HALF), F32),
         )
-        top, total, acc = pieces(tab, b, STEP_F, step, start)
+        top, total, acc = pieces_two(tab, b, STEP_F, step, start)
         ot_ref[b] = acc * (1.0 / total)
         lse_ref[b] = top + jnp.log(total)
         return carry
@@ -359,16 +381,19 @@
     return pl.ds(pl.multiple_of(start, size), size)
 
 
-def reduce_stages(place, chunks, base, out, both, kept, xbuf, xsum, zbuf, zsum, fbuf, sems, arrived):
+def reduce_stages(place, chunks, halved, base, out, both, kept, xbuf, xsum, zbuf, zsum, fbuf, sems, arrived):
     rows = base.shape[0] // chunks
     half, piece = rows // 2, rows // 8
     x, odd, upper = place.x, lax.rem(place.z, 2), place.z // 2
     pair = half // 2
 
     def x_copy(k):
+        seq, tp = place.x_partner
+        over_tp = (k >= halved[0]) & (k < halved[1])
         return remote(
             base.at[rows_at(k * rows + (1 - x) * half, half)], xbuf.at[rows_at(k * half, half)],
-            sems["xs"].at[k], sems["xr"].at[k], place.x_partner,
+            sems["xs"].at[k], sems["xr"].at[k],
+            (jnp.where(over_tp, place.seq, seq), jnp.where(over_tp, place.tp_partner[1], tp)),
         )
 
     def z_copy(k):
@@ -453,11 +478,9 @@
 
     def tick(t):
         for s, stage in reversed(list(enumerate(stages))):
-            k = t - SLACK * s
-
-            @pl.when((k >= 0) & (k < chunks))
+            @pl.when((t >= s) & (t - s < chunks))
             def _():
-                stage(k)
+                stage(t - s)
 
     def drain(k, carry):
         for copy in (x_copy, z_copy, far_z_copy, far_zg_copy, zg_copy, xg_copy):
@@ -471,7 +494,7 @@
         lax.fori_loop(0, chunks, drain, 0)
         keep.wait()
 
-    return tick, finale, chunks + SLACK * (len(stages) - 1)
+    return tick, finale, chunks + len(stages) - 1
 
 
 SEM_NAMES = ("xs", "xr", "zs", "zr", "zgs", "zgr", "xgs", "xgr", "cs", "cr")
@@ -479,7 +502,7 @@
 
 
 def finish_kernel(
-    chunks, first_ticks, gain_ref, dq_ref, mine_ref, theirs_ref, near_ref, far_up_ref, far_ref,
+    chunks, first_ticks, gain_ref, dq_ref, mine_ref, theirs_ref, near_ref, far_up_ref, far_ref, over_x_ref,
     normed_ref, normed_sib_ref, x_ref, dh_ref, w_ref, w2, w3, vec_ref,
     both, gx_ref, vec_out,
     out, base, far, ybuf, xbuf, xsum, zbuf, zsum, fbuf, dq_in, dkv_in, dkv_st, dkv_sib, mixed, mixed_sib,
@@ -494,6 +517,8 @@
     rows = base.shape[0] // chunks
     early = near_ref.shape[0]
     crossed = far_up_ref.shape[0] // rows
+    met = crossed + over_x_ref.shape[0] // rows
+    strip = rows // 2
     greet_all(count, me, place.seq, place.tp)
     dkv_pair = remote(theirs_ref, dkv_sib, ms.at[2], mr.at[2], place.core_partner)
     dkv_pair.start()
@@ -515,6 +540,18 @@
     near_copy.start()
     far_copy = pltpu.make_async_copy(far_up_ref, ybuf.at[pl.ds(0, far_up_ref.shape[0])], loc.at[2])
     far_copy.start()
+    over_copy = pltpu.make_async_copy(
+        over_x_ref, ybuf.at[pl.ds(crossed * rows, over_x_ref.shape[0])], loc.at[13]
+    )
+    over_copy.start()
+    strips = [
+        pltpu.make_async_copy(
+            far_ref.at[rows_at(j * rows + place.x * strip, strip)],
+            base.at[rows_at((crossed + j) * rows + (1 - place.x) * strip, strip)],
+            loc.at[14 + j],
+        )
+        for j in range(met - crossed)
+    ]
     locals_ = [(dq_ref.at[me], dq_in.at[me]), (normed_ref, normed), (normed_sib_ref, normed_sib)]
     locals_ += [(x_ref, x_s), (dh_ref, gx_ref)]
     col = w_s.shape[3]
@@ -533,7 +570,7 @@
         return carry
 
     settled = early // rows
-    lax.fori_loop(crossed, settled, cross, 0)
+    lax.fori_loop(met, settled, cross, 0)
     mine_copy.wait()
     dkv_pair.wait()
 
@@ -550,20 +587,35 @@
     lax.fori_loop(1, count, start_kv, 0)
     dkv_in[me] = dkv_st[me]
     near_copy.wait()
-    far_copy.wait()
-    for copy in locals_:
+    for copy in strips + locals_:
         copy.start()
+    for copy in [far_copy, over_copy] + strips:
+        copy.wait()
+
+    def add_in(into, other):
+        base[into, :] = (base[into, :].astype(F32) + ybuf[other, :].astype(F32)).astype(BF16)
 
     def arrived(k):
-        @pl.when(k >= crossed)
+        x_met = (k >= crossed) & (k < met)
+
+        @pl.when(k >= met)
         def _():
             tp_copy(k, base, 0).wait_recv()
 
-        span = rows_at(k * rows, rows)
-        base[span, :] = (base[span, :].astype(F32) + ybuf[span, :].astype(F32)).astype(BF16)
+        @pl.when(jnp.logical_not(x_met))
+        def _():
+            span = rows_at(k * rows, rows)
+            add_in(span, span)
+
+        @pl.when(x_met)
+        def _():
+            add_in(rows_at(k * rows + place.x * strip, strip), rows_at(k * rows, strip))
+            add_in(
+                rows_at(k * rows + (1 - place.x) * strip, strip), rows_at(k * rows + strip, strip)
+            )
 
     tick, drain, ticks = reduce_stages(
-        place, chunks, base, out, both, loc.at[12], xbuf, xsum, zbuf, zsum, fbuf, sems, arrived
+        place, chunks, (crossed, met), base, out, both, loc.at[12], xbuf, xsum, zbuf, zsum, fbuf, sems, arrived
     )
 
     def plain(t, carry):
@@ -676,11 +728,11 @@
         tp_copy(k, base, 0).wait_send()
         return carry
 
-    lax.fori_loop(crossed, chunks, sent, 0)
+    lax.fori_loop(met, chunks, sent, 0)
     drain()
 
 
-def finish(gain, dq_chunks, mine, theirs, near, far_up, far, normed, normed_sib, x, d_hidden, weights, vectors):
+def finish(gain, dq_chunks, mine, theirs, near, far_up, far, over_x, normed, normed_sib, x, d_hidden, weights, vectors):
     early, cols = near.shape
     late = 3 * weights[1].shape[2]
     total = early + late
@@ -713,7 +765,7 @@
     ]
     scratch += [dma((2, chunks) if name[0] == "z" else (chunks,)) for name in SEM_NAMES]
     scratch += [dma((count,))] * 4 + [dma((chunks,))] * 2 + [dma((3,))] * 2
-    scratch += [dma((VECTOR_STEPS,))] * 2 + [dma((13,))]
+    scratch += [dma((VECTOR_STEPS,))] * 2 + [dma((14 + over_x.shape[0] // CHUNK_ROWS,))]
     return pl.pallas_call(
         functools.partial(finish_kernel, chunks, FIRST_TICKS),
         out_shape=(
@@ -721,7 +773,7 @@
             jax.ShapeDtypeStruct((rows, cols), F32),
             jax.ShapeDtypeStruct(vectors.shape, F32),
         ),
-        in_specs=vmem(1) + [anywhere] * 13 + vmem(1),
+        in_specs=vmem(1) + [anywhere] * 14 + vmem(1),
         out_specs=(anywhere, vmem(1)[0], vmem(1)[0]),
         scratch_shapes=scratch,
         compiler_params=pltpu.CompilerParams(
@@ -729,7 +781,8 @@
         ),
         name="finish",
     )(
-        gain, dq_chunks, mine, theirs, near, far_up, far, normed, normed_sib, x, d_hidden, *weights, vectors
+        gain, dq_chunks, mine, theirs, near, far_up, far, over_x, normed, normed_sib, x, d_hidden, *weights,
+        vectors,
     )
 
 
@@ -759,8 +812,8 @@
 
 
 def begin_kernel(
-    x_ref, gain_ref, shift_ref, bias_ref, w_ref, wo_ref,
-    normed_ref, normed_sib, q_in, kv_own, kv_sib, bias_far, w2, w3, wo2, wo3,
+    x_ref, gain_ref, shift_ref, bias_ref, w_ref, wo_ref, wu_ref,
+    normed_ref, normed_sib, q_in, kv_own, kv_sib, bias_far, w2, w3, wo2, wo3, wu0,
     w0, w1, q_st, kv_st, *sems,
 ):
     place = Place()
@@ -781,6 +834,8 @@
         pltpu.make_async_copy(w_own, w0, ls.at[0]),
         pltpu.make_async_copy(w_ref.at[:, :, rows_at((1 - core) * col, col)], w1, ls.at[1]),
     ]
+    wu_copy = pltpu.make_async_copy(wu_ref.at[:, rows_at(core * wu0.shape[1], wu0.shape[1])], wu0, ls.at[2])
+    wu_copy.start()
     for copy in w_loads:
         copy.start()
     wo_far = remote(wo_ref.at[rows_at(core * wo_rows, wo_rows)], wo2, ws.at[1], wr.at[1], place.tp_partner)
@@ -838,7 +893,8 @@
         store_packed(who, quarter, dot(0) + bias_at(0), q_st)
 
         def send(i, carry):
-            other = chunk_of(who, quarter, i // 2, lax.rem(i, 2))
+            turned = lax.rem(i + 2 * (place.seq // 2) + 2, 8)
+            other = chunk_of(who, quarter, turned // 2, lax.rem(turned, 2))
 
             @pl.when(other != me)
             def _():
@@ -894,9 +950,10 @@
     lax.fori_loop(0, count, forwarded, 0)
     wo_last.wait()
     normed_pair.wait()
-
-
-def begin(x, gains, shifts, bias, w, wo):
+    wu_copy.wait()
+
+
+def begin(x, gains, shifts, bias, w, wo, wu):
     rows, width = x.shape
     count = 32
     dma = pltpu.SemaphoreType.DMA
@@ -917,19 +974,20 @@
             jax.ShapeDtypeStruct(w_quarter, BF16),
             jax.ShapeDtypeStruct(wo_quarter, BF16),
             jax.ShapeDtypeStruct(wo_quarter, BF16),
+            jax.ShapeDtypeStruct((wu.shape[0], wu.shape[1] // 2), BF16),
         ),
-        in_specs=vmem(4) + [anywhere] * 2,
-        out_specs=tuple(vmem(1) + [anywhere] + vmem(6) + [anywhere] * 2),
+        in_specs=vmem(4) + [anywhere] * 3,
+        out_specs=tuple(vmem(1) + [anywhere] + vmem(6) + [anywhere] * 3),
         scratch_shapes=[pltpu.VMEM(w_quarter, BF16)] * 2
         + [pltpu.VMEM(q_shape, BF16), pltpu.VMEM(kv_shape, BF16)]
         + [dma((count,))] * 6
         + [dma((6,))] * 2
-        + [dma((2,))],
+        + [dma((3,))],
         compiler_params=pltpu.CompilerParams(
             collective_id=3, has_side_effects=True, vmem_limit_bytes=VMEM_LIMIT
         ),
         name="begin",
-    )(x, gains, shifts, bias, w, wo)
+    )(x, gains, shifts, bias, w, wo, wu)
 
 
 def norm_parts(values):
@@ -976,7 +1034,7 @@
 def middle_kernel(
     gains, shifts, bias_out, bias_down, bias_own, bias_far, att_ref, x_ref, og_ref,
     wo_ref, wo2, wo3, wu_ref, wu2, wd_ref,
-    result, da_in, dh, vec, near_ref, far_up_ref, far_ref,
+    result, da_in, dh, vec, near_ref, far_up_ref, far_ref, over_x_ref,
     att_in, att_s, att_sib, wo_s, wu_s, wd_s, x_s, branch_s, hidden_s, inner_s, inner_sib, act_s, act_sib,
     dg_s, dup_sib, down_s, dd_s, dd_sib, db_s, db_sib, da_st,
     ats, atr, das, dar, ws, wr, cs, cr, loc,
@@ -1179,7 +1237,8 @@
         store_packed(who, quarter, dot_nt(db_s[...], wo_s[quarter]), da_st)
 
         def send(i, carry, quarter=quarter):
-            other = chunk_of(who, quarter, i // 2, lax.rem(i, 2))
+            turned = lax.rem(i + 2 * (place.seq // 2) + 2, 8)
+            other = chunk_of(who, quarter, turned // 2, lax.rem(turned, 2))
 
             @pl.when(other != me)
             def _():
@@ -1218,6 +1277,11 @@
         (wd_s.at[0], near_ref.at[pl.ds(up_rows, hid)]),
         (wd_s.at[2], far_ref.at[pl.ds(0, hid)]),
     ]
+    strip = CHUNK_ROWS // 2
+    for j in range(hid // CHUNK_ROWS):
+        span = rows_at(j * CHUNK_ROWS + (1 - place.x) * strip, strip)
+        for i, slot in enumerate((0, 2)):
+            stores.append((wd_s.at[slot, span], over_x_ref.at[pl.ds(j * CHUNK_ROWS + i * strip, strip)]))
     stores = [pltpu.make_async_copy(src, dst, loc.at[i]) for i, (src, dst) in enumerate(stores)]
     for copy in stores[:4]:
         copy.start()
@@ -1281,7 +1345,7 @@
         held(rows, width),
         held(*att.shape),
     ]
-    scratch += [dma((count,))] * 4 + [dma((3,))] * 2 + [dma((9,))] * 2 + [dma((12,))]
+    scratch += [dma((count,))] * 4 + [dma((3,))] * 2 + [dma((9,))] * 2 + [dma((6 + 2 * hid // CHUNK_ROWS,))]
     return pl.pallas_call(
         middle_kernel,
         out_shape=(
@@ -1292,9 +1356,10 @@
             jax.ShapeDtypeStruct((hid + width + out_rows, width), BF16),
             jax.ShapeDtypeStruct((width, hid), BF16),
             jax.ShapeDtypeStruct((hid + out_rows, width), BF16),
+            jax.ShapeDtypeStruct((hid, width), BF16),
         ),
         in_specs=vmem(6) + [anywhere] * 9,
-        out_specs=tuple(vmem(4) + [anywhere] * 3),
+        out_specs=tuple(vmem(4) + [anywhere] * 4),
         scratch_shapes=scratch,
         compiler_params=pltpu.CompilerParams(
             collective_id=4, has_side_effects=True, vmem_limit_bytes=VMEM_MIDDLE
@@ -1322,21 +1387,20 @@
     bias = jnp.concatenate([bias_up.reshape(2, width), bias_qv.reshape(1, width)]).astype(F32)
     bias = jnp.pad(bias, ((0, 5), (0, 0)))
     tables = block_tables(lengths, prefixes, placement, core)
-    normed, normed_sib, q_own, kv_own, kv_sib, bias_far, wq2, wq3, wo2, wo3 = begin(
-        tokens_in, norm_gains, norm_shifts, bias, w3, w_out
-    )
-    w_up, normed = lax.optimization_barrier((w_up, normed))
-    half = w_up.shape[1] // 2
-    wu2 = to_tp(lax.dynamic_slice_in_dim(w_up, core * half, half, 1))
+    normed, normed_sib, q_own, kv_own, kv_sib, bias_far, wq2, wq3, wo2, wo3, wu0 = begin(
+        tokens_in, norm_gains, norm_shifts, bias, w3, w_out, w_up
+    )
+    wu2 = to_tp(wu0)
     att_chunks, out_t, mass, kv_pack, kv_turned = attend(core, tables, q_own, kv_own, kv_sib)
-    result, da_own, d_hidden, vectors, near, far_up, far = middle(
+    result, da_own, d_hidden, vectors, near, far_up, far, over_x = middle(
         norm_gains, norm_shifts, bias_out.astype(F32)[None], bias_down.astype(F32)[None], bias, bias_far,
         att_chunks, tokens_in, out_grad, [w_out, wo2, wo3], w_up, wu2, w_down,
     )
     far_up = to_tp(far_up)
+    over_x = lax.ppermute(over_x, "seq", [(i, i ^ 2) for i in range(lax.axis_size("seq"))])
     dq_chunks, mine, theirs = attend_back(core, tables, q_own, da_own, out_t, mass, kv_pack, kv_turned)
     both, grad_x, vectors = finish(
-        norm_gains, dq_chunks, mine, theirs, near, far_up, far, normed, normed_sib, tokens_in, d_hidden,
+        norm_gains, dq_chunks, mine, theirs, near, far_up, far, over_x, normed, normed_sib, tokens_in, d_hidden,
         [w3, wq2, wq3], vectors,
     )
     up, down, out = (n // 256 for n in (width, wu2.shape[1], wo2.shape[0]))

time: 584 us -> 572 us (0.979); the launches traced: 577 us -> 573 us
    pallas_call x1, Pallas kernels: 223 us -> 212 us  [finish(): pl.pallas_call(functools.partial(finish_kernel, chunks, FIRST_TICKS), out...]
    pallas_call x1, Pallas kernels: 54.1 us -> 60.3 us  [attend_back(): pl.pallas_call(attend_back_kernel, out_shape=(jax.ShapeDtypeStruct((block...]
  transfers between devices with their start and end apart: 2 -> 3, of which waited for: 0 -> 0; matrix products, arithmetic and copies ran while one was open for 1% -> 1% of each run, Pallas kernels for 18% -> 19%
where the time goes in v6:
time: 572 us; the launch traced here: 573 us
  Pallas kernels  554 us (97%)
  local copies, waits for them, and re-layouts  9.79 us (2%)
    pallas_call x1, Pallas kernels, finish(): pl.pallas_call(functools.partial(finish_kernel, chunks, FIRST_TICKS), out...  212 us
    pallas_call x1, Pallas kernels, middle(): pl.pallas_call(middle_kernel, out_shape=(jax.ShapeDtypeStruct((rows, widt...  117 us
    pallas_call x1, Pallas kernels, begin(): pl.pallas_call(begin_kernel, out_shape=(jax.ShapeDtypeStruct((rows, width...  95.8 us
    pallas_call x1, Pallas kernels, attend_back(): pl.pallas_call(attend_back_kernel, out_shape=(jax.ShapeDtypeStruct((block...  60.3 us
    pallas_call x1, Pallas kernels, attend(): pl.pallas_call(attend_kernel, out_shape=(jax.ShapeDtypeStruct((blocks, QU...  49.1 us
    pallas_call x4, Pallas kernels, join(): pl.pallas_call(join_turned_kernel if turned else join_kernel, grid_spec=p...  20.6 us
  transfers between devices with their start and end apart: 3, of which 0 were waited for; matrix products, arithmetic and copies ran while one was open for 1% of the time, Pallas kernels for 19%

profile of v6, /device:TPU:0, one launch (start us, length us, event | category | flops | bytes accessed | tf_op | source)
XLA Modules:
  0.0 572.5 jit_solution(14779776938517516772)
XLA Ops:
  0.6 0.7 copy.28
  1.3 0.7 reshape.237
  2.0 0.6 fusion.3.bias_ref.bias_own
  2.7 0.0 copy-start.3
  2.7 95.8 %begin.1 = (bf16[512,1024]{1,0:T(8,128)(2,1)}, bf16[512,1024]{1,0:T(8,128)(2,1)}, bf16[32,128,128]{2,1,0:T(8,128)(2,1)}, bf16[32,256,128]{2,1,0:T(8,128)(2,1)}, ...) custom-call(bf16[512,1024]{1,0:T(8,128)(2,1)} %x_ref.5, ...), custom_call_target="tpu_custom_call" | custom-call | tf_op jit(solution)/shard_map/begin/pallas_call | solution.py:964
  98.5 1.5 collective-permute-start
  100.0 0.1 select_reduce_fusion.3
  100.1 0.1 broadcast_add_fusion
  100.2 0.2 select_reduce_fusion
  100.4 0.7 maximum_minimum_fusion.high_ref
  101.1 0.2 fusion.4
  101.3 0.6 broadcast_in_dim.55.low_ref
  102.0 0.6 broadcast_in_dim.56
  102.6 0.6 broadcast_in_dim.57
  103.2 0.6 stack.17.tab
  103.8 49.1 %attend.1 = (bf16[32,128,128]{2,1,0:T(8,128)(2,1)}, f32[32,64,256]{2,1,0:T(8,128)}, f32[32,1,256]{2,1,0:T(1,128)}, bf16[17408,128]{1,0:T(8,128)(2,1)}, bf16[128,17408]{1,0:T(8,128)(2,1)}) custom-call(s32[1]{0:T(128)} %bitcast.3.part_ref.core_ref, s32[5,32]{1,0:T(8,128)} %stack.17.tab, s32[32,1,256]{2,1,0:T(1,128)} %broadcast_in_dim.55.low_ref, ...), custom_call_target="tpu_custom_call" | custom-call | flops 40000000000 | bytes 20971520 | tf_op jit(solution)/shard_map/attend/pallas_call | solution.py:251
  152.9 117.0 %middle.1 = (bf16[512,1024]{1,0:T(8,128)(2,1)}, bf16[32,128,128]{2,1,0:T(8,128)(2,1)}, f32[512,1024]{1,0:T(8,128)}, f32[16,1024]{1,0:T(8,128)}, bf16[2304,1024]{...) custom-call(f32[4,1024]{1,0:T(4,128)} %gain_ref.3, ...), custom_call_target="tpu_custom_call" | custom-call | tf_op jit(solution)/shard_map/middle/pallas_call | solution.py:1349
  269.9 1.5 collective-permute-start.1
  271.4 1.3 collective-permute-start.2
  272.8 60.3 %attend_back.1 = (bf16[32,128,128]{2,1,0:T(8,128)(2,1)}, bf16[32,256,128]{2,1,0:T(8,128)(2,1)}, bf16[32,256,128]{2,1,0:T(8,128)(2,1)}) custom-call(s32[1]{0:T(128)} %bitcast.3.part_ref.core_ref, s32[5,32]{1,0:T(8,128)} %stack.17.tab, s32[32,1,256]{2,1,0:T(1,128)} %broadcast_in_dim.55.low_ref, s32[32,1,256]{2,1,0:T(1,128)} %maximum_minimum_fusion.high_ref, ...), custom_call_target="tpu_custom_call" | custom-call | flops 60000002048 | bytes 31457280 | tf_op jit(solution)/shard_map/attend_back/pallas_call | solution.py:274
  333.0 211.8 %finish.1 = (bf16[2,3072,1024]{2,1,0:T(8,128)(2,1)}, f32[512,1024]{1,0:T(8,128)}, f32[16,1024]{1,0:T(8,128)}) custom-call(f32[4,1024]{1,0:T(4,128)} %gain_ref.3, bf16[32,128,128]{2,1,0:T(8,128)(2,1)} %get-tuple-element.56.dq_ref, bf16[32,256,128]{2,1,0:T(8,128)(2,1)} %get-tuple-element.57.mine_ref, bf16[32,256,128]{2,1,0:T(8,128)(2,1)} %get-tuple-element.58.theirs_ref, ...), custom_call_target="tpu_custom_call" | custom-call | tf_op jit(solution)/shard_map/finish/pallas_call | solution.py:769
  544.8 0.8 slice.18
  545.6 1.4 fusion.10
  547.0 1.5 fusion.9
  548.5 2.4 join.5
  550.9 6.1 %join.4 = f32[3,1024,512]{2,1,0:T(8,128)} custom-call(s32[1]{0:T(128)} %bitcast.3.part_ref.core_ref, bf16[2,3072,1024]{2,1,0:T(8,128)(2,1)} %get-tuple-element.70.in_ref), custom_call_target="tpu_custom_call" | custom-call | tf_op jit(solution)/shard_map/join/pallas_call | solution.py:800
  557.1 6.0 %join.7 = f32[2048,1024]{1,0:T(8,128)} custom-call(s32[1]{0:T(128)} %bitcast.3.part_ref.core_ref, bf16[2,3072,1024]{2,1,0:T(8,128)(2,1)} %get-tuple-element.70.in_ref), custom_call_target="tpu_custom_call" | custom-call | tf_op jit(solution)/shard_map/join/pallas_call | solution.py:800
  563.0 6.0 %join.6 = f32[1024,2048]{1,0:T(8,128)} custom-call(s32[1]{0:T(128)} %bitcast.3.part_ref.core_ref, bf16[2,3072,1024]{2,1,0:T(8,128)(2,1)} %get-tuple-element.70.in_ref), custom_call_target="tpu_custom_call" | custom-call | tf_op jit(solution)/shard_map/join/pallas_call | solution.py:800
  569.1 0.6 constant_dynamic-slice_fusion
  569.6 0.6 dynamic_slice.7
  570.3 1.0 copy.34
  571.2 1.3 copy.35
  (22 shorter events, 0.1 us)
Async XLA Ops:
  2.7 97.3 %copy-start.6 = (s32[32]{0:T(128)S(1)}, s32[32]{0:T(128)}, u32[]{:S(2)}) copy-start(s32[32]{0:T(128)} %param.29) | copy-start | bytes 388
  2.7 97.3 %copy-start.5 = (s32[12]{0:T(128)S(1)}, s32[12]{0:T(128)}, u32[]{:S(2)}) copy-start(s32[12]{0:T(128)} %param.27) | copy-start | bytes 148
  2.7 97.5 %copy-start.4 = (s32[12]{0:T(128)S(1)}, s32[12]{0:T(128)}, u32[]{:S(2)}) copy-start(s32[12]{0:T(128)} %param.28) | copy-start | bytes 148
  2.7 99.3 %copy-start.2 = (bf16[1024]{0:T(1024)(128)(2,1)S(1)}, bf16[1024]{0:T(1024)(128)(2,1)}, u32[]{:S(2)}) copy-start(bf16[1024]{0:T(1024)(128)(2,1)} %param.19) | copy-start | bytes 6148
  2.7 99.9 %copy-start.3 = (bf16[1024]{0:T(1024)(128)(2,1)S(1)}, bf16[1024]{0:T(1024)(128)(2,1)}, u32[]{:S(2)}) copy-start(bf16[1024]{0:T(1024)(128)(2,1)} %param.23) | copy-start | bytes 6148
  98.5 54.4 %collective-permute-start = (bf16[1024,1024]{1,0:T(8,128)(2,1)}, bf16[1024,1024]{1,0:T(8,128)(2,1)}, u32[]{:S(2)}, u32[]{:S(2)}) collective-permute-start(bf16[1024,1024]{1,0:T(8,128)(2,1)} %get-tuple-element.49), channel_id=1, source_target_pairs={{0,1},{1,0},{2,3},{3,2},{4,5},{5,4},{6,7},{7,6},{8,9},{9,8},{10,11... | collective-permute-start | bytes 6291464 | tf_op jit(solution)/shard_map/ppermute | solution.py:1383
  269.9 63.1 %collective-permute-start.1 = (bf16[1024,1024]{1,0:T(8,128)(2,1)}, bf16[1024,1024]{1,0:T(8,128)(2,1)}, u32[]{:S(2)}, u32[]{:S(2)}) collective-permute-start(bf16[1024,1024]{1,0:T(8,128)(2,1)} %get-tuple-element.60), channel_id=1, source_target_pairs={{0,1},{1,0},{2,3},{3,2},{4,5},{5,4},{6,7},{7,6},{8,9},{9,8},{10,11... | collective-permute-start | bytes 6291464 | tf_op jit(solution)/shard_map/ppermute | solution.py:1383
  271.4 61.6 %collective-permute-start.2 = (bf16[1024,1024]{1,0:T(8,128)(2,1)}, bf16[1024,1024]{1,0:T(8,128)(2,1)}, u32[]{:S(2)}, u32[]{:S(2)}) collective-permute-start(bf16[1024,1024]{1,0:T(8,128)(2,1)} %get-tuple-element.62), channel_id=1, source_target_pairs={{0,4},{2,6},{4,0},{6,2},{8,12},{10,14},{12,8},{14,10},{16,20},{18,... | collective-permute-start | bytes 6291464 | tf_op jit(solution)/shard_map/ppermute | solution.py:1400
  563.0 7.2 %copy-start.1 = (bf16[512,1024]{1,0:T(8,128)(2,1)S(1)}, bf16[512,1024]{1,0:T(8,128)(2,1)}, u32[]{:S(2)}) copy-start(bf16[512,1024]{1,0:T(8,128)(2,1)} %get-tuple-element.100) | copy-start | bytes 3145732
  569.1 2.2 copy-start

commit v7 on v6

--- a/solution.py
+++ b/solution.py
@@ -705,21 +705,25 @@
         (place.seq ^ bit, place.tp) for bit in (4, 8)
     ]
 
-    def vector_step(step):
-        slots[step] = vec_out[...]
-        copy = remote(
+    def vector_copy(step):
+        return remote(
             slots.at[step], slots.at[VECTOR_STEPS + step], vs.at[step], vr.at[step], partners[step]
         )
-        copy.start()
-        copy.wait()
-        vec_out[...] += slots[VECTOR_STEPS + step]
+
+    def vector_tick(step):
+        if step > 0:
+            vector_copy(step - 1).wait()
+            vec_out[...] += slots[VECTOR_STEPS + step - 1]
+        if step < VECTOR_STEPS:
+            slots[step] = vec_out[...]
+            vector_copy(step).start()
 
     def last(t, carry):
         tick(t)
-        for step in range(VECTOR_STEPS):
+        for step in range(VECTOR_STEPS + 1):
             @pl.when(t == first_ticks + 3 + step)
             def _():
-                vector_step(step)
+                vector_tick(step)
         return carry
 
     lax.fori_loop(first_ticks + 3, ticks, last, 0)
@@ -850,7 +854,7 @@
         ).astype(BF16)
         return carry
 
-    lax.fori_loop(0, x_ref.shape[0] // 64, norm, 0)
+    lax.fori_loop(0, x_ref.shape[0] // 64, norm, 0, unroll=2)
 
     normed_pair = remote(normed_ref, normed_sib, ws.at[4], wr.at[4], place.core_partner)
     normed_pair.start()
@@ -1113,7 +1117,7 @@
         inner_s[span, :] = layer_norm(hidden, gains[2:3, :], shifts[2:3, :]).astype(BF16)
         return carry
 
-    lax.fori_loop(0, rows // 64, into, 0)
+    lax.fori_loop(0, rows // 64, into, 0, unroll=2)
     inner_pair.start()
     for quarter in range(4):
         if quarter == 3:
@@ -1168,7 +1172,7 @@
         dd_s[span, :] = d_down.astype(BF16)
         return gain + col_sum(upstream * xhat), shift + col_sum(upstream), bias + col_sum(d_down)
 
-    gain, shift, bias = lax.fori_loop(0, rows // 64, turn, (none,) * 3)
+    gain, shift, bias = lax.fori_loop(0, rows // 64, turn, (none,) * 3, unroll=2)
     vec[...] = jnp.zeros_like(vec)
     vec[3:4, :] = gain
     vec[7:8, :] = shift
@@ -1218,7 +1222,7 @@
             bias + col_sum(d_branch),
         )
 
-    sums = lax.fori_loop(0, rows // 64, out_of, (none,) * 5)
+    sums = lax.fori_loop(0, rows // 64, out_of, (none,) * 5, unroll=2)
     for row, value in zip((2, 6, 1, 5, 8), sums):
         vec[row : row + 1, :] = value
     db_pair.start()
@@ -1404,8 +1408,8 @@
         [w3, wq2, wq3], vectors,
     )
     up, down, out = (n // 256 for n in (width, wu2.shape[1], wo2.shape[0]))
-    g_up = join(core, both, 512, 0, up // 2, w_up.shape, lambda p, i: (i, p))
-    g_down = join(core, both, 512, up // 2, down // 2, w_down.shape, lambda p, i: (p * (down // 2) + i, 0))
+    g_up = join(core, both, 1024, 0, up // 4, w_up.shape, lambda p, i: (i, p))
+    g_down = join(core, both, 1024, up // 4, down // 4, w_down.shape, lambda p, i: (p * (down // 4) + i, 0))
     g_out = join(core, both, 256, up + down, out, w_out.shape, lambda p, i: (p * out + i, 0))
     g_qkv = join(
         core, both, 256, up + down + out, 3, (3, width, w_qkv.shape[2]), lambda p, i: (i, 0, p), turned=True

time: 572 us -> 564 us (0.986)
  Pallas kernels: 554 us -> 543 us
    pallas_call x1, Pallas kernels: 212 us -> 200 us  [finish(): pl.pallas_call(functools.partial(finish_kernel, chunks, FIRST_TICKS), out...]
  transfers between devices with their start and end apart: 3 -> 3, of which waited for: 0 -> 0; matrix products, arithmetic and copies ran while one was open for 1% -> 1% of each run, Pallas kernels for 19% -> 20%
where the time goes in v7:
time: 564 us; the launch traced here: 561 us
  Pallas kernels  543 us (96%)
  local copies, waits for them, and re-layouts  9.79 us (2%)
    pallas_call x1, Pallas kernels, finish(): pl.pallas_call(functools.partial(finish_kernel, chunks, FIRST_TICKS), out...  200 us
    pallas_call x1, Pallas kernels, middle(): pl.pallas_call(middle_kernel, out_shape=(jax.ShapeDtypeStruct((rows, widt...  115 us
    pallas_call x1, Pallas kernels, begin(): pl.pallas_call(begin_kernel, out_shape=(jax.ShapeDtypeStruct((rows, width...  95.8 us
    pallas_call x1, Pallas kernels, attend_back(): pl.pallas_call(attend_back_kernel, out_shape=(jax.ShapeDtypeStruct((block...  62.6 us
    pallas_call x1, Pallas kernels, attend(): pl.pallas_call(attend_kernel, out_shape=(jax.ShapeDtypeStruct((blocks, QU...  50.6 us
    pallas_call x4, Pallas kernels, join(): pl.pallas_call(join_turned_kernel if turned else join_kernel, grid_spec=p...  19.2 us
  transfers between devices with their start and end apart: 3, of which 0 were waited for; matrix products, arithmetic and copies ran while one was open for 1% of the time, Pallas kernels for 20%

profile of v7, /device:TPU:0, one launch (start us, length us, event | category | flops | bytes accessed | tf_op | source)
XLA Modules:
  0.0 561.1 jit_solution(10806970127027690204)
XLA Ops:
  0.6 0.7 copy.28
  1.3 0.7 reshape.237
  2.0 0.6 fusion.3.bias_ref.bias_own
  2.7 0.0 copy-start.3
  2.7 95.8 %begin.1 = (bf16[512,1024]{1,0:T(8,128)(2,1)}, bf16[512,1024]{1,0:T(8,128)(2,1)}, bf16[32,128,128]{2,1,0:T(8,128)(2,1)}, bf16[32,256,128]{2,1,0:T(8,128)(2,1)}, ...) custom-call(bf16[512,1024]{1,0:T(8,128)(2,1)} %x_ref.5, ...), custom_call_target="tpu_custom_call" | custom-call | tf_op jit(solution)/shard_map/begin/pallas_call | solution.py:968
  98.5 1.5 collective-permute-start
  100.0 0.1 select_reduce_fusion.3
  100.1 0.1 broadcast_add_fusion
  100.2 0.2 select_reduce_fusion
  100.4 0.7 maximum_minimum_fusion.high_ref
  101.1 0.2 fusion.4
  101.3 0.6 broadcast_in_dim.55.low_ref
  102.0 0.6 broadcast_in_dim.56
  102.6 0.6 broadcast_in_dim.57
  103.2 0.6 stack.17.tab
  103.8 50.6 %attend.1 = (bf16[32,128,128]{2,1,0:T(8,128)(2,1)}, f32[32,64,256]{2,1,0:T(8,128)}, f32[32,1,256]{2,1,0:T(1,128)}, bf16[17408,128]{1,0:T(8,128)(2,1)}, bf16[128,17408]{1,0:T(8,128)(2,1)}) custom-call(s32[1]{0:T(128)} %bitcast.3.part_ref.core_ref, s32[5,32]{1,0:T(8,128)} %stack.17.tab, s32[32,1,256]{2,1,0:T(1,128)} %broadcast_in_dim.55.low_ref, ...), custom_call_target="tpu_custom_call" | custom-call | flops 40000000000 | bytes 20971520 | tf_op jit(solution)/shard_map/attend/pallas_call | solution.py:251
  154.4 115.3 %middle.1 = (bf16[512,1024]{1,0:T(8,128)(2,1)}, bf16[32,128,128]{2,1,0:T(8,128)(2,1)}, f32[512,1024]{1,0:T(8,128)}, f32[16,1024]{1,0:T(8,128)}, bf16[2304,1024]{...) custom-call(f32[4,1024]{1,0:T(4,128)} %gain_ref.3, ...), custom_call_target="tpu_custom_call" | custom-call | tf_op jit(solution)/shard_map/middle/pallas_call | solution.py:1353
  269.7 1.5 collective-permute-start.1
  271.2 1.3 collective-permute-start.2
  272.6 62.6 %attend_back.1 = (bf16[32,128,128]{2,1,0:T(8,128)(2,1)}, bf16[32,256,128]{2,1,0:T(8,128)(2,1)}, bf16[32,256,128]{2,1,0:T(8,128)(2,1)}) custom-call(s32[1]{0:T(128)} %bitcast.3.part_ref.core_ref, s32[5,32]{1,0:T(8,128)} %stack.17.tab, s32[32,1,256]{2,1,0:T(1,128)} %broadcast_in_dim.55.low_ref, s32[32,1,256]{2,1,0:T(1,128)} %maximum_minimum_fusion.high_ref, ...), custom_call_target="tpu_custom_call" | custom-call | flops 60000002048 | bytes 31457280 | tf_op jit(solution)/shard_map/attend_back/pallas_call | solution.py:274
  335.2 199.5 %finish.1 = (bf16[2,3072,1024]{2,1,0:T(8,128)(2,1)}, f32[512,1024]{1,0:T(8,128)}, f32[16,1024]{1,0:T(8,128)}) custom-call(f32[4,1024]{1,0:T(4,128)} %gain_ref.3, bf16[32,128,128]{2,1,0:T(8,128)(2,1)} %get-tuple-element.56.dq_ref, bf16[32,256,128]{2,1,0:T(8,128)(2,1)} %get-tuple-element.57.mine_ref, bf16[32,256,128]{2,1,0:T(8,128)(2,1)} %get-tuple-element.58.theirs_ref, ...), custom_call_target="tpu_custom_call" | custom-call | tf_op jit(solution)/shard_map/finish/pallas_call | solution.py:773
  534.7 0.8 slice.18
  535.5 1.4 fusion.10
  536.9 1.5 fusion.9
  538.4 2.4 join.5
  540.8 6.1 %join.4 = f32[3,1024,512]{2,1,0:T(8,128)} custom-call(s32[1]{0:T(128)} %bitcast.3.part_ref.core_ref, bf16[2,3072,1024]{2,1,0:T(8,128)(2,1)} %get-tuple-element.70.in_ref), custom_call_target="tpu_custom_call" | custom-call | tf_op jit(solution)/shard_map/join/pallas_call | solution.py:804
  547.0 5.3 join.7
  552.2 5.3 join.6
  557.6 0.6 constant_dynamic-slice_fusion
  558.2 0.6 dynamic_slice.7
  558.8 1.0 copy.34
  559.7 1.3 copy.35
  (22 shorter events, 0.1 us)
Async XLA Ops:
  2.7 97.3 %copy-start.6 = (s32[32]{0:T(128)S(1)}, s32[32]{0:T(128)}, u32[]{:S(2)}) copy-start(s32[32]{0:T(128)} %param.29) | copy-start | bytes 388
  2.7 97.3 %copy-start.5 = (s32[12]{0:T(128)S(1)}, s32[12]{0:T(128)}, u32[]{:S(2)}) copy-start(s32[12]{0:T(128)} %param.27) | copy-start | bytes 148
  2.7 97.5 %copy-start.4 = (s32[12]{0:T(128)S(1)}, s32[12]{0:T(128)}, u32[]{:S(2)}) copy-start(s32[12]{0:T(128)} %param.28) | copy-start | bytes 148
  2.7 99.3 %copy-start.2 = (bf16[1024]{0:T(1024)(128)(2,1)S(1)}, bf16[1024]{0:T(1024)(128)(2,1)}, u32[]{:S(2)}) copy-start(bf16[1024]{0:T(1024)(128)(2,1)} %param.19) | copy-start | bytes 6148
  2.7 99.9 %copy-start.3 = (bf16[1024]{0:T(1024)(128)(2,1)S(1)}, bf16[1024]{0:T(1024)(128)(2,1)}, u32[]{:S(2)}) copy-start(bf16[1024]{0:T(1024)(128)(2,1)} %param.23) | copy-start | bytes 6148
  98.5 56.0 %collective-permute-start = (bf16[1024,1024]{1,0:T(8,128)(2,1)}, bf16[1024,1024]{1,0:T(8,128)(2,1)}, u32[]{:S(2)}, u32[]{:S(2)}) collective-permute-start(bf16[1024,1024]{1,0:T(8,128)(2,1)} %get-tuple-element.49), channel_id=1, source_target_pairs={{0,1},{1,0},{2,3},{3,2},{4,5},{5,4},{6,7},{7,6},{8,9},{9,8},{10,11... | collective-permute-start | bytes 6291464 | tf_op jit(solution)/shard_map/ppermute | solution.py:1387
  269.7 65.5 %collective-permute-start.1 = (bf16[1024,1024]{1,0:T(8,128)(2,1)}, bf16[1024,1024]{1,0:T(8,128)(2,1)}, u32[]{:S(2)}, u32[]{:S(2)}) collective-permute-start(bf16[1024,1024]{1,0:T(8,128)(2,1)} %get-tuple-element.60), channel_id=1, source_target_pairs={{0,1},{1,0},{2,3},{3,2},{4,5},{5,4},{6,7},{7,6},{8,9},{9,8},{10,11... | collective-permute-start | bytes 6291464 | tf_op jit(solution)/shard_map/ppermute | solution.py:1387
  271.2 64.0 %collective-permute-start.2 = (bf16[1024,1024]{1,0:T(8,128)(2,1)}, bf16[1024,1024]{1,0:T(8,128)(2,1)}, u32[]{:S(2)}, u32[]{:S(2)}) collective-permute-start(bf16[1024,1024]{1,0:T(8,128)(2,1)} %get-tuple-element.62), channel_id=1, source_target_pairs={{0,4},{2,6},{4,0},{6,2},{8,12},{10,14},{12,8},{14,10},{16,20},{18,... | collective-permute-start | bytes 6291464 | tf_op jit(solution)/shard_map/ppermute | solution.py:1404
  552.2 6.5 %copy-start.1 = (bf16[512,1024]{1,0:T(8,128)(2,1)S(1)}, bf16[512,1024]{1,0:T(8,128)(2,1)}, u32[]{:S(2)}) copy-start(bf16[512,1024]{1,0:T(8,128)(2,1)} %get-tuple-element.100) | copy-start | bytes 3145732
  557.6 2.2 copy-start

commit v8 on v7

--- a/solution.py
+++ b/solution.py
@@ -477,7 +477,7 @@
     stages = [stage_x, stage_z, stage_far_z, stage_far_zg, stage_zg, stage_xg, stage_core]
 
     def tick(t):
-        for s, stage in reversed(list(enumerate(stages))):
+        for s, stage in enumerate(stages):
             @pl.when((t >= s) & (t - s < chunks))
             def _():
                 stage(t - s)

time: 564 us -> 555 us (0.984)
    pallas_call x1, Pallas kernels: 62.6 us -> 56.6 us  [attend_back(): pl.pallas_call(attend_back_kernel, out_shape=(jax.ShapeDtypeStruct((block...]
  transfers between devices with their start and end apart: 3 -> 3, of which waited for: 0 -> 0; matrix products, arithmetic and copies ran while one was open for 1% -> 1% of each run, Pallas kernels for 20% -> 18%
where the time goes in v8:
time: 555 us; the launch traced here: 557 us
  Pallas kernels  539 us (97%)
  local copies, waits for them, and re-layouts  9.79 us (2%)
    pallas_call x1, Pallas kernels, finish(): pl.pallas_call(functools.partial(finish_kernel, chunks, FIRST_TICKS), out...  203 us
    pallas_call x1, Pallas kernels, middle(): pl.pallas_call(middle_kernel, out_shape=(jax.ShapeDtypeStruct((rows, widt...  118 us
    pallas_call x1, Pallas kernels, begin(): pl.pallas_call(begin_kernel, out_shape=(jax.ShapeDtypeStruct((rows, width...  95.8 us
    pallas_call x1, Pallas kernels, attend_back(): pl.pallas_call(attend_back_kernel, out_shape=(jax.ShapeDtypeStruct((block...  56.6 us
    pallas_call x1, Pallas kernels, attend(): pl.pallas_call(attend_kernel, out_shape=(jax.ShapeDtypeStruct((blocks, QU...  46.4 us
    pallas_call x4, Pallas kernels, join(): pl.pallas_call(join_turned_kernel if turned else join_kernel, grid_spec=p...  19.2 us
  transfers between devices with their start and end apart: 3, of which 0 were waited for; matrix products, arithmetic and copies ran while one was open for 1% of the time, Pallas kernels for 18%

profile of v8, /device:TPU:0, one launch (start us, length us, event | category | flops | bytes accessed | tf_op | source)
XLA Modules:
  0.0 556.9 jit_solution(8100544972239912394)
XLA Ops:
  0.6 0.7 copy.28
  1.3 0.7 reshape.237
  2.0 0.6 fusion.3.bias_ref.bias_own
  2.7 0.0 copy-start.3
  2.7 95.8 %begin.1 = (bf16[512,1024]{1,0:T(8,128)(2,1)}, bf16[512,1024]{1,0:T(8,128)(2,1)}, bf16[32,128,128]{2,1,0:T(8,128)(2,1)}, bf16[32,256,128]{2,1,0:T(8,128)(2,1)}, ...) custom-call(bf16[512,1024]{1,0:T(8,128)(2,1)} %x_ref.5, ...), custom_call_target="tpu_custom_call" | custom-call | tf_op jit(solution)/shard_map/begin/pallas_call | solution.py:968
  98.5 1.5 collective-permute-start
  100.0 0.1 select_reduce_fusion.3
  100.1 0.1 broadcast_add_fusion
  100.2 0.2 select_reduce_fusion
  100.4 0.7 maximum_minimum_fusion.high_ref
  101.1 0.2 fusion.4
  101.3 0.6 broadcast_in_dim.55.low_ref
  102.0 0.6 broadcast_in_dim.56
  102.6 0.6 broadcast_in_dim.57
  103.2 0.6 stack.17.tab
  103.8 46.4 %attend.1 = (bf16[32,128,128]{2,1,0:T(8,128)(2,1)}, f32[32,64,256]{2,1,0:T(8,128)}, f32[32,1,256]{2,1,0:T(1,128)}, bf16[17408,128]{1,0:T(8,128)(2,1)}, bf16[128,17408]{1,0:T(8,128)(2,1)}) custom-call(s32[1]{0:T(128)} %bitcast.3.part_ref.core_ref, s32[5,32]{1,0:T(8,128)} %stack.17.tab, s32[32,1,256]{2,1,0:T(1,128)} %broadcast_in_dim.55.low_ref, ...), custom_call_target="tpu_custom_call" | custom-call | flops 40000000000 | bytes 20971520 | tf_op jit(solution)/shard_map/attend/pallas_call | solution.py:251
  150.2 117.5 %middle.1 = (bf16[512,1024]{1,0:T(8,128)(2,1)}, bf16[32,128,128]{2,1,0:T(8,128)(2,1)}, f32[512,1024]{1,0:T(8,128)}, f32[16,1024]{1,0:T(8,128)}, bf16[2304,1024]{...) custom-call(f32[4,1024]{1,0:T(4,128)} %gain_ref.3, ...), custom_call_target="tpu_custom_call" | custom-call | tf_op jit(solution)/shard_map/middle/pallas_call | solution.py:1353
  267.8 1.6 collective-permute-start.1
  269.3 1.3 collective-permute-start.2
  270.6 56.6 %attend_back.1 = (bf16[32,128,128]{2,1,0:T(8,128)(2,1)}, bf16[32,256,128]{2,1,0:T(8,128)(2,1)}, bf16[32,256,128]{2,1,0:T(8,128)(2,1)}) custom-call(s32[1]{0:T(128)} %bitcast.3.part_ref.core_ref, s32[5,32]{1,0:T(8,128)} %stack.17.tab, s32[32,1,256]{2,1,0:T(1,128)} %broadcast_in_dim.55.low_ref, s32[32,1,256]{2,1,0:T(1,128)} %maximum_minimum_fusion.high_ref, ...), custom_call_target="tpu_custom_call" | custom-call | flops 60000002048 | bytes 31457280 | tf_op jit(solution)/shard_map/attend_back/pallas_call | solution.py:274
  327.2 203.4 %finish.1 = (bf16[2,3072,1024]{2,1,0:T(8,128)(2,1)}, f32[512,1024]{1,0:T(8,128)}, f32[16,1024]{1,0:T(8,128)}) custom-call(f32[4,1024]{1,0:T(4,128)} %gain_ref.3, bf16[32,128,128]{2,1,0:T(8,128)(2,1)} %get-tuple-element.56.dq_ref, bf16[32,256,128]{2,1,0:T(8,128)(2,1)} %get-tuple-element.57.mine_ref, bf16[32,256,128]{2,1,0:T(8,128)(2,1)} %get-tuple-element.58.theirs_ref, ...), custom_call_target="tpu_custom_call" | custom-call | tf_op jit(solution)/shard_map/finish/pallas_call | solution.py:773
  530.6 0.8 slice.18
  531.3 1.4 fusion.10
  532.8 1.5 fusion.9
  534.2 2.4 join.5
  536.7 6.1 %join.4 = f32[3,1024,512]{2,1,0:T(8,128)} custom-call(s32[1]{0:T(128)} %bitcast.3.part_ref.core_ref, bf16[2,3072,1024]{2,1,0:T(8,128)(2,1)} %get-tuple-element.70.in_ref), custom_call_target="tpu_custom_call" | custom-call | tf_op jit(solution)/shard_map/join/pallas_call | solution.py:804
  542.8 5.3 join.7
  548.0 5.3 join.6
  553.4 0.6 constant_dynamic-slice_fusion
  554.0 0.6 dynamic_slice.7
  554.6 1.0 copy.34
  555.6 1.3 copy.35
  (22 shorter events, 0.1 us)
Async XLA Ops:
  2.7 97.3 %copy-start.6 = (s32[32]{0:T(128)S(1)}, s32[32]{0:T(128)}, u32[]{:S(2)}) copy-start(s32[32]{0:T(128)} %param.29) | copy-start | bytes 388
  2.7 97.3 %copy-start.5 = (s32[12]{0:T(128)S(1)}, s32[12]{0:T(128)}, u32[]{:S(2)}) copy-start(s32[12]{0:T(128)} %param.27) | copy-start | bytes 148
  2.7 97.5 %copy-start.4 = (s32[12]{0:T(128)S(1)}, s32[12]{0:T(128)}, u32[]{:S(2)}) copy-start(s32[12]{0:T(128)} %param.28) | copy-start | bytes 148
  2.7 99.3 %copy-start.2 = (bf16[1024]{0:T(1024)(128)(2,1)S(1)}, bf16[1024]{0:T(1024)(128)(2,1)}, u32[]{:S(2)}) copy-start(bf16[1024]{0:T(1024)(128)(2,1)} %param.19) | copy-start | bytes 6148
  2.7 99.9 %copy-start.3 = (bf16[1024]{0:T(1024)(128)(2,1)S(1)}, bf16[1024]{0:T(1024)(128)(2,1)}, u32[]{:S(2)}) copy-start(bf16[1024]{0:T(1024)(128)(2,1)} %param.23) | copy-start | bytes 6148
  98.5 51.7 %collective-permute-start = (bf16[1024,1024]{1,0:T(8,128)(2,1)}, bf16[1024,1024]{1,0:T(8,128)(2,1)}, u32[]{:S(2)}, u32[]{:S(2)}) collective-permute-start(bf16[1024,1024]{1,0:T(8,128)(2,1)} %get-tuple-element.49), channel_id=1, source_target_pairs={{0,1},{1,0},{2,3},{3,2},{4,5},{5,4},{6,7},{7,6},{8,9},{9,8},{10,11... | collective-permute-start | bytes 6291464 | tf_op jit(solution)/shard_map/ppermute | solution.py:1387
  267.8 59.4 %collective-permute-start.1 = (bf16[1024,1024]{1,0:T(8,128)(2,1)}, bf16[1024,1024]{1,0:T(8,128)(2,1)}, u32[]{:S(2)}, u32[]{:S(2)}) collective-permute-start(bf16[1024,1024]{1,0:T(8,128)(2,1)} %get-tuple-element.60), channel_id=1, source_target_pairs={{0,1},{1,0},{2,3},{3,2},{4,5},{5,4},{6,7},{7,6},{8,9},{9,8},{10,11... | collective-permute-start | bytes 6291464 | tf_op jit(solution)/shard_map/ppermute | solution.py:1387
  269.3 57.9 %collective-permute-start.2 = (bf16[1024,1024]{1,0:T(8,128)(2,1)}, bf16[1024,1024]{1,0:T(8,128)(2,1)}, u32[]{:S(2)}, u32[]{:S(2)}) collective-permute-start(bf16[1024,1024]{1,0:T(8,128)(2,1)} %get-tuple-element.62), channel_id=1, source_target_pairs={{0,4},{2,6},{4,0},{6,2},{8,12},{10,14},{12,8},{14,10},{16,20},{18,... | collective-permute-start | bytes 6291464 | tf_op jit(solution)/shard_map/ppermute | solution.py:1404
  548.0 6.5 %copy-start.1 = (bf16[512,1024]{1,0:T(8,128)(2,1)S(1)}, bf16[512,1024]{1,0:T(8,128)(2,1)}, u32[]{:S(2)}) copy-start(bf16[512,1024]{1,0:T(8,128)(2,1)} %get-tuple-element.100) | copy-start | bytes 3145732
  553.4 2.2 copy-start
